TPU v7x, 32 devices: a whole 2x2x4 slice. The times are simulated.
32 devices in a mesh: seq: 8 (over z, y), head: 4 (over x, core).
Axes of the slice: x: 2, y: 2, z: 4, core: 2. Of those that a mesh axis runs over, the one named last changes fastest.
Arguments:
- inputs: bfloat16 [2048, 2048], P('seq', 'head'), may hold values from -6 to 6
- w_query: bfloat16 [2048, 2048], P(None, 'head'), may hold values from -0.125 to 0.125
- w_key: bfloat16 [2048, 2048], P(None, 'head'), may hold values from -0.125 to 0.125
- w_value: bfloat16 [2048, 2048], P(None, 'head'), may hold values from -0.125 to 0.125
- sketch: float32 [2, 64, 32], replicated, may hold values from -0.75 to 0.75
- prefix_state: float32 [32, 1024, 64], P('head'), may hold values from -56 to 56
- prefix_norm: float32 [32, 1024], P('head'), as said below
- d_attn: bfloat16 [2048, 2048], P('seq', 'head'), may hold values from -128 to 128
- d_state_end: float32 [32, 1024, 64], P('head'), may hold values from -6 to 6
- d_norm_end: float32 [32, 1024], P('head'), may hold values from -4 to 4
Outputs:
- d_input: bfloat16 [2048, 2048], P('seq', 'head')
- d_query: bfloat16 [2048, 2048], P('seq', 'head')
- d_key: bfloat16 [2048, 2048], P('seq', 'head')
- d_value: bfloat16 [2048, 2048], P('seq', 'head')
- d_prefix_state: float32 [32, 1024, 64], P('head')
- d_prefix_norm: float32 [32, 1024], P('head')
Inputs may be any that keep to these rules, and one draw needn't show every extreme that they name: For every head, prefix_norm laid out as a 32 x 32 matrix is symmetric positive semidefinite.
All inputs are finite; a program needn't handle non-finite values.
Results may differ from a plain program's by a relative error of at most 0.012.
Values may be sent and summed in bfloat16 or wider, within the bound.
No kernel may reach another device: no remote copies, remote signals or barrier semaphores. Data moves between devices by JAX's collectives and lax.ppermute only.
A program may use at most 192 MiB of HBM per device.

v0:
```python
from functools import partial

import jax
import jax.numpy as jnp
from jax import lax
from jax.sharding import PartitionSpec as P

HIGHEST_PRECISION = lax.Precision.HIGHEST


def prefix(value, axis, combine, identity):
    count, index = (lax.axis_size(axis), lax.axis_index(axis))
    everything = jax.tree.map(
        lambda part, kind: lax.all_gather(part.astype(kind), axis),
        value,
        (jnp.bfloat16, jnp.bfloat16),
    )
    start = jax.tree.map(
        lambda part, zero: jnp.broadcast_to(jnp.asarray(zero, part.dtype), part.shape),
        value,
        identity,
    )

    def lap(k, before):
        reached = k < index
        new = combine(
            before, jax.tree.map(lambda part, own: part[k].astype(own.dtype), everything, value)
        )
        return jax.tree.map(lambda a, b: jnp.where(reached, a, b), new, before)

    return lax.fori_loop(0, count, lap, start)


def carried_in(value, axis, join, neutral):
    count = lax.axis_size(axis)
    place = lax.axis_index(axis)
    ahead = count - 1 - place
    gathered = jax.tree.map(
        lambda a, kind: lax.all_gather(a.astype(kind), axis),
        value,
        jax.tree.map(lambda a: jnp.bfloat16 if a.dtype == jnp.float32 else a.dtype, value),
    )
    state = jax.tree.map(lambda a, e: jnp.zeros_like(a) + jnp.asarray(e, a.dtype), value, neutral)

    def one(lap, state):
        source = count - 1 - lap
        return join(
            state,
            jax.tree.map(
                lambda a, own: lax.dynamic_index_in_dim(a, source, 0, False).astype(own.dtype),
                gathered,
                value,
            ),
        )

    return lax.fori_loop(0, ahead, one, state)


def sketch_map(values, sketch):
    left_map = jnp.einsum("hbd,de->hbe", values, sketch[0], precision=HIGHEST_PRECISION)
    right_map = jnp.einsum("hbd,de->hbe", values, sketch[1], precision=HIGHEST_PRECISION)
    return left_map * right_map * sketch.shape[2] ** (-0.5)


def square_features(sketched):
    outer_prod = sketched[:, :, :, None] * sketched[:, :, None, :]
    return outer_prod.reshape(sketched.shape[0], sketched.shape[1], -1)


def attend_block(carried, block_data, sketch):
    value_state, norm_state = carried
    query_block, key_block, value_block = block_data
    sketch_query = sketch_map(query_block, sketch)
    sketch_key = sketch_map(key_block, sketch)
    feat_query = square_features(sketch_query)
    block_size = query_block.shape[1]
    causal = lax.broadcasted_iota(jnp.int32, (block_size, block_size), 0) >= lax.broadcasted_iota(
        jnp.int32, (block_size, block_size), 1
    )
    dot_prod = jnp.einsum("hid,hjd->hij", sketch_query, sketch_key, precision=HIGHEST_PRECISION)
    scores = jnp.where(causal, dot_prod * dot_prod, jnp.zeros_like(dot_prod))
    numerator = jnp.einsum("hif,hfd->hid", feat_query, value_state, precision=HIGHEST_PRECISION)
    numerator = numerator + jnp.einsum(
        "hij,hjd->hid", scores, value_block, precision=HIGHEST_PRECISION
    )
    denominator = (
        1.0
        + jnp.einsum("hif,hf->hi", feat_query, norm_state, precision=HIGHEST_PRECISION)
        + scores.sum(-1)
    )
    outputs = numerator / denominator[:, :, None]
    feat_key = square_features(sketch_key)
    value_state = value_state + jnp.einsum(
        "hjf,hjd->hfd", feat_key, value_block, precision=HIGHEST_PRECISION
    )
    norm_state = norm_state + feat_key.sum(1)
    return ((value_state, norm_state), outputs)


def split_blocks(values, block_size):
    head_count, total_rows, depth_size = values.shape
    return values.reshape(head_count, total_rows // block_size, block_size, depth_size).transpose(
        1, 0, 2, 3
    )


def join_blocks(values):
    block_count, head_count, block_size, depth_size = values.shape
    return values.transpose(1, 0, 2, 3).reshape(head_count, block_count * block_size, depth_size)


def attend_local(query, key, value, value_state, norm_state, sketch):
    block_size = min(query.shape[1], 512)
    block_step = partial(attend_block, sketch=sketch)
    carried, outputs = lax.scan(
        block_step,
        (value_state, norm_state),
        (
            split_blocks(query, block_size),
            split_blocks(key, block_size),
            split_blocks(value, block_size),
        ),
    )
    return join_blocks(outputs)


def local_totals(key, value, sketch):
    block_size = min(key.shape[1], 512)

    def add_block(carried, block_data):
        key_block, value_block = block_data
        feat_key = square_features(sketch_map(key_block, sketch))
        state_sum = carried[0] + jnp.einsum(
            "hjf,hjd->hfd", feat_key, value_block, precision=HIGHEST_PRECISION
        )
        return ((state_sum, carried[1] + feat_key.sum(1)), None)

    feat_size = sketch.shape[2] * sketch.shape[2]
    start_state = jnp.zeros((key.shape[0], feat_size, key.shape[2]), jnp.float32)
    start_norm = jnp.zeros((key.shape[0], feat_size), jnp.float32)
    carried, unused = lax.scan(
        add_block,
        (start_state, start_norm),
        (split_blocks(key, block_size), split_blocks(value, block_size)),
    )
    return carried


def add_pair(earlier, later):
    return (earlier[0] + later[0], earlier[1] + later[1])


def pull_weight(gradient, weight):
    return lax.dot_general(
        gradient, weight, (((1,), (1,)), ((), ())), preferred_element_type=jnp.float32
    )


def body(
    inputs,
    w_query,
    w_key,
    w_value,
    sketch,
    prefix_state,
    prefix_norm,
    d_attn,
    d_state_end,
    d_norm_end,
):
    tok_rows = inputs.shape[0]
    width = w_query.shape[1]
    head_count = prefix_state.shape[0]
    head_size = width // head_count
    shard_cols = lax.all_gather(inputs, "head", axis=1, tiled=True)
    query, key, value = tuple(
        (
            jnp.dot(shard_cols, weight, preferred_element_type=jnp.float32)
            for weight in (w_query, w_key, w_value)
        )
    )

    def to_heads(values):
        return (
            values.reshape(tok_rows, head_count, head_size).transpose(1, 0, 2).astype(jnp.float32)
        )

    def flatten(values):
        return values.transpose(1, 0, 2).reshape(tok_rows, width).astype(jnp.bfloat16)

    query_heads = to_heads(lax.optimization_barrier(query.astype(jnp.bfloat16)))
    key_heads = to_heads(lax.optimization_barrier(key.astype(jnp.bfloat16)))
    value_heads = to_heads(lax.optimization_barrier(value.astype(jnp.bfloat16)))

    def totals_of(key_in, value_in):
        return local_totals(key_in, value_in, sketch)

    (state_here, norm_here), pull_totals = jax.vjp(totals_of, key_heads, value_heads)
    zero_state = jnp.zeros_like(prefix_state)
    zero_norm = jnp.zeros_like(prefix_norm)
    state_before, norm_before = prefix(
        (state_here, norm_here), "seq", add_pair, (zero_state, zero_norm)
    )
    state_prev = prefix_state + state_before
    norm_prev = prefix_norm + norm_before

    def outputs_of(query_in, key_in, value_in, state_in, norm_in):
        return attend_local(query_in, key_in, value_in, state_in, norm_in, sketch)

    unused, pull_local = jax.vjp(
        outputs_of, query_heads, key_heads, value_heads, state_prev, norm_prev
    )
    grad_query, grad_key, grad_value, cot_state, cot_norm = pull_local(to_heads(d_attn))
    d_query = flatten(grad_query)
    state_after, norm_after = carried_in(
        (cot_state, cot_norm), "seq", add_pair, (zero_state, zero_norm)
    )
    state_after = d_state_end + state_after
    norm_after = d_norm_end + norm_after
    extra_key, extra_value = pull_totals((state_after, norm_after))
    d_key = flatten(grad_key + extra_key)
    d_value = flatten(grad_value + extra_value)
    whole_term = (
        pull_weight(d_query, w_query) + pull_weight(d_key, w_key) + pull_weight(d_value, w_value)
    )
    d_input = lax.psum_scatter(
        whole_term.astype(jnp.bfloat16), "head", scatter_dimension=1, tiled=True
    )
    total_state, total_norm = (
        lax.psum(cot_state.astype(jnp.bfloat16), "seq").astype(jnp.float32),
        lax.psum(cot_norm.astype(jnp.bfloat16), "seq").astype(jnp.float32),
    )
    d_prefix_state = d_state_end + total_state
    d_prefix_norm = d_norm_end + total_norm
    return (d_input, d_query, d_key, d_value, d_prefix_state, d_prefix_norm)


def solution(mesh):
    return jax.shard_map(
        body,
        mesh=mesh,
        in_specs=(
            P("seq", "head"),
            P(None, "head"),
            P(None, "head"),
            P(None, "head"),
            P(),
            P("head", None, None),
            P("head", None),
            P("seq", "head"),
            P("head", None, None),
            P("head", None),
        ),
        out_specs=(
            P("seq", "head"),
            P("seq", "head"),
            P("seq", "head"),
            P("seq", "head"),
            P("head", None, None),
            P("head", None),
        ),
        check_vma=False,
    )
```

profile of v0, /device:TPU:0, one launch (start us, length us, event | category | flops | bytes accessed | tf_op | source)
XLA Modules:
  0.0 565.8 jit_solution(3602541207023008726)
XLA Ops:
  8.0 21.1 %all-gather.7.cloned.1.call-done = bf16[256,2048]{1,0:T(8,128)(2,1)} async-done(((bf16[256,512]{1,0:T(8,128)(2,1)}), bf16[256,2048]{1,0:T(8,128)(2,1)}) %all-gather.7.cloned.1.call-update) | async-done | bytes 1048592 | tf_op jit(solution)/shard_map/all_gather | solution.py:175
  47.1 5.4 convolution_convert_fusion.1
  55.8 33.7 %all_gather.28 = bf16[8,8,1024]{2,1,0:T(8,128)(2,1)} all-gather(bf16[1,8,1024]{2,1,0:T(8,128)(2,1)S(1)} %convert_element_type.143), channel_id=1, replica_groups=mesh['seq'=8,'head'=4] {'seq'}, dimensions={0}, use_global_device_ids=true | all-gather | bytes 147456 | tf_op jit(solution)/shard_map/all_gather | solution.py:14
  98.4 80.2 %all-gather.9.cloned.1.call-done = bf16[64,1024,64]{1,2,0:T(8,128)(2,1)} async-done(((bf16[8,1024,64]{1,2,0:T(8,128)(2,1)}), bf16[64,1024,64]{1,2,0:T(8,128)(2,1)}) %all-gather.9.cloned.1.call-update) | async-done | bytes 8388624 | tf_op jit(solution)/shard_map/all_gather | solution.py:14
  178.6 72.7 %while.22 = (s32[]{:T(128)}, f32[8,1024,64]{2,1,0:T(8,128)}, f32[8,1024]{1,0:T(8,128)S(1)}, s32[]{:T(128)}, bf16[8,8,1024,64]{2,3,1,0:T(8,128)(2,1)}, /*index=5*/bf16[8,8,1024]{2,1,0:T(8,128)(2,1)}, s32[]{:T(128)}, s32[]{:T(128)}) while((s32[]{:T(128)}, f32[8,1024,64]{2,1,0:T(8,128)}, f32[8,1024]{1,0:T(8,128)S(1)}, s32[]{:T(128)}, ...), condition=%wide.region_2.3_spmd.clone, body=%wide.region_1.0_spmd.clone.sunk | while | flops 2129924 | bytes 9519219 | solution.py:31
  189.7 5.4 add_select_fusion.4
  199.0 5.4 add_select_fusion.4
  208.2 5.4 add_select_fusion.4
  217.4 5.4 add_select_fusion.4
  226.7 5.4 add_select_fusion.4
  235.9 5.4 add_select_fusion.4
  245.2 5.4 add_select_fusion.4
  252.1 6.9 %fusion.50 = f32[8,1,256]{2,1,0:T(1,128)S(1)} fusion(f32[8,256,1024]{1,2,0:T(8,128)} %bitcast.130, f32[8,1024,1]{1,0,2:T(8,128)S(1)} %bitcast.161), kind=kOutput, calls=%fused_computation.77 | convolution fusion | flops 25165824 | bytes 8429568 | tf_op jit(solution)/shard_map/jvp()/while/body/eval_jaxpr/hif,hf->hi/dot_general | solution.py:88
  259.0 10.2 %convolution_convert_fusion = bf16[8,1024,64]{1,2,0:T(8,128)(2,1)} fusion(f32[8,256,1024]{1,2,0:T(8,128)S(1)} %bitcast.132, f32[8,256]{1,0:T(8,128)S(1)} %get-tuple-element.673, f32[256,512]{0,1:T(8,128)} %copy.74), kind=kOutput, calls=%fused_computation.36 | convolution fusion | flops 1611268096 | bytes 9969664 | tf_op jit(solution)/shard_map/transpose(jvp())/while/body/eval_jaxpr/hif,hfd->hid/dot_general | solution.py:82
  279.9 17.3 %fusion.4 = f32[8,256,64]{1,2,0:T(8,128)} fusion(f32[8,256,1024]{1,2,0:T(8,128)} %bitcast.137), kind=kOutput, calls=%fused_computation.25 | convolution fusion | flops 1610612736 | bytes 8912896 | tf_op jit(solution)/shard_map/transpose(jvp())/while/body/eval_jaxpr/hjf,hjd->hfd/dot_general | solution.py:93
  297.2 12.3 %fusion.31 = f32[8,256]{1,0:T(8,128)S(1)} fusion(f32[8,256,64]{1,2,0:T(8,128)S(1)} %fusion.13, f32[8,256,1024]{1,2,0:T(8,128)} %bitcast.131, f32[8,1024,64]{2,1,0:T(8,128)} %copy.78, f32[8,1024,64]{2,1,0:T(8,128)S(1)} %copy-done.3, f32[8,256,64]{1,2,0:T(8,128)S(1)} %bitcast.142, f32[8,256]{1,0:T(8,128)S(1)} %get-tuple-element.672), kind=kOutput, calls=%fused_computation.52 | convolution fusion | flops 1611659264 | bytes 13647872 | tf_op jit(solution)/shard_map/jvp()/while/body/eval_jaxpr/hif,hfd->hid/dot_general | solution.py:82
  309.6 7.2 %fusion.77 = bf16[8,1,1024]{2,1,0:T(2,128)(2,1)S(1)} fusion(f32[8,256,1024]{1,2,0:T(8,128)S(1)} %bitcast.135, f32[8,256,1]{1,0,2:T(8,128)S(1)} %get-tuple-element.677), kind=kOutput, calls=%fused_computation.106 | convolution fusion | flops 25165824 | bytes 8413184 | tf_op jit(solution)/shard_map/transpose(jvp())/while/body/eval_jaxpr/hif,hf->hi/dot_general | solution.py:88
  316.9 10.5 %multiply_add_fusion = f32[8,256,1024]{2,1,0:T(8,128)} fusion(f32[8,1024]{1,0:T(8,128)S(1)} %add.139, f32[8,256]{1,0:T(8,128)S(1)} %get-tuple-element.678, f32[8,1024,64]{2,1,0:T(8,128)S(1)} %copy-done.6, f32[8,1024,64]{2,1,0:T(8,128)S(1)} %copy-done.3, f32[8,256]{1,0:T(8,128)S(1)} %get-tuple-element.673, f32[256,512]{0,1:T(8,128)S(1)} %copy-done.9), kind=kOutput, calls=%fused_computation.12 | convolution fusion | flops 1615462400 | bytes 13156352 | tf_op jit(solution)/shard_map/transpose(jvp())/while/body/eval_jaxpr/hif,hfd->hid/dot_general | solution.py:82
  327.3 9.2 %copy.85 = f32[8,256,1024]{1,2,0:T(8,128)} copy(f32[8,256,1024]{2,1,0:T(8,128)} %multiply_add_fusion) | data formatting | bytes 16777216 | tf_op jit(solution)/shard_map/transpose(jvp())/while/body/eval_jaxpr/hif,hfd->hid/add_any | solution.py:82
  336.5 35.8 %psum.15 = bf16[8,1024]{1,0:T(8,128)(2,1)S(1)} all-reduce(bf16[8,1024]{1,0:T(8,128)(2,1)S(1)} %bitcast.162), channel_id=1, replica_groups=mesh['seq'=8,'head'=4] {'seq'}, use_global_device_ids=true, to_apply=%region_15.16 | all-reduce | flops 8192 | bytes 32768 | tf_op jit(solution)/shard_map/psum | solution.py:231
  372.3 32.9 %all-gather.2 = bf16[64,1024]{1,0:T(8,128)(2,1)} all-gather(bf16[8,1024]{1,0:T(8,128)(2,1)S(1)} %bitcast.163), channel_id=4, replica_groups=mesh['seq'=8,'head'=4] {'seq'}, dimensions={0}, use_global_device_ids=true | all-gather | bytes 147456 | tf_op jit(solution)/shard_map/all_gather | solution.py:39
  426.7 63.7 %while.21 = (s32[]{:T(128)}, f32[8,1024,64]{2,1,0:T(8,128)}, f32[8,1024]{1,0:T(8,128)S(1)}, s32[]{:T(128)}, bf16[8,8,1024,64]{2,3,1,0:T(8,128)(2,1)}, /*index=5*...) while((s32[]{:T(128)}, f32[8,1024,64]{2,1,0:T(8,128)}, ...), condition=%wide.region_10.11_spmd, body=%wide.region_9.10_spmd.sunk | while | flops 1064966 | bytes 9519259 | solution.py:56
  429.9 5.3 convert_add_fusion.6
  439.0 5.3 convert_add_fusion.6
  457.2 5.3 convert_add_fusion.6
  466.3 5.3 convert_add_fusion.6
  484.5 5.3 convert_add_fusion.6
  491.1 10.7 %broadcast_add_fusion = f32[8,256,1024]{2,1,0:T(8,128)} fusion(f32[8,1024]{1,0:T(8,128)S(1)} %get-tuple-element.676, bf16[8,256,64]{1,2,0:T(8,128)(2,1)} %bitcast.145, f32[8,1024,64]{2,1,0:T(8,128)} %copy.91, f32[8,1024,64]{2,1,0:T(8,128)} %get-tuple-element.565), kind=kOutput, calls=%fused_computation.13 | convolution fusion | flops 1613234176 | bytes 12877824 | tf_op jit(solution)/shard_map/transpose(jvp())/while/body/eval_jaxpr/hjf,hjd->hfd/dot_general | solution.py:133
  501.8 9.3 %copy.93 = f32[8,256,1024]{1,2,0:T(8,128)} copy(f32[8,256,1024]{2,1,0:T(8,128)} %broadcast_add_fusion) | data formatting | bytes 16777216 | tf_op jit(solution)/shard_map/transpose(jvp())/while/body/eval_jaxpr/hjf,hjd->hfd/add_any | solution.py:133
  511.1 8.9 %multiply_reduce_fusion = (f32[8,256,32]{1,2,0:T(8,128)S(1)}, f32[8,256,32]{1,2,0:T(8,128)S(1)}) fusion(f32[8,256,32]{1,2,0:T(8,128)S(1)} %get-tuple-element.681, f32[8,256,1024]{1,2,0:T(8,128)} %copy.93, f32[8,256,32,32]{1,3,2,0:T(8,128)} %bitcast.141), kind=kLoop, calls=%fused_computation.6 | loop fusion | flops 8257536 | bytes 17563648 | tf_op jit(solution)/shard_map/transpose(jvp())/while/body/eval_jaxpr/reduce_sum | solution.py:66
  524.8 10.1 %fusion.26 = bf16[8,256,64]{1,2,0:T(8,128)(2,1)S(1)} fusion(f32[8,256,64]{1,2,0:T(8,128)S(1)} %copy-done.32, f32[8,256,1024]{1,2,0:T(8,128)} %bitcast.138, f32[8,1024,64]{2,1,0:T(8,128)S(1)} %copy-done.7, f32[8,1024,64]{2,1,0:T(8,128)S(1)} %copy-done.1), kind=kOutput, calls=%fused_computation.46 | convolution fusion | flops 1611399168 | bytes 13369344 | tf_op jit(solution)/shard_map/transpose(jvp())/while/body/eval_jaxpr/hjf,hjd->hfd/dot_general | solution.py:133
  542.9 16.2 %reduce-scatter.2.cloned.1.call-done = bf16[256,512]{1,0:T(8,128)(2,1)} async-done(((bf16[256,2048]{1,0:T(8,128)(2,1)}), bf16[256,512]{1,0:T(8,128)(2,1)}) %reduce-scatter.2.cloned.1.call-update) | async-done | bytes 262160 | tf_op jit(solution)/shard_map/reduce_scatter | solution.py:226
  (184 shorter events, 149.0 us)
Async XLA Ops:
  7.2 46.6 %copy-start = (bf16[2048,512]{1,0:T(8,128)(2,1)S(1)}, bf16[2048,512]{1,0:T(8,128)(2,1)}, u32[]{:S(2)}) copy-start(bf16[2048,512]{1,0:T(8,128)(2,1)} %param.15) | copy-start | bytes 6291460
  7.2 24.6 %copy-start.31 = (f32[2,64,32]{1,2,0:T(8,128)S(1)}, f32[2,64,32]{1,2,0:T(8,128)}, u32[]{:S(2)}) copy-start(f32[2,64,32]{1,2,0:T(8,128)} %param.18) | copy-start | bytes 49156
  7.2 21.9 %all-gather.7.cloned.1.call-start = ((), (), s32[]{:S(2)}) async-start(), calls=%async_computation.1 | async-start | bytes 1310720 | tf_op jit(solution)/shard_map/all_gather | solution.py:175
  7.9 170.7 %all-gather.9.cloned.1.call-start = ((), (), s32[]{:S(2)}) async-start(), calls=%async_computation.4 | async-start | bytes 9437184 | tf_op jit(solution)/shard_map/all_gather | solution.py:14
  36.5 7.3 %copy-start.12 = (bf16[256,512]{0,1:T(8,128)(2,1)}, bf16[256,512]{0,1:T(8,128)(2,1)S(1)}, u32[]{:S(2)}) copy-start(bf16[256,512]{0,1:T(8,128)(2,1)S(1)} %copy.75) | copy-start | bytes 786436
  47.1 5.5 copy-start.34
  52.6 371.2 %all-gather.11.cloned.1.call-start = ((), (), s32[]{:S(2)}) async-start(), calls=%async_computation.5 | async-start | bytes 9437184 | tf_op jit(solution)/shard_map/all_gather | solution.py:39
  89.8 8.6 %copy-start.21 = (f32[8,256,32]{1,2,0:T(8,128)}, f32[8,256,32]{1,2,0:T(8,128)S(1)}, u32[]{:S(2)}) copy-start(f32[8,256,32]{1,2,0:T(8,128)S(1)} %fusion.57) | copy-start | bytes 786436
  252.1 6.9 %copy-start.2 = (f32[8,256,32,32]{1,3,2,0:T(8,128)S(1)}, f32[8,256,32,32]{1,3,2,0:T(8,128)}, u32[]{:S(2)}) copy-start(f32[8,256,32,32]{1,3,2,0:T(8,128)} %broadcast_multiply_fusion.1) | copy-start | bytes 25165828
  273.1 3.9 copy-start.13
  279.9 17.3 %copy-start.3 = (f32[8,1024,64]{2,1,0:T(8,128)S(1)}, f32[8,1024,64]{2,1,0:T(8,128)}, u32[]{:S(2)}) copy-start(f32[8,1024,64]{2,1,0:T(8,128)} %get-tuple-element.563) | copy-start | bytes 6291460
  279.9 17.4 %copy-start.9 = (f32[256,512]{0,1:T(8,128)S(1)}, f32[256,512]{0,1:T(8,128)}, u32[]{:S(2)}) copy-start(f32[256,512]{0,1:T(8,128)} %copy.74) | copy-start | bytes 1572868
  297.2 12.4 %slice-start = ((s8[8388608]{0:T(1024)(128)(4,1)}), s8[4194304]{0:T(1024)(128)(4,1)S(1)}, s32[]{:S(2)}) async-start(s8[8388608]{0:T(1024)(128)(4,1)} %bitcast.133), calls=%async_computation.6 | async-start | bytes 8388608
  297.2 12.4 %slice-start.1 = ((s8[8388608]{0:T(1024)(128)(4,1)}), s8[4194304]{0:T(1024)(128)(4,1)S(1)}, s32[]{:S(2)}) async-start(s8[8388608]{0:T(1024)(128)(4,1)} %bitcast.133), calls=%async_computation.7 | async-start | bytes 8388608
  309.6 7.2 %copy-start.6 = (f32[8,1024,64]{2,1,0:T(8,128)S(1)}, f32[8,1024,64]{2,1,0:T(8,128)}, u32[]{:S(2)}) copy-start(f32[8,1024,64]{2,1,0:T(8,128)} %copy.78) | copy-start | bytes 6291460
  336.5 71.7 %copy-start.11 = (f32[8,256,32]{1,2,0:T(8,128)S(1)}, f32[8,256,32]{1,2,0:T(8,128)}, u32[]{:S(2)}) copy-start(f32[8,256,32]{1,2,0:T(8,128)} %copy-done.10) | copy-start | bytes 786436
  372.3 35.9 %copy-start.28 = (f32[8,256,32]{1,2,0:T(8,128)S(1)}, f32[8,256,32]{1,2,0:T(8,128)}, u32[]{:S(2)}) copy-start(f32[8,256,32]{1,2,0:T(8,128)} %get-tuple-element.641) | copy-start | bytes 786436
  372.3 35.9 %copy-start.29 = (f32[8,256,32]{1,2,0:T(8,128)S(1)}, f32[8,256,32]{1,2,0:T(8,128)}, u32[]{:S(2)}) copy-start(f32[8,256,32]{1,2,0:T(8,128)} %get-tuple-element.643) | copy-start | bytes 786436
  372.3 38.0 %copy-start.23 = (f32[8,256,32]{1,2,0:T(8,128)S(1)}, f32[8,256,32]{1,2,0:T(8,128)}, u32[]{:S(2)}) copy-start(f32[8,256,32]{1,2,0:T(8,128)} %get-tuple-element.682) | copy-start | bytes 786436
  405.2 6.5 %copy-start.5 = (f32[8,256,1024]{1,2,0:T(8,128)S(1)}, f32[8,256,1024]{1,2,0:T(8,128)}, u32[]{:S(2)}) copy-start(f32[8,256,1024]{1,2,0:T(8,128)} %copy.85) | copy-start | bytes 25165828
  410.3 5.6 copy-start.17
  411.7 5.5 copy-start.30
  418.6 5.2 copy-start.19
  423.8 115.5 %all-reduce.2.cloned.1.call-start = ((), (), s32[]{:S(2)}) async-start(), calls=%async_computation.3 | async-start | bytes 2097152 | tf_op jit(solution)/shard_map/psum | solution.py:230
  424.4 134.8 %reduce-scatter.2.cloned.1.call-start = ((), (), s32[]{:S(2)}) async-start(), calls=%async_computation.2 | async-start | bytes 1310720 | tf_op jit(solution)/shard_map/reduce_scatter | solution.py:226
  426.7 63.7 %copy-start.35 = (f32[8,1024]{1,0:T(8,128)S(1)}, f32[8,1024]{1,0:T(8,128)}, u32[]{:S(2)}) copy-start(f32[8,1024]{1,0:T(8,128)} %param.23) | copy-start | bytes 98308
  511.1 8.9 %copy-start.24 = (f32[8,256,32]{1,2,0:T(8,128)S(1)}, f32[8,256,32]{1,2,0:T(8,128)}, u32[]{:S(2)}) copy-start(f32[8,256,32]{1,2,0:T(8,128)} %get-tuple-element.682) | copy-start | bytes 786436
  511.1 9.6 %copy-start.16 = (f32[8,256,32]{1,2,0:T(8,128)S(1)}, f32[8,256,32]{1,2,0:T(8,128)}, u32[]{:S(2)}) copy-start(f32[8,256,32]{1,2,0:T(8,128)} %copy-done.15) | copy-start | bytes 786436
  511.1 10.2 %copy-start.18 = (f32[8,256,32]{1,2,0:T(8,128)S(1)}, f32[8,256,32]{1,2,0:T(8,128)}, u32[]{:S(2)}) copy-start(f32[8,256,32]{1,2,0:T(8,128)} %copy-done.17) | copy-start | bytes 786436
  511.1 10.2 %copy-start.26 = (f32[8,256,64]{1,2,0:T(8,128)S(1)}, f32[8,256,64]{1,2,0:T(8,128)}, u32[]{:S(2)}) copy-start(f32[8,256,64]{1,2,0:T(8,128)} %fusion.45) | copy-start | bytes 1572868
  511.1 10.9 %copy-start.25 = (bf16[2048,512]{1,0:T(8,128)(2,1)S(1)}, bf16[2048,512]{1,0:T(8,128)(2,1)}, u32[]{:S(2)}) copy-start(bf16[2048,512]{1,0:T(8,128)(2,1)} %param.16) | copy-start | bytes 6291460
  524.8 10.1 %copy-start.27 = (bf16[2048,512]{1,0:T(8,128)(2,1)S(1)}, bf16[2048,512]{1,0:T(8,128)(2,1)}, u32[]{:S(2)}) copy-start(bf16[2048,512]{1,0:T(8,128)(2,1)} %param.17) | copy-start | bytes 6291460
  (11 other events, 26.6 us)
Sparse Core Ops, SparseCore 0:
  9.6 19.4 all-gather.6
  52.7 125.9 all-gather.8
  269.4 125.1 all-gather.10
  427.8 75.4 all-reduce.1
  536.9 22.2 reduce-scatter.1
where the time goes:
time: 572 us; the launch traced here: 566 us
  matrix products  129 us (23%)
  waiting for transfers between devices  119 us (21%)
  other arithmetic  116 us (20%)
  blocking collectives  102 us (18%)
  local copies, waits for them, and re-layouts  85.2 us (15%)
  between operations  14.6 us (3%)
    all_gather x1, waiting for transfers between devices, prefix(): lax.all_gather(part.astype(kind), axis)  80.2 us
    select_n x16, other arithmetic, lap(): return jax.tree.map(lambda a, b: jnp.where(reached, a, b), new, before)  47.8 us
    add x14, other arithmetic, add_pair(): return (earlier[0] + later[0], earlier[1] + later[1])  41.9 us
    psum x1, blocking collectives, body(): lax.psum(cot_norm.astype(jnp.bfloat16), 'seq').astype(jnp.float32)  35.8 us
    all_gather x1, blocking collectives, prefix(): lax.all_gather(part.astype(kind), axis)  33.7 us
    dot_general x3, matrix products, attend_block(): jnp.einsum('hif,hfd->hid', feat_query, value_state, precision=HIGHEST_PRE...  33.1 us
    all_gather x1, blocking collectives, carried_in(): lax.all_gather(a.astype(kind), axis)  32.9 us
    dot_general x3, matrix products, add_block(): jnp.einsum('hjf,hjd->hfd', feat_key, value_block, precision=HIGHEST_PRECI...  26.2 us
  transfers between devices with their start and end apart: 5, of which 3 were waited for; matrix products, arithmetic and copies ran while one was open for 38% of the time, Pallas kernels for 0%

commit v1 on v0

v1 whole, which is shorter than its diff:
```python
import math
from functools import partial

import jax
import jax.numpy as jnp
import numpy as np
from jax import lax
from jax.experimental import pallas as pl
from jax.experimental.pallas import tpu as pltpu
from jax.sharding import Mesh, PartitionSpec as P

F32 = jnp.float32
BF16 = jnp.bfloat16
LANES = 128
VMEM = pltpu.VMEM
MIB = 1024 * 1024

NN = (((1,), (0,)), ((), ()))
NT = (((1,), (1,)), ((), ()))
TN = (((0,), (0,)), ((), ()))


def mm(a, b, dims=NN):
    return lax.dot_general(a, b, dims, preferred_element_type=F32)


def split(x):
    hi = x.astype(BF16)
    return hi, (x - hi.astype(F32)).astype(BF16)


def tile_count(sk):
    return -(-(sk // 2 + 1) // (LANES // sk))


def pair_map(sk):
    step = LANES // sk
    width = tile_count(sk) * LANES
    lane = np.arange(width)
    tile, within = lane // LANES, lane % LANES
    j, a = within // sk, within % sk
    first, second = (a + j) % sk, (a - step * tile) % sk
    keep = step * tile + j <= sk // 2
    table = np.zeros((sk * sk, width), np.float32)
    for one in lane[keep]:
        x, y = first[one], second[one]
        r = step * tile[one] + j[one]
        if r == 0:
            table[x * sk + y, one] = 1.0
        else:
            value = 0.5 if 2 * r == sk else 1.0
            table[x * sk + y, one] = value
            table[y * sk + x, one] = value
    return table


def lane_weights(sk, width):
    lane = lax.broadcasted_iota(jnp.int32, (1, width), 1)
    r = (LANES // sk) * (lane // LANES) + (lane % LANES) // sk
    return jnp.where(
        r <= sk // 2, jnp.where((r == 0) | (2 * r == sk), 1.0, 2.0), 0.0
    ).astype(F32)


def sketched(x, weights):
    both = mm(jnp.concatenate([x, x], axis=1), weights)
    return tuple(both[:, LANES * i : LANES * (i + 1)] for i in range(4))


def turned(e, sk, tiles):
    step = LANES // sk
    return [e] + [pltpu.roll(e, step * t, 1) for t in range(1, tiles)]


def features(e, d, sk, tiles):
    return jnp.concatenate([(d * x).astype(BF16) for x in turned(e, sk, tiles)], axis=1)


def feature_pull(cot, e, d, sk, tiles):
    step = LANES // sk
    cot_e = cot_d = None
    for t, x in enumerate(turned(e, sk, tiles)):
        part = cot[:, LANES * t : LANES * (t + 1)]
        to_d = part * x
        to_e = part * d
        if t:
            to_e = pltpu.roll(to_e, LANES - step * t, 1)
        cot_d = to_d if cot_d is None else cot_d + to_d
        cot_e = to_e if cot_e is None else cot_e + to_e
    return cot_e, cot_d


def lane_of(rows):
    return lax.broadcasted_iota(jnp.int32, (rows, LANES), 1)


def base_kernel(sk, start_ref, state_ref, norm_ref, dstate_ref, dnorm_ref, map_ref, fwd_ref, bwd_ref, rows_ref):
    table = map_ref[...]
    half = state_ref.shape[1]

    def mapped(x):
        hi, lo = split(x)
        return mm(hi, table) + mm(lo, table)

    row = start_ref[0] + pl.program_id(0)
    for which, (s_ref, n_ref, o_ref, scale) in enumerate(
        ((state_ref, norm_ref, fwd_ref, 1.0), (dstate_ref, dnorm_ref, bwd_ref, 1.0 / half))
    ):
        rows_ref[which] = mapped(n_ref[...]) * scale
        o_ref[0, :half] = mapped(s_ref[0])
        o_ref[0, half:] = jnp.broadcast_to(
            rows_ref[which, pl.ds(row, 1), :], (LANES - half, o_ref.shape[2])
        )


def project_kernel(hd, count, where_ref, *refs):
    pieces = refs[:count]
    weights = refs[count:-1]
    out = refs[-1]
    depth = pieces[0].shape[1]
    sums = []
    for w in weights:
        total = None
        for i, x in enumerate(pieces):
            rows = pl.ds(pl.multiple_of(where_ref[i] * depth, depth), depth)
            part = mm(x[...], w[rows, :])
            total = part if total is None else total + part
        sums.append(total)
    heads = out.shape[0]
    if len(sums) == 2:
        for h in range(heads):
            cols = slice(h * hd, (h + 1) * hd)
            out[h] = jnp.concatenate([sums[0][:, cols], sums[1][:, cols]], axis=1).astype(BF16)
    else:
        half = out.shape[1]
        for h in range(heads):
            cols = slice(h * hd, (h + 1) * hd)
            out[h] = jnp.concatenate(
                [sums[0][:half, cols], sums[0][half:, cols]], axis=1
            ).astype(BF16)


def key_kernel(sk, hd, vk_ref, base_ref, wb_ref, state_ref, feat_ref, kdot_ref, total_ref):
    blocks, _, rows, _ = vk_ref.shape
    width = base_ref.shape[2]
    tiles = width // LANES
    weights = lane_weights(sk, width)
    lane = lane_of(rows)
    state = base_ref[0]
    for c in range(blocks):
        state_ref[0, c] = state.astype(BF16)
        vk = vk_ref[c, 0]
        e0, e1, d0, d1 = sketched(vk, wb_ref[...])
        e, d = e0 * e1, d0 * d1
        feat = features(e, d, sk, tiles)
        feat_ref[0, c] = feat
        hi, lo = split(e)
        kdot_ref[0, c] = jnp.where(
            lane < 2 * sk, hi.astype(F32), jnp.where(lane < 3 * sk, lo.astype(F32), 0.0)
        ).astype(BF16)
        ones = jnp.where(lane < hd, vk.astype(F32), 1.0).astype(BF16)
        state = state + mm(ones, feat, TN) * weights
    total_ref[0] = state


def query_kernel(
    sk, hd, q_ref, g_ref, vk_ref, kdot_ref, state_ref, wa_ref, wb_ref, ba_ref, bb_ref,
    dq_ref, qdot_ref, dn_ref, cot_ref, total_ref,
):
    blocks, _, rows, _ = vk_ref.shape
    half = rows // 2
    width = state_ref.shape[3]
    tiles = width // LANES
    lane = lane_of(rows)
    low = lane < hd
    causal = lax.broadcasted_iota(jnp.int32, (rows, rows), 0) >= lax.broadcasted_iota(
        jnp.int32, (rows, rows), 1
    )
    r_i = lax.broadcasted_iota(jnp.int32, (2 * LANES, LANES), 0) % LANES
    c_i = lax.broadcasted_iota(jnp.int32, (2 * LANES, LANES), 1)
    adder = jnp.where((r_i < hd) & (c_i >= hd), -1.0 / (LANES - hd), 0.0).astype(BF16)
    total = jnp.zeros((LANES, width), F32)
    for c in range(blocks):
        q = q_ref[c, 0]
        top = sketched(q, wa_ref[...])
        bottom = sketched(q, wb_ref[...])
        e0, e1, d0, d1 = tuple(jnp.concatenate([a, b], axis=0) for a, b in zip(top, bottom))
        e, d = e0 * e1, d0 * d1
        feat = features(e, d, sk, tiles)
        hi, lo = split(e)
        qdot = jnp.where(
            (lane >= sk) & (lane < 2 * sk), lo.astype(F32), jnp.where(lane < 3 * sk, hi.astype(F32), 0.0)
        ).astype(BF16)
        qdot_ref[0, c] = qdot
        kdot = kdot_ref[0, c]
        state = state_ref[0, c]
        ones = jnp.where(low, vk_ref[c, 0].astype(F32), 1.0).astype(BF16)
        dots = jnp.where(causal, mm(qdot, kdot, NT), 0.0)
        num = mm(feat, state, NT) + mm((dots * dots).astype(BF16), ones)
        inv = 1.0 / (1.0 + num)
        inv = jnp.where(low, pltpu.roll(inv, hd, 1), inv)
        g = g_ref[c, 0].astype(F32)
        g = jnp.concatenate([g, pltpu.roll(g, hd, 1)], axis=0)
        g_hi, g_lo = split(jnp.where(low, g * num, 0.0))
        den = mm(jnp.concatenate([g_hi, g_lo], axis=1), adder)
        dn = (jnp.where(low, g, den * inv) * inv).astype(BF16)
        dn_ref[0, c] = dn
        cot_dots = (2.0 * dots * mm(dn, ones, NT)).astype(BF16)
        near = mm(cot_dots, kdot)
        cot = mm(dn, state)
        cot_e, cot_d = feature_pull(cot, e, d, sk, tiles)
        cot_e = cot_e + jnp.where((lane < sk) | (lane >= 2 * sk), near, 0.0)
        back = jnp.concatenate(
            [(cot_e * e1).astype(BF16), (cot_e * e0).astype(BF16), (cot_d * d1).astype(BF16), (cot_d * d0).astype(BF16)],
            axis=1,
        )
        dq_ref[c, 0] = (mm(back[:half], ba_ref[...]) + mm(back[half:], bb_ref[...])).astype(BF16)
        here = mm(dn, feat, TN)
        cot_ref[0, c] = here
        total = total + here
    total_ref[0] = total[: total_ref.shape[1]].astype(BF16)


def reverse_kernel(
    sk, hd, vk_ref, feat_ref, kdot_ref, qdot_ref, dn_ref, cot_ref, base_ref, wb_ref, bb_ref, dvk_ref, end_ref
):
    blocks, _, rows, _ = vk_ref.shape
    width = base_ref.shape[2]
    tiles = width // LANES
    weights = lane_weights(sk, width)
    lane = lane_of(rows)
    low = lane < hd
    causal = lax.broadcasted_iota(jnp.int32, (rows, rows), 0) <= lax.broadcasted_iota(
        jnp.int32, (rows, rows), 1
    )
    state = base_ref[0]
    for c in reversed(range(blocks)):
        after = state.astype(BF16)
        vk = vk_ref[c, 0]
        e0, e1, d0, d1 = sketched(vk, wb_ref[...])
        e, d = e0 * e1, d0 * d1
        qdot = qdot_ref[0, c]
        dn = dn_ref[0, c]
        ones = jnp.where(low, vk.astype(F32), 1.0).astype(BF16)
        dots = jnp.where(causal, mm(kdot_ref[0, c], qdot, NT), 0.0)
        cot_dots = (2.0 * dots * mm(ones, dn, NT)).astype(BF16)
        near = mm(cot_dots, qdot)
        dv = mm(feat_ref[0, c], after, NT) + mm((dots * dots).astype(BF16), dn)
        cot = mm(ones, after)
        cot_e, cot_d = feature_pull(cot, e, d, sk, tiles)
        cot_e = cot_e + jnp.where(lane < 2 * sk, near, 0.0)
        back = jnp.concatenate(
            [(cot_e * e1).astype(BF16), (cot_e * e0).astype(BF16), (cot_d * d1).astype(BF16), (cot_d * d0).astype(BF16)],
            axis=1,
        )
        dvk_ref[c, 0] = (jnp.where(low, dv, 0.0) + mm(back, bb_ref[...])).astype(BF16)
        state = state + cot_ref[0, c] * weights
    end_ref[0] = state


def unpack_query_kernel(hd, dq_ref, w_ref, out_ref, part_ref):
    heads, half, _ = dq_ref.shape
    low = lane_of(half) < hd
    for pair in range(heads // 2):
        a = dq_ref[2 * pair].astype(F32)
        b = dq_ref[2 * pair + 1].astype(F32)
        cols = slice(pair * LANES, (pair + 1) * LANES)
        out_ref[:half, cols] = jnp.where(low, a, pltpu.roll(b, hd, 1)).astype(BF16)
        out_ref[half:, cols] = jnp.where(low, pltpu.roll(a, hd, 1), b).astype(BF16)
    whole = out_ref[...]
    depth = out_ref.shape[1]
    for i in range(w_ref.shape[0] // depth):
        part_ref[i] = mm(whole, w_ref[i * depth : (i + 1) * depth, :], NT)


def unpack_key_kernel(hd, order_ref, dvk_ref, wk_ref, wv_ref, part_ref, dk_ref, dv_ref, out_ref):
    heads, rows, _ = dvk_ref.shape
    low = lane_of(rows) < hd
    for pair in range(heads // 2):
        a = dvk_ref[2 * pair].astype(F32)
        b = dvk_ref[2 * pair + 1].astype(F32)
        cols = slice(pair * LANES, (pair + 1) * LANES)
        dv_ref[:, cols] = jnp.where(low, a, pltpu.roll(b, hd, 1)).astype(BF16)
        dk_ref[:, cols] = jnp.where(low, pltpu.roll(a, hd, 1), b).astype(BF16)
    dk = dk_ref[...]
    dv = dv_ref[...]
    depth = dk_ref.shape[1]
    for i in range(out_ref.shape[0]):
        block = order_ref[i]
        at = pl.ds(pl.multiple_of(block * depth, depth), depth)
        total = part_ref[block] + mm(dk, wk_ref[at, :], NT) + mm(dv, wv_ref[at, :], NT)
        out_ref[i] = total.astype(BF16)


def expand_kernel(hd, all_ref, dstate_ref, dnorm_ref, map_ref, state_ref, norm_ref):
    heads, rows, width = all_ref.shape
    flat = all_ref[...].reshape(heads * rows, width)
    spread = mm(flat, map_ref[...], NT)
    for h in range(heads):
        state_ref[h] = dstate_ref[h] + spread[h * rows : h * rows + hd]
        norm_ref[h : h + 1] = dnorm_ref[h : h + 1] + spread[h * rows + hd : h * rows + hd + 1] * float(LANES - hd)


def params(mib, **more):
    return pltpu.CompilerParams(vmem_limit_bytes=mib * MIB, **more)


def shape(dims, kind):
    return jax.ShapeDtypeStruct(dims, kind)


def spec(block, index=None):
    if index is None:
        index = lambda h, *_: (h,) + (0,) * (len(block) - 1)
    return pl.BlockSpec(block, index)


def fixed(array):
    dims = array.shape
    return pl.BlockSpec(dims, lambda *_: (0,) * len(dims))


def hop(x, axis, distance):
    count = lax.axis_size(axis)
    return lax.ppermute(x, axis, [(i, i ^ distance) for i in range(count)])


def body(groups, local, inputs, w_query, w_key, w_value, sketch, prefix_state, prefix_norm, d_attn, d_state_end, d_norm_end):
    rows, depth = inputs.shape
    width = w_query.shape[1]
    heads, feat, hd = prefix_state.shape
    sk = sketch.shape[2]
    tiles = tile_count(sk)
    lanes = tiles * LANES
    half = rows // 2
    mine = heads // local
    ranks = lax.axis_size("head")
    rank = lax.axis_index("head")
    place = lax.axis_index("local")
    group = lax.axis_index("group")

    def exchange(x):
        return lax.all_to_all(x, "local", 0, 0, tiled=True) if local > 1 else x

    pieces = {0: inputs}
    distance = ranks // 2
    while distance:
        pieces.update({at ^ distance: hop(x, "head", distance) for at, x in list(pieces.items())})
        distance //= 2
    keys = sorted(pieces)
    where = jnp.stack([rank ^ at for at in keys]).astype(jnp.int32)

    grad = d_attn.reshape(2, half, heads, hd).transpose(2, 1, 0, 3).reshape(heads, half, 2 * hd)
    grad = exchange(grad).reshape(local, mine, half, LANES)

    step = LANES // sk
    left, right = sketch[0], sketch[1] * sk ** (-0.5)
    turns = np.concatenate([(np.arange(sk) + j) % sk for j in range(step)])
    full = jnp.concatenate(
        [jnp.tile(left, (1, step)), jnp.tile(right, (1, step)), left[:, turns], right[:, turns]], axis=1
    )
    hi = lax.reduce_precision(full, 8, 7)
    lo = (full - hi).astype(BF16)
    hi = hi.astype(BF16)
    none = jnp.zeros_like(hi)
    wa = jnp.concatenate([hi, none, lo, none], axis=0)
    wb = jnp.concatenate([none, hi, none, lo], axis=0)
    ba = jnp.concatenate([hi, none], axis=0).T
    bb = jnp.concatenate([none, hi], axis=0).T
    table = jnp.asarray(pair_map(sk), BF16)

    state_t = prefix_state.transpose(0, 2, 1)
    dstate_t = d_state_end.transpose(0, 2, 1)
    start = (place * mine).astype(jnp.int32)[None]
    one_head = pl.BlockSpec((1, hd, feat), lambda h, s: (s[0] + h, 0, 0))
    state_spec = spec((1, LANES, lanes))
    base, base_after = pl.pallas_call(
        partial(base_kernel, sk),
        grid_spec=pltpu.PrefetchScalarGridSpec(
            num_scalar_prefetch=1,
            grid=(mine,),
            in_specs=[one_head, fixed(prefix_norm), one_head, fixed(d_norm_end), fixed(table)],
            out_specs=[state_spec] * 2,
            scratch_shapes=[pltpu.VMEM((2, heads, lanes), F32)],
        ),
        out_shape=[shape((mine, LANES, lanes), F32)] * 2,
        compiler_params=params(24),
        name="base_states",
    )(start, state_t, prefix_norm, dstate_t, d_norm_end, table)

    smem = pl.BlockSpec(memory_space=pltpu.SMEM)
    vmem = pl.BlockSpec(memory_space=pltpu.VMEM)

    def project(name, weights, out_rows):
        return pl.pallas_call(
            partial(project_kernel, hd, len(keys)),
            in_specs=[smem] + [vmem] * (len(keys) + len(weights)),
            out_specs=vmem,
            out_shape=shape((heads, out_rows, LANES), BF16),
            compiler_params=params(24),
            name=name,
        )(where, *[pieces[at] for at in keys], *weights)

    vk = project("project_key_value", (w_value, w_key), rows)
    vk = exchange(vk).reshape(local, mine, rows, LANES)
    query = project("project_query", (w_query,), half)
    query = exchange(query).reshape(local, mine, half, LANES)

    across = lambda n: spec((local, 1, n, LANES), lambda h: (0, h, 0, 0))
    own = lambda *dims: spec((1,) + dims, lambda h: (h,) + (0,) * len(dims))

    def key_side(start_state):
        return pl.pallas_call(
            partial(key_kernel, sk, hd),
            grid=(mine,),
            in_specs=[across(rows), state_spec, fixed(wb)],
            out_specs=[own(local, LANES, lanes), own(local, rows, lanes), own(local, rows, LANES), state_spec],
            out_shape=[
                shape((mine, local, LANES, lanes), BF16),
                shape((mine, local, rows, lanes), BF16),
                shape((mine, local, rows, LANES), BF16),
                shape((mine, LANES, lanes), F32),
            ],
            compiler_params=params(32),
            name="key_side",
        )(vk, start_state, wb)

    def of_groups(x, wanted):
        everything = lax.all_gather(x.astype(BF16), "group").astype(F32)
        chosen = wanted(jnp.arange(groups))
        return jnp.where(chosen.reshape((groups,) + (1,) * x.ndim), everything, 0.0).sum(0)

    if groups > 1:
        sums = key_side(jnp.zeros_like(base))[3]
        base = base + of_groups(sums, lambda at: at < group)
    states, key_feats, kdot, _ = key_side(base)

    query_out = pl.pallas_call(
        partial(query_kernel, sk, hd),
        grid=(mine,),
        in_specs=[
            across(half), across(half), across(rows), own(local, rows, LANES), own(local, LANES, lanes),
            fixed(wa), fixed(wb), fixed(ba), fixed(bb),
        ],
        out_specs=[
            across(half), own(local, rows, LANES), own(local, rows, LANES), own(local, LANES, lanes),
            own(hd + 16, lanes),
        ],
        out_shape=[
            shape((local, mine, half, LANES), BF16),
            shape((mine, local, rows, LANES), BF16),
            shape((mine, local, rows, LANES), BF16),
            shape((mine, local, LANES, lanes), F32),
            shape((mine, hd + 16, lanes), BF16),
        ],
        compiler_params=params(48),
        name="query_side",
    )(query, grad, vk, kdot, states, wa, wb, ba, bb)
    dq, qdot, dn, cots, window = query_out
    dq = exchange(dq.reshape(heads, half, LANES))

    if groups > 1:
        scale = np.where(np.arange(lanes) >= 0, 1.0, 0.0).astype(np.float32)
        later = of_groups(cots.sum(1), lambda at: at > group)
        base_after = base_after + later * lane_weights(sk, lanes)

    dvk, _ = pl.pallas_call(
        partial(reverse_kernel, sk, hd),
        grid=(mine,),
        in_specs=[
            across(rows), own(local, rows, lanes), own(local, rows, LANES), own(local, rows, LANES),
            own(local, rows, LANES), own(local, LANES, lanes), state_spec, fixed(wb), fixed(bb),
        ],
        out_specs=[across(rows), state_spec],
        out_shape=[shape((local, mine, rows, LANES), BF16), shape((mine, LANES, lanes), F32)],
        compiler_params=params(48),
        name="key_gradients",
    )(vk, key_feats, kdot, qdot, dn, cots, base_after, wb, bb)
    dvk = exchange(dvk.reshape(heads, rows, LANES))

    if groups > 1:
        window = lax.psum(window, "group")
    window = lax.all_gather(window, "local", axis=0, tiled=True)
    state_out, d_prefix_norm = pl.pallas_call(
        partial(expand_kernel, hd),
        in_specs=[vmem] * 4,
        out_specs=[vmem] * 2,
        out_shape=[shape((heads, hd, feat), F32), shape((heads, feat), F32)],
        compiler_params=params(32),
        name="prefix_gradients",
    )(window, dstate_t, d_norm_end, table)
    d_prefix_state = state_out.transpose(0, 2, 1)

    d_query, part = pl.pallas_call(
        partial(unpack_query_kernel, hd),
        in_specs=[vmem] * 2,
        out_specs=[vmem] * 2,
        out_shape=[shape((rows, width), BF16), shape((ranks, rows, depth), F32)],
        compiler_params=params(24),
        name="input_from_query",
    )(dq, w_query)

    order, distance = [0], 1
    while distance < ranks:
        order = [at for at in range(ranks)]
        distance *= 2
    order = sorted(range(ranks), key=lambda at: [-(at >> bit & 1) for bit in range(ranks.bit_length() - 1)])
    order_of = jnp.stack([rank ^ at for at in order]).astype(jnp.int32)
    d_key, d_value, sums = pl.pallas_call(
        partial(unpack_key_kernel, hd),
        in_specs=[smem] + [vmem] * 4,
        out_specs=[vmem] * 3,
        out_shape=[shape((rows, width), BF16), shape((rows, width), BF16), shape((ranks, rows, depth), BF16)],
        compiler_params=params(32),
        name="input_from_key_value",
    )(order_of, dvk, w_key, w_value, part)
    distance = 1
    while distance < ranks:
        count = sums.shape[0] // 2
        came = hop(sums[:count], "head", distance)
        sums = (sums[count:].astype(F32) + came.astype(F32)).astype(BF16)
        distance *= 2
    return sums[0], d_query, d_key, d_value, d_prefix_state, d_prefix_norm


def solution(mesh):
    seq, head = mesh.shape["seq"], mesh.shape["head"]

    def run(*args):
        heads = args[5].shape[0] // head
        local = math.gcd(heads, seq)
        groups = seq // local
        inner = Mesh(mesh.devices.reshape(groups, local, head), ("group", "local", "head"))
        tokens = ("group", "local")
        return jax.shard_map(
            partial(body, groups, local),
            mesh=inner,
            in_specs=(
                P(tokens, "head"),
                P(None, "head"),
                P(None, "head"),
                P(None, "head"),
                P(),
                P("head", None, None),
                P("head", None),
                P(tokens, "head"),
                P("head", None, None),
                P("head", None),
            ),
            out_specs=(
                P(tokens, "head"),
                P(tokens, "head"),
                P(tokens, "head"),
                P(tokens, "head"),
                P("head", None, None),
                P("head", None),
            ),
            check_vma=False,
        )(*args)

    return run
```

time: 572 us -> 161 us (0.28)
  matrix products: 129 us -> 0 us
  other arithmetic: 116 us -> 1.48 us
  waiting for transfers between devices: 119 us -> 24.1 us
  blocking collectives: 102 us -> 32.2 us
  local copies, waits for them, and re-layouts: 85.2 us -> 34.8 us
  Pallas kernels: 0 us -> 36.1 us
  starting transfers between devices: 0.16 us -> 29.7 us
  between operations: 14.6 us -> 0.91 us
    dot_general x32 -> x0, matrix products: 129 us -> none  [the longest x3 33.1 us: attend_block(): jnp.einsum('hif,hfd->hid', feat_query, value_state, precision=HIGHEST_PRE...]
    all_gather x3 -> x0, waiting for transfers between devices: 101 us -> none  [the longest x1 80.2 us: prefix(): lax.all_gather(part.astype(kind), axis)]
    select_n x16 -> x0, other arithmetic: 47.8 us -> none  [lap(): return jax.tree.map(lambda a, b: jnp.where(reached, a, b), new, before)]
    add x17 -> x0, other arithmetic: 46.9 us -> none  [the longest x14 41.9 us: add_pair(): return (earlier[0] + later[0], earlier[1] + later[1])]
    dynamic_slice x30 -> x0, local copies, waits for them, and re-layouts: 46.5 us -> none  [the longest x16 24.8 us: lap(): part[k].astype(own.dtype)]
    pallas_call x0 -> x9, Pallas kernels: none -> 36.1 us  [the longest x1 11.2 us: body(): pl.pallas_call(partial(query_kernel, sk, hd), grid=(mine,), in_specs=[acr...]
    psum x1 -> x0, blocking collectives: 35.8 us -> none  [body(): lax.psum(cot_norm.astype(jnp.bfloat16), 'seq').astype(jnp.float32)]
    all_gather x2 -> x1, blocking collectives: 66.6 us -> 32.2 us  [body(): window = lax.all_gather(window, 'local', axis=0, tiled=True)]
  transfers between devices with their start and end apart: 5 -> 10, of which waited for: 3 -> 6; matrix products, arithmetic and copies ran while one was open for 38% -> 4% of each run, Pallas kernels for 0% -> 14%
where the time goes in v1:
time: 161 us; the launch traced here: 159 us
  Pallas kernels  36.1 us (22%)
  local copies, waits for them, and re-layouts  34.8 us (22%)
  blocking collectives  32.2 us (20%)
  starting transfers between devices  29.7 us (18%)
  waiting for transfers between devices  24.1 us (15%)
    all_gather x1, blocking collectives, body(): window = lax.all_gather(window, 'local', axis=0, tiled=True)  32.2 us
    unnamed x77, local copies, waits for them, and re-layouts  30.7 us
    all_to_all x5, starting transfers between devices, exchange(): return lax.all_to_all(x, 'local', 0, 0, tiled=True) if local > 1 else x  25.4 us
    all_to_all x5, waiting for transfers between devices, exchange(): return lax.all_to_all(x, 'local', 0, 0, tiled=True) if local > 1 else x  20.9 us
    pallas_call x1, Pallas kernels, body(): pl.pallas_call(partial(query_kernel, sk, hd), grid=(mine,), in_specs=[acr...  11.2 us
    pallas_call x1, Pallas kernels, body(): pl.pallas_call(partial(reverse_kernel, sk, hd), grid=(mine,), in_specs=[a...  8.8 us
    ppermute x5, starting transfers between devices, hop(): return lax.ppermute(x, axis, [(i, i ^ distance) for i in range(count)])  4.32 us
    pallas_call x2, Pallas kernels, project(): pl.pallas_call(partial(project_kernel, hd, len(keys)), in_specs=[smem] +...  3.99 us
  transfers between devices with their start and end apart: 10, of which 6 were waited for; matrix products, arithmetic and copies ran while one was open for 4% of the time, Pallas kernels for 14%

profile of v1, /device:TPU:0, one launch (start us, length us, event | category | flops | bytes accessed | tf_op | source)
XLA Modules:
  0.0 159.3 jit_solution(7546950761880451561)
XLA Ops:
  0.7 3.0 %collective-permute-start.1 = (bf16[256,512]{1,0:T(8,128)(2,1)}, bf16[256,512]{1,0:T(8,128)(2,1)S(1)}, u32[]{:S(2)}, u32[]{:S(2)}) collective-permute-start(bf16[256,512]{1,0:T(8,128)(2,1)} %refs_0_.3), channel_id=1, source_target_pairs={{0,2},{1,3},{2,0},{3,1},{4,6},{5,7},{6,4},{7,5},{8,10},{9,11},{10,... | collective-permute-start | bytes 786440 | tf_op jit(solution)/shard_map/ppermute | solution.py:325
  3.7 1.1 copy.33
  5.7 5.8 %all-to-all-start.2 = ((bf16[8,128,128]{2,1,0:T(8,128)(2,1)}), bf16[8,128,128]{2,1,0:T(8,128)(2,1)S(1)}, u32[]{:S(2)}, u32[]{:S(2)}) async-start(bf16[8,128,128]{2,1,0:T(8,128)(2,1)} %copy.35), calls=%async_computation.2 | async-start | bytes 524288 | tf_op jit(solution)/shard_map/all_to_all | solution.py:343
  13.5 1.6 copy-done.1
  15.1 2.7 %project_key_value.1 = bf16[8,256,128]{2,1,0:T(8,128)(2,1)} custom-call(s32[4]{0:T(128)S(1)} %pad_add_fusion.1.where_ref, bf16[256,512]{1,0:T(8,128)(2,1)S(1)} %copy-done.18, bf16[256,512]{1,0:T(8,128)(2,1)S(1)} %collective-permute-done.refs_1_, bf16[256,512]{1,0:T(8,128)(2,1)S(1)} %collective-permute-done.1.refs_2_, ...), custom_call_target="tpu_custom_call" | custom-call | tf_op jit(solution)/shard_map/project_key_value/pallas_call | solution.py:395
  17.8 2.4 %all-to-all-done.2 = bf16[8,128,128]{2,1,0:T(8,128)(2,1)S(1)} async-done(((bf16[8,128,128]{2,1,0:T(8,128)(2,1)}), bf16[8,128,128]{2,1,0:T(8,128)(2,1)S(1)}, u32[]{:S(2)}, u32[]{:S(2)}) %all-to-all-start.2) | async-done | bytes 262176 | tf_op jit(solution)/shard_map/all_to_all | solution.py:343
  20.9 3.6 %all-to-all-start = ((bf16[8,256,128]{2,1,0:T(8,128)(2,1)}), bf16[8,256,128]{2,1,0:T(8,128)(2,1)S(1)}, u32[]{:S(2)}, u32[]{:S(2)}) async-start(bf16[8,256,128]{2,1,0:T(8,128)(2,1)} %project_key_value.1), calls=%async_computation | async-start | bytes 1048576 | tf_op jit(solution)/shard_map/all_to_all | solution.py:343
  24.5 1.6 copy-done.3
  27.1 1.3 project_query.1
  29.1 10.1 %all-to-all-done = bf16[8,256,128]{2,1,0:T(8,128)(2,1)S(1)} async-done(((bf16[8,256,128]{2,1,0:T(8,128)(2,1)}), bf16[8,256,128]{2,1,0:T(8,128)(2,1)S(1)}, u32[]{:S(2)}, u32[]{:S(2)}) %all-to-all-start) | async-done | bytes 524320 | tf_op jit(solution)/shard_map/all_to_all | solution.py:343
  39.2 4.2 %all-to-all-start.1 = ((bf16[8,128,128]{2,1,0:T(8,128)(2,1)}), bf16[8,128,128]{2,1,0:T(8,128)(2,1)}, u32[]{:S(2)}, u32[]{:S(2)}) async-start(bf16[8,128,128]{2,1,0:T(8,128)(2,1)} %copy-done.21), calls=%async_computation.1 | async-start | bytes 524288 | tf_op jit(solution)/shard_map/all_to_all | solution.py:343
  46.3 1.6 copy-done.5
  47.9 1.3 copy-done.7
  49.2 1.6 copy-done.10
  50.8 1.7 %base_states.1 = (f32[1,128,640]{2,1,0:T(8,128)S(1)}, f32[1,128,640]{2,1,0:T(8,128)S(1)}) custom-call(s32[1]{0:T(128)} %bitcast.5.start_ref, f32[8,64,1024]{2,1,0:T(8,128)S(1)} %bitcast.36, f32[8,1024]{1,0:T(8,128)S(1)} %copy-done.35, f32[8,64,1024]{2,1,0:T(8,128)S(1)} %bitcast.31, f32[8,1024]{1,0:T(8,128)S(1)} %copy-done.31, bf16[1024,640]{1,0:T(8,128)(2,1)S(1)} %copy-done.7), custom_call_target="tpu_custom_call" | custom-call | tf_op jit(solution)/shard_map/base_states/pallas_call | solution.py:377
  53.2 3.7 %key_side.1 = (bf16[1,8,128,640]{3,2,1,0:T(8,128)(2,1)S(1)}, bf16[1,8,256,640]{3,2,1,0:T(8,128)(2,1)S(1)}, bf16[1,8,256,128]{3,2,1,0:T(8,128)(2,1)S(1)}, f32[1,128,640]{2,1,0:T(8,128)}) custom-call(bf16[8,1,256,128]{3,2,1,0:T(8,128)(2,1)S(1)} %bitcast.33, f32[1,128,640]{2,1,0:T(8,128)S(1)} %get-tuple-element.24.base_ref, bf16[256,512]{1,0:T(8,128)(2,1)S(1)} %copy.32.wb_ref), custom_call_target="tpu_custom_call" | custom-call | tf_op jit(solution)/shard_map/key_side/pallas_call | solution.py:413
  56.9 1.5 copy-done.9
  59.4 1.3 copy-done.14
  63.6 11.2 %query_side.1 = (bf16[8,1,128,128]{3,2,1,0:T(8,128)(2,1)S(1)}, bf16[1,8,256,128]{3,2,1,0:T(8,128)(2,1)S(1)}, bf16[1,8,256,128]{3,2,1,0:T(8,128)(2,1)S(1)}, f32[1...) custom-call(bf16[8,1,128,128]{3,2,1,0:T(8,128)(2,1)} %bitcast.14.q_ref, bf16[8,1,128,128]{3,2,1,0:T(8,128)(2,1)S(1)} %bitcast.37, ...), custom_call_target="tpu_custom_call" | custom-call | tf_op jit(solution)/shard_map/query_side/pallas_call | solution.py:438
  77.7 5.7 %all-to-all-start.4 = ((bf16[8,128,128]{2,1,0:T(8,128)(2,1)}), bf16[8,128,128]{2,1,0:T(8,128)(2,1)}, u32[]{:S(2)}, u32[]{:S(2)}) async-start(bf16[8,128,128]{2,1,0:T(8,128)(2,1)} %bitcast.39), calls=%async_computation.4 | async-start | bytes 524288 | tf_op jit(solution)/shard_map/all_to_all | solution.py:343
  86.4 8.8 %key_gradients.1 = (bf16[8,1,256,128]{3,2,1,0:T(8,128)(2,1)S(1)}, f32[1,128,640]{2,1,0:T(8,128)}) custom-call(bf16[8,1,256,128]{3,2,1,0:T(8,128)(2,1)S(1)} %bitcast.35, bf16[1,8,256,640]{3,2,1,0:T(8,128)(2,1)} %copy-done.9, bf16[1,8,256,128]{3,2,1,0:T(8,128)(2,1)S(1)} %get-tuple-element.26.kdot_ref, bf16[1,8,256,128]{3,2,1,0:T(8,128)(2,1)S(1)} %copy-done.25, ...), custom_call_target="tpu_custom_call" | custom-call | tf_op jit(solution)/shard_map/key_gradients/pallas_call | solution.py:467
  96.0 6.0 %all-to-all-start.3 = ((bf16[8,256,128]{2,1,0:T(8,128)(2,1)}), bf16[8,256,128]{2,1,0:T(8,128)(2,1)S(1)}, u32[]{:S(2)}, u32[]{:S(2)}) async-start(bf16[8,256,128]{2,1,0:T(8,128)(2,1)} %bitcast.38), calls=%async_computation.3 | async-start | bytes 1048576 | tf_op jit(solution)/shard_map/all_to_all | solution.py:343
  102.1 1.6 copy-done.4
  103.7 1.8 %input_from_query.1 = (bf16[256,512]{1,0:T(8,128)(2,1)}, f32[4,256,512]{2,1,0:T(8,128)S(1)}) custom-call(bf16[8,128,128]{2,1,0:T(8,128)(2,1)} %all-to-all-done.4.dq_ref, bf16[2048,512]{1,0:T(8,128)(2,1)S(1)} %copy-done.4), custom_call_target="tpu_custom_call" | custom-call | tf_op jit(solution)/shard_map/input_from_query/pallas_call | solution.py:494
  105.6 1.3 copy-done.11
  106.9 8.4 %all-to-all-done.3.dvk_ref = bf16[8,256,128]{2,1,0:T(8,128)(2,1)S(1)} async-done(((bf16[8,256,128]{2,1,0:T(8,128)(2,1)}), bf16[8,256,128]{2,1,0:T(8,128)(2,1)S(1)}, u32[]{:S(2)}, u32[]{:S(2)}) %all-to-all-start.3) | async-done | bytes 524320 | tf_op jit(solution)/shard_map/all_to_all | solution.py:343
  115.3 1.6 copy-done.2
  116.9 1.6 copy-done.12
  118.4 2.4 %input_from_key_value.1 = (bf16[256,512]{1,0:T(8,128)(2,1)}, bf16[256,512]{1,0:T(8,128)(2,1)}, bf16[4,256,512]{2,1,0:T(8,128)(2,1)S(1)}) custom-call(s32[4]{0:T(128)S(1)} %pad_add_fusion.order_ref, bf16[8,256,128]{2,1,0:T(8,128)(2,1)S(1)} %all-to-all-done.3.dvk_ref, bf16[2048,512]{1,0:T(8,128)(2,1)S(1)} %copy-done.2, bf16[2048,512]{1,0:T(8,128)(2,1)S(1)} %copy-done, ...), custom_call_target="tpu_custom_call" | custom-call | tf_op jit(solution)/shard_map/input_from_key_value/pallas_call | solution.py:509
  121.0 1.9 %collective-permute-done.3 = bf16[2,256,512]{2,1,0:T(8,128)(2,1)S(1)} collective-permute-done((bf16[2,256,512]{2,1,0:T(8,128)(2,1)S(1)}, bf16[2,256,512]{2,1,0:T(8,128)(2,1)S(1)}, u32[]{:S(2)}, u32[]{:S(2)}) %collective-permute-start.3) | collective-permute-done | bytes 524320 | tf_op jit(solution)/shard_map/ppermute | solution.py:325
  123.8 32.2 %all_gather.3.all_ref = bf16[8,80,640]{2,1,0:T(8,128)(2,1)S(1)} all-gather(bf16[1,80,640]{2,1,0:T(8,128)(2,1)S(1)} %copy-done.34), channel_id=1, replica_groups=mesh['seq'=8,'head'=4] {'seq'}, dimensions={0}, use_global_device_ids=true | all-gather | bytes 921600 | tf_op jit(solution)/shard_map/all_gather | solution.py:483
  156.0 2.5 %prefix_gradients.1 = (f32[8,64,1024]{2,1,0:T(8,128)}, f32[8,1024]{1,0:T(8,128)}) custom-call(bf16[8,80,640]{2,1,0:T(8,128)(2,1)S(1)} %all_gather.3.all_ref, f32[8,64,1024]{2,1,0:T(8,128)S(1)} %bitcast.32, f32[8,1024]{1,0:T(8,128)S(1)} %copy-done.32, bf16[1024,640]{1,0:T(8,128)(2,1)S(1)} %copy-done.8), custom_call_target="tpu_custom_call" | custom-call | tf_op jit(solution)/shard_map/prefix_gradients/pallas_call | solution.py:484
  (96 shorter events, 21.3 us)
Async XLA Ops:
  0.6 10.9 %copy-start.18 = (bf16[256,512]{1,0:T(8,128)(2,1)S(1)}, bf16[256,512]{1,0:T(8,128)(2,1)}, u32[]{:S(2)}) copy-start(bf16[256,512]{1,0:T(8,128)(2,1)} %refs_0_.3) | copy-start | bytes 786436
  0.6 12.9 %copy-start = (bf16[2048,512]{1,0:T(8,128)(2,1)S(1)}, bf16[2048,512]{1,0:T(8,128)(2,1)}, u32[]{:S(2)}) copy-start(bf16[2048,512]{1,0:T(8,128)(2,1)} %wv_ref.1) | copy-start | bytes 6291460
  0.7 11.0 %collective-permute-start.1 = (bf16[256,512]{1,0:T(8,128)(2,1)}, bf16[256,512]{1,0:T(8,128)(2,1)S(1)}, u32[]{:S(2)}, u32[]{:S(2)}) collective-permute-start(bf16[256,512]{1,0:T(8,128)(2,1)} %refs_0_.3), channel_id=1, source_target_pairs={{0,2},{1,3},{2,0},{3,1},{4,6},{5,7},{6,4},{7,5},{8,10},{9,11},{10,... | collective-permute-start | bytes 786440 | tf_op jit(solution)/shard_map/ppermute | solution.py:325
  5.7 14.5 %all-to-all-start.2 = ((bf16[8,128,128]{2,1,0:T(8,128)(2,1)}), bf16[8,128,128]{2,1,0:T(8,128)(2,1)S(1)}, u32[]{:S(2)}, u32[]{:S(2)}) async-start(bf16[8,128,128]{2,1,0:T(8,128)(2,1)} %copy.35), calls=%async_computation.2 | async-start | bytes 524288 | tf_op jit(solution)/shard_map/all_to_all | solution.py:343
  11.6 1.6 %collective-permute-start = (bf16[256,512]{1,0:T(8,128)(2,1)S(1)}, bf16[256,512]{1,0:T(8,128)(2,1)S(1)}, u32[]{:S(2)}, u32[]{:S(2)}) collective-permute-start(bf16[256,512]{1,0:T(8,128)(2,1)S(1)} %copy-done.18), channel_id=1, source_target_pairs={{0,1},{1,0},{2,3},{3,2},{4,5},{5,4},{6,7},{7,6},{8,9},{9,8},{10,11... | collective-permute-start | bytes 786440 | tf_op jit(solution)/shard_map/ppermute | solution.py:325
  11.6 1.9 %collective-permute-start.2 = (bf16[256,512]{1,0:T(8,128)(2,1)S(1)}, bf16[256,512]{1,0:T(8,128)(2,1)S(1)}, u32[]{:S(2)}, u32[]{:S(2)}) collective-permute-start(bf16[256,512]{1,0:T(8,128)(2,1)S(1)} %collective-permute-done.1.refs_2_), channel_id=1, source_target_pairs={{0,1},{1,0},{2,3},{3,2},{4,5},{5,4},{6,7},{7,6},{8,9},{9,8},{10,11... | collective-permute-start | bytes 786440 | tf_op jit(solution)/shard_map/ppermute | solution.py:325
  13.5 1.6 copy-start.1
  15.1 2.7 %copy-start.19 = (bf16[256,512]{1,0:T(8,128)(2,1)}, bf16[256,512]{1,0:T(8,128)(2,1)S(1)}, u32[]{:S(2)}) copy-start(bf16[256,512]{1,0:T(8,128)(2,1)S(1)} %collective-permute-done.2.refs_3_) | copy-start | bytes 786436
  15.1 9.4 %copy-start.36 = (f32[2,64,32]{1,2,0:T(8,128)S(1)}, f32[2,64,32]{1,2,0:T(8,128)}, u32[]{:S(2)}) copy-start(f32[2,64,32]{1,2,0:T(8,128)} %param.18) | copy-start | bytes 49156
  20.9 18.3 %all-to-all-start = ((bf16[8,256,128]{2,1,0:T(8,128)(2,1)}), bf16[8,256,128]{2,1,0:T(8,128)(2,1)S(1)}, u32[]{:S(2)}, u32[]{:S(2)}) async-start(bf16[8,256,128]{2,1,0:T(8,128)(2,1)} %project_key_value.1), calls=%async_computation | async-start | bytes 1048576 | tf_op jit(solution)/shard_map/all_to_all | solution.py:343
  24.5 19.0 %copy-start.37 = (s32[128]{0:T(128)S(1)}, s32[128]{0:T(128)}, u32[]{:S(2)}) copy-start(s32[128]{0:T(128)} %constant.35) | copy-start | bytes 1540
  24.5 1.6 %copy-start.3 = (bf16[2048,512]{1,0:T(8,128)(2,1)S(1)}, bf16[2048,512]{1,0:T(8,128)(2,1)}, u32[]{:S(2)}) copy-start(bf16[2048,512]{1,0:T(8,128)(2,1)} %w_ref.1) | copy-start | bytes 6291460
  29.1 17.1 %copy-start.31 = (f32[8,1024]{1,0:T(8,128)S(1)}, f32[8,1024]{1,0:T(8,128)}, u32[]{:S(2)}) copy-start(f32[8,1024]{1,0:T(8,128)} %dnorm_ref.3) | copy-start | bytes 98308
  29.1 17.1 %copy-start.35 = (f32[8,1024]{1,0:T(8,128)S(1)}, f32[8,1024]{1,0:T(8,128)}, u32[]{:S(2)}) copy-start(f32[8,1024]{1,0:T(8,128)} %norm_ref.1) | copy-start | bytes 98308
  39.2 20.2 %all-to-all-start.1 = ((bf16[8,128,128]{2,1,0:T(8,128)(2,1)}), bf16[8,128,128]{2,1,0:T(8,128)(2,1)}, u32[]{:S(2)}, u32[]{:S(2)}) async-start(bf16[8,128,128]{2,1,0:T(8,128)(2,1)} %copy-done.21), calls=%async_computation.1 | async-start | bytes 524288 | tf_op jit(solution)/shard_map/all_to_all | solution.py:343
  46.3 1.6 %copy-start.5 = (f32[8,1024,64]{1,2,0:T(8,128)S(1)}, f32[8,1024,64]{1,2,0:T(8,128)}, u32[]{:S(2)}) copy-start(f32[8,1024,64]{1,2,0:T(8,128)} %param.22) | copy-start | bytes 6291460
  47.9 1.3 copy-start.7
  49.2 1.6 copy-start.10
  56.9 1.5 copy-start.9
  59.4 1.3 copy-start.14
  77.7 18.4 %all-to-all-start.4 = ((bf16[8,128,128]{2,1,0:T(8,128)(2,1)}), bf16[8,128,128]{2,1,0:T(8,128)(2,1)}, u32[]{:S(2)}, u32[]{:S(2)}) async-start(bf16[8,128,128]{2,1,0:T(8,128)(2,1)} %bitcast.39), calls=%async_computation.4 | async-start | bytes 524288 | tf_op jit(solution)/shard_map/all_to_all | solution.py:343
  96.0 19.2 %all-to-all-start.3 = ((bf16[8,256,128]{2,1,0:T(8,128)(2,1)}), bf16[8,256,128]{2,1,0:T(8,128)(2,1)S(1)}, u32[]{:S(2)}, u32[]{:S(2)}) async-start(bf16[8,256,128]{2,1,0:T(8,128)(2,1)} %bitcast.38), calls=%async_computation.3 | async-start | bytes 1048576 | tf_op jit(solution)/shard_map/all_to_all | solution.py:343
  102.1 1.6 copy-start.4
  105.6 1.3 copy-start.11
  115.3 1.6 copy-start.2
  116.9 1.6 copy-start.12
  118.4 5.3 %copy-start.34 = (bf16[1,80,640]{2,1,0:T(8,128)(2,1)S(1)}, bf16[1,80,640]{2,1,0:T(8,128)(2,1)}, u32[]{:S(2)}) copy-start(bf16[1,80,640]{2,1,0:T(8,128)(2,1)} %copy-done.33) | copy-start | bytes 307204
  120.9 35.1 %copy-start.6 = (f32[8,1024,64]{1,2,0:T(8,128)S(1)}, f32[8,1024,64]{1,2,0:T(8,128)}, u32[]{:S(2)}) copy-start(f32[8,1024,64]{1,2,0:T(8,128)} %param.22) | copy-start | bytes 6291460
  120.9 35.1 %copy-start.8 = (bf16[1024,640]{1,0:T(8,128)(2,1)S(1)}, bf16[1024,640]{1,0:T(8,128)(2,1)}, u32[]{:S(2)}) copy-start(bf16[1024,640]{1,0:T(8,128)(2,1)} %constant.29.clone.map_ref) | copy-start | bytes 3932164
  120.9 35.1 %copy-start.32 = (f32[8,1024]{1,0:T(8,128)S(1)}, f32[8,1024]{1,0:T(8,128)}, u32[]{:S(2)}) copy-start(f32[8,1024]{1,0:T(8,128)} %dnorm_ref.3) | copy-start | bytes 98308
  120.9 2.0 %collective-permute-start.3 = (bf16[2,256,512]{2,1,0:T(8,128)(2,1)S(1)}, bf16[2,256,512]{2,1,0:T(8,128)(2,1)S(1)}, u32[]{:S(2)}, u32[]{:S(2)}) collective-permute-start(bf16[2,256,512]{2,1,0:T(8,128)(2,1)S(1)} %slice.21), channel_id=1, source_target_pairs={{0,1},{1,0},{2,3},{3,2},{4,5},{5,4},{6,7},{7,6},{8,9},{9,8},{10,11... | collective-permute-start | bytes 1572872 | tf_op jit(solution)/shard_map/ppermute | solution.py:325
  123.1 35.5 %collective-permute-start.4 = (bf16[1,256,512]{2,1,0:T(8,128)(2,1)S(1)}, bf16[1,256,512]{2,1,0:T(8,128)(2,1)S(1)}, u32[]{:S(2)}, u32[]{:S(2)}) collective-permute-start(bf16[1,256,512]{2,1,0:T(8,128)(2,1)S(1)} %slice.29), channel_id=1, source_target_pairs={{0,2},{1,3},{2,0},{3,1},{4,6},{5,7},{6,4},{7,5},{8,10},{9,11},{10,... | collective-permute-start | bytes 786440 | tf_op jit(solution)/shard_map/ppermute | solution.py:325
  (16 other events, 13.8 us)

commit v2 on v1

v2 whole, which is shorter than its diff:
```python
import math
from functools import partial

import jax
import jax.numpy as jnp
import numpy as np
from jax import lax
from jax.experimental import pallas as pl
from jax.experimental.pallas import tpu as pltpu
from jax.sharding import Mesh, PartitionSpec as P

F32 = jnp.float32
BF16 = jnp.bfloat16
LANES = 128
VMEM = pltpu.VMEM
MIB = 1024 * 1024

NN = (((1,), (0,)), ((), ()))
NT = (((1,), (1,)), ((), ()))
TN = (((0,), (0,)), ((), ()))


def mm(a, b, dims=NN):
    return lax.dot_general(a, b, dims, preferred_element_type=F32)


def split(x):
    hi = x.astype(BF16)
    return hi, (x - hi.astype(F32)).astype(BF16)


def tile_count(sk):
    return -(-(sk // 2 + 1) // (LANES // sk))


def pair_map(sk):
    step = LANES // sk
    width = tile_count(sk) * LANES
    lane = np.arange(width)
    tile, within = lane // LANES, lane % LANES
    j, a = within // sk, within % sk
    first, second = (a + j) % sk, (a - step * tile) % sk
    keep = step * tile + j <= sk // 2
    table = np.zeros((sk * sk, width), np.float32)
    for one in lane[keep]:
        x, y = first[one], second[one]
        r = step * tile[one] + j[one]
        if r == 0:
            table[x * sk + y, one] = 1.0
        else:
            value = 0.5 if 2 * r == sk else 1.0
            table[x * sk + y, one] = value
            table[y * sk + x, one] = value
    return table


def lane_weights(sk, width):
    lane = lax.broadcasted_iota(jnp.int32, (1, width), 1)
    r = (LANES // sk) * (lane // LANES) + (lane % LANES) // sk
    return jnp.where(
        r <= sk // 2, jnp.where((r == 0) | (2 * r == sk), 1.0, 2.0), 0.0
    ).astype(F32)


def sketched(x, weights):
    both = mm(jnp.concatenate([x, x], axis=1), weights)
    return tuple(both[:, LANES * i : LANES * (i + 1)] for i in range(4))


def turned(e, sk, tiles):
    step = LANES // sk
    return [e] + [pltpu.roll(e, step * t, 1) for t in range(1, tiles)]


def features(e, d, sk, tiles):
    return jnp.concatenate([(d * x).astype(BF16) for x in turned(e, sk, tiles)], axis=1)


def feature_pull(cot, e, d, sk, tiles):
    step = LANES // sk
    cot_e = cot_d = None
    for t, x in enumerate(turned(e, sk, tiles)):
        part = cot[:, LANES * t : LANES * (t + 1)]
        to_d = part * x
        to_e = part * d
        if t:
            to_e = pltpu.roll(to_e, LANES - step * t, 1)
        cot_d = to_d if cot_d is None else cot_d + to_d
        cot_e = to_e if cot_e is None else cot_e + to_e
    return cot_e, cot_d


def lane_of(rows):
    return lax.broadcasted_iota(jnp.int32, (rows, LANES), 1)


def slot_of(place, other, local):
    return lax.rem(other - place + local, local)


def came_in(place, other, local):
    return lax.rem(place - other + local, local)


def prepare_kernel(
    sk, place_ref, sketch_ref, state_ref, norm_ref, dstate_ref, dnorm_ref, map_ref,
    fwd_ref, bwd_ref, wa_ref, wb_ref, ba_ref, bb_ref, rows_ref,
):
    table = map_ref[...]
    mine, half, _ = state_ref.shape
    step = LANES // sk
    left, right = sketch_ref[0], sketch_ref[1] * sk ** (-0.5)

    def turns(x):
        return [x] + [jnp.concatenate([x[j:], x[:j]], axis=0) for j in range(1, step)]

    full = jnp.concatenate([left] * step + [right] * step + turns(left) + turns(right), axis=0)
    hi, lo = split(full)
    none = jnp.zeros_like(full)
    ba_ref[...] = jnp.concatenate([hi.astype(F32), none], axis=1).astype(BF16)
    bb_ref[...] = jnp.concatenate([none, hi.astype(F32)], axis=1).astype(BF16)
    hi, lo = hi.astype(F32).T, lo.astype(F32).T
    none = jnp.zeros_like(hi)
    wa_ref[...] = jnp.concatenate([hi, none, lo, none], axis=0).astype(BF16)
    wb_ref[...] = jnp.concatenate([none, hi, none, lo], axis=0).astype(BF16)

    def mapped(x):
        hi, lo = split(x)
        return mm(hi, table) + mm(lo, table)

    for which, (s_ref, n_ref, o_ref, scale) in enumerate(
        ((state_ref, norm_ref, fwd_ref, 1.0), (dstate_ref, dnorm_ref, bwd_ref, 1.0 / half))
    ):
        rows_ref[which] = mapped(n_ref[...]) * scale
        for m in range(mine):
            o_ref[m, :half] = mapped(s_ref[m])
            o_ref[m, half:] = jnp.broadcast_to(
                rows_ref[which, pl.ds(place_ref[0] * mine + m, 1), :], (LANES - half, o_ref.shape[2])
            )


def gradient_kernel(hd, local, grad_ref, out_ref):
    rows = grad_ref.shape[0]
    half = rows // 2
    low = lane_of(half) < hd
    mine = out_ref.shape[1]
    for pair in range(local * mine // 2):
        both = grad_ref[:, pair * LANES : (pair + 1) * LANES].astype(F32)
        top, bottom = both[:half], both[half:]
        for at, block in (
            (2 * pair, jnp.where(low, top, pltpu.roll(bottom, hd, 1))),
            (2 * pair + 1, jnp.where(low, pltpu.roll(top, hd, 1), bottom)),
        ):
            out_ref[at // mine, at % mine] = block.astype(BF16)


def bring(weights, where_ref, depth, held_ref, done_ref):
    copies = [
        [
            pltpu.make_async_copy(
                w.at[pl.ds(pl.multiple_of(where_ref[i] * depth, depth), depth)], held_ref.at[k, i], done_ref.at[k, i]
            )
            for i in range(held_ref.shape[1])
        ]
        for k, w in enumerate(weights)
    ]
    for i in range(held_ref.shape[1]):
        for k in range(len(weights)):
            copies[k][i].start()
    return copies


def project_kernel(hd, local, count, place_ref, where_ref, *refs):
    pieces = refs[:count]
    weights = refs[count : count + 3]
    out_refs = refs[count + 3 : -3]
    blocks_ref, held_ref, done_ref = refs[-3:]
    depth = pieces[0].shape[1]
    rows = pieces[0].shape[0]
    half = rows // 2
    mine = blocks_ref.shape[1]
    copies = bring(weights, where_ref, depth, held_ref, done_ref)
    sums = []
    for k in range(len(weights)):
        total = None
        for i, x in enumerate(pieces):
            copies[k][i].wait()
            part = mm(x[...], held_ref[k, i])
            total = part if total is None else total + part
        sums.append(total)
    value, key, query = sums
    for h in range(local * mine):
        cols = slice(h * hd, (h + 1) * hd)
        slot = slot_of(place_ref[0], h // mine, local)
        blocks_ref[slot, h % mine, :rows] = jnp.concatenate([value[:, cols], key[:, cols]], axis=1).astype(BF16)
        blocks_ref[slot, h % mine, rows:] = jnp.concatenate(
            [query[:half, cols], query[half:, cols]], axis=1
        ).astype(BF16)
    for s, out_ref in enumerate(out_refs):
        out_ref[...] = blocks_ref[s]


def key_kernel(sk, hd, local, place_ref, *refs):
    slots = refs[:local]
    base_ref, wb_ref, qkv_ref, state_ref, feat_ref, kdot_ref, total_ref = refs[local:]
    blocks, mine, packed, _ = qkv_ref.shape
    for s, slot in enumerate(slots):
        qkv_ref[came_in(place_ref[0], s, blocks)] = slot[...]
    rows = packed * 2 // 3
    width = base_ref.shape[2]
    tiles = width // LANES
    weights = lane_weights(sk, width)
    lane = lane_of(rows)
    for m in range(mine):
        state = base_ref[m]
        for c in range(blocks):
            state_ref[m, c] = state.astype(BF16)
            vk = qkv_ref[c, m, :rows]
            e0, e1, d0, d1 = sketched(vk, wb_ref[...])
            e, d = e0 * e1, d0 * d1
            feat = features(e, d, sk, tiles)
            feat_ref[m, c] = feat
            hi, lo = split(e)
            kdot_ref[m, c] = jnp.where(
                lane < 2 * sk, hi.astype(F32), jnp.where(lane < 3 * sk, lo.astype(F32), 0.0)
            ).astype(BF16)
            ones = jnp.where(lane < hd, vk.astype(F32), 1.0).astype(BF16)
            state = state + mm(ones, feat, TN) * weights
        total_ref[m] = state


def query_kernel(
    sk, hd, qkv_ref, g_ref, kdot_ref, state_ref, wa_ref, wb_ref, ba_ref, bb_ref,
    dq_ref, qdot_ref, dn_ref, cot_ref, total_ref,
):
    blocks, mine, packed, _ = qkv_ref.shape
    rows = packed * 2 // 3
    half = rows // 2
    width = state_ref.shape[3]
    tiles = width // LANES
    lane = lane_of(rows)
    low = lane < hd
    causal = lax.broadcasted_iota(jnp.int32, (rows, rows), 0) >= lax.broadcasted_iota(
        jnp.int32, (rows, rows), 1
    )
    r_i = lax.broadcasted_iota(jnp.int32, (2 * LANES, LANES), 0) % LANES
    c_i = lax.broadcasted_iota(jnp.int32, (2 * LANES, LANES), 1)
    adder = jnp.where((r_i < hd) & (c_i >= hd), -1.0 / (LANES - hd), 0.0).astype(BF16)
    for m in range(mine):
        total = jnp.zeros((LANES, width), F32)
        for c in range(blocks):
            q = qkv_ref[c, m, rows:]
            top = sketched(q, wa_ref[...])
            bottom = sketched(q, wb_ref[...])
            e0, e1, d0, d1 = tuple(jnp.concatenate([a, b], axis=0) for a, b in zip(top, bottom))
            e, d = e0 * e1, d0 * d1
            feat = features(e, d, sk, tiles)
            hi, lo = split(e)
            qdot = jnp.where(
                (lane >= sk) & (lane < 2 * sk),
                lo.astype(F32),
                jnp.where(lane < 3 * sk, hi.astype(F32), 0.0),
            ).astype(BF16)
            qdot_ref[m, c] = qdot
            kdot = kdot_ref[m, c]
            state = state_ref[m, c]
            ones = jnp.where(low, qkv_ref[c, m, :rows].astype(F32), 1.0).astype(BF16)
            dots = jnp.where(causal, mm(qdot, kdot, NT), 0.0)
            num = mm(feat, state, NT) + mm((dots * dots).astype(BF16), ones)
            inv = 1.0 / (1.0 + num)
            inv = jnp.where(low, pltpu.roll(inv, hd, 1), inv)
            g = g_ref[c, m].astype(F32)
            g = jnp.concatenate([g, pltpu.roll(g, hd, 1)], axis=0)
            g_hi, g_lo = split(jnp.where(low, g * num, 0.0))
            den = mm(jnp.concatenate([g_hi, g_lo], axis=1), adder)
            dn = (jnp.where(low, g, den * inv) * inv).astype(BF16)
            dn_ref[m, c] = dn
            cot_dots = (2.0 * dots * mm(dn, ones, NT)).astype(BF16)
            near = mm(cot_dots, kdot)
            cot = mm(dn, state)
            cot_e, cot_d = feature_pull(cot, e, d, sk, tiles)
            cot_e = cot_e + jnp.where((lane < sk) | (lane >= 2 * sk), near, 0.0)
            back = jnp.concatenate(
                [
                    (cot_e * e1).astype(BF16),
                    (cot_e * e0).astype(BF16),
                    (cot_d * d1).astype(BF16),
                    (cot_d * d0).astype(BF16),
                ],
                axis=1,
            )
            dq_ref[m, c] = (mm(back[:half], ba_ref[...]) + mm(back[half:], bb_ref[...])).astype(BF16)
            here = mm(dn, feat, TN)
            cot_ref[m, c] = here
            total = total + here
        total_ref[m] = total[: total_ref.shape[1]].astype(BF16)


def reverse_kernel(
    sk, hd, place_ref, qkv_ref, dq_ref, feat_ref, kdot_ref, qdot_ref, dn_ref, cot_ref, base_ref, wb_ref, bb_ref, *refs
):
    out_refs = refs[:-1]
    blocks_ref = refs[-1]
    blocks, mine, packed, _ = qkv_ref.shape
    rows = packed * 2 // 3
    width = base_ref.shape[2]
    tiles = width // LANES
    weights = lane_weights(sk, width)
    lane = lane_of(rows)
    low = lane < hd
    causal = lax.broadcasted_iota(jnp.int32, (rows, rows), 0) <= lax.broadcasted_iota(
        jnp.int32, (rows, rows), 1
    )
    for m in range(mine):
        state = base_ref[m]
        for c in reversed(range(blocks)):
            after = state.astype(BF16)
            vk = qkv_ref[c, m, :rows]
            e0, e1, d0, d1 = sketched(vk, wb_ref[...])
            e, d = e0 * e1, d0 * d1
            qdot = qdot_ref[m, c]
            dn = dn_ref[m, c]
            ones = jnp.where(low, vk.astype(F32), 1.0).astype(BF16)
            dots = jnp.where(causal, mm(kdot_ref[m, c], qdot, NT), 0.0)
            cot_dots = (2.0 * dots * mm(ones, dn, NT)).astype(BF16)
            near = mm(cot_dots, qdot)
            dv = mm(feat_ref[m, c], after, NT) + mm((dots * dots).astype(BF16), dn)
            cot = mm(ones, after)
            cot_e, cot_d = feature_pull(cot, e, d, sk, tiles)
            cot_e = cot_e + jnp.where(lane < 2 * sk, near, 0.0)
            back = jnp.concatenate(
                [
                    (cot_e * e1).astype(BF16),
                    (cot_e * e0).astype(BF16),
                    (cot_d * d1).astype(BF16),
                    (cot_d * d0).astype(BF16),
                ],
                axis=1,
            )
            slot = slot_of(place_ref[0], c, blocks)
            blocks_ref[slot, m, :rows] = (jnp.where(low, dv, 0.0) + mm(back, bb_ref[...])).astype(BF16)
            blocks_ref[slot, m, rows:] = dq_ref[m, c]
            state = state + cot_ref[m, c] * weights
    for s, out_ref in enumerate(out_refs):
        out_ref[...] = blocks_ref[s]


def input_kernel(hd, local, place_ref, order_ref, *refs):
    slots = refs[:local]
    weights = refs[local : local + 3]
    dq_ref, dk_ref, dv_ref, out_ref, all_ref, held_ref, done_ref = refs[local + 3 :]
    copies = bring(weights, order_ref, dk_ref.shape[1], held_ref, done_ref)
    _, mine, packed, _ = all_ref.shape
    for s, slot in enumerate(slots):
        all_ref[came_in(place_ref[0], s, local)] = slot[...]
    rows = packed * 2 // 3
    half = rows // 2
    low = lane_of(rows) < hd

    def block(head):
        return all_ref[head // mine, head % mine].astype(F32)

    for pair in range(local * mine // 2):
        a, b = block(2 * pair), block(2 * pair + 1)
        cols = slice(pair * LANES, (pair + 1) * LANES)
        dv_ref[:, cols] = jnp.where(low, a[:rows], pltpu.roll(b[:rows], hd, 1)).astype(BF16)
        dk_ref[:, cols] = jnp.where(low, pltpu.roll(a[:rows], hd, 1), b[:rows]).astype(BF16)
        a, b = a[rows:], b[rows:]
        dq_ref[:half, cols] = jnp.where(low[:half], a, pltpu.roll(b, hd, 1)).astype(BF16)
        dq_ref[half:, cols] = jnp.where(low[:half], pltpu.roll(a, hd, 1), b).astype(BF16)
    dq, dk, dv = dq_ref[...], dk_ref[...], dv_ref[...]
    for i in range(out_ref.shape[0]):
        total = None
        for k, x in enumerate((dq, dk, dv)):
            copies[k][i].wait()
            part = mm(x, held_ref[k, i], NT)
            total = part if total is None else total + part
        out_ref[i] = total.astype(BF16)


def expand_kernel(hd, local, place_ref, *refs):
    pieces = refs[:local]
    dstate_ref, dnorm_ref, map_ref, state_ref, norm_ref, all_ref = refs[local:]
    mine, rows, width = pieces[0].shape
    for k, piece in enumerate(pieces):
        all_ref[lax.bitwise_xor(place_ref[0], k)] = piece[...]
    heads = local * mine
    spread = mm(all_ref[...].reshape(heads * rows, width), map_ref[...], NT)
    for h in range(heads):
        state_ref[h] = dstate_ref[h] + spread[h * rows : h * rows + hd]
        norm_ref[h : h + 1] = dnorm_ref[h : h + 1] + spread[h * rows + hd : h * rows + hd + 1] * float(LANES - hd)


def call(kernel, name, out_shape, scalars, arrays, stay=(), mib=16, scratch=()):
    smem = pl.BlockSpec(memory_space=pltpu.SMEM)
    vmem = pl.BlockSpec(memory_space=pltpu.VMEM)
    return pl.pallas_call(
        kernel,
        in_specs=[smem] * len(scalars) + [vmem] * len(arrays) + [pl.BlockSpec(memory_space=pl.ANY)] * len(stay),
        out_specs=[vmem] * len(out_shape),
        out_shape=[jax.ShapeDtypeStruct(dims, kind) for dims, kind in out_shape],
        scratch_shapes=list(scratch),
        compiler_params=pltpu.CompilerParams(vmem_limit_bytes=mib * MIB),
        name=name,
    )(*scalars, *arrays, *stay)


def hop(x, axis, distance):
    count = lax.axis_size(axis)
    return lax.ppermute(x, axis, [(i, i ^ distance) for i in range(count)])


def body(groups, local, inputs, w_query, w_key, w_value, sketch, prefix_state, prefix_norm, d_attn, d_state_end, d_norm_end):
    rows, depth = inputs.shape
    width = w_query.shape[1]
    heads, feat, hd = prefix_state.shape
    sk = sketch.shape[2]
    tiles = tile_count(sk)
    lanes = tiles * LANES
    half = rows // 2
    packed = rows + half
    mine = heads // local
    ranks = lax.axis_size("head")
    rank = lax.axis_index("head")
    place = lax.axis_index("local")
    group = lax.axis_index("group")
    here = place.astype(jnp.int32)[None]

    def send(x, shift):
        return lax.ppermute(x, "local", [(i, (i + shift) % local) for i in range(local)])

    def exchange(x):
        order = sorted(range(1, local), key=lambda s: -min(s, local - s))
        came = {s: send(x[s], s) for s in order}
        came[0] = x[0]
        return [came[s] for s in range(local)]

    pieces = {0: inputs}
    distance = ranks // 2
    while distance:
        pieces.update({at ^ distance: hop(x, "head", distance) for at, x in list(pieces.items())})
        distance //= 2
    keys = sorted(pieces)
    where = jnp.stack([rank ^ at for at in keys]).astype(jnp.int32)

    (grad,) = call(
        partial(gradient_kernel, hd, local), "gather_cotangents", [((local, mine, half, LANES), BF16)], [], [d_attn]
    )
    grad = lax.all_to_all(grad, "local", 0, 0, tiled=True)

    table = jnp.asarray(pair_map(sk), BF16)

    state_t = prefix_state.transpose(0, 2, 1)
    dstate_t = d_state_end.transpose(0, 2, 1)
    own = lambda x: lax.dynamic_slice_in_dim(x, place * mine, mine, 0)
    base, base_after, wa, wb, ba, bb = call(
        partial(prepare_kernel, sk),
        "prepare",
        [((mine, LANES, lanes), F32)] * 2 + [((4 * hd, 4 * LANES), BF16)] * 2 + [((4 * LANES, 2 * hd), BF16)] * 2,
        [here],
        [sketch.transpose(0, 2, 1), own(state_t), prefix_norm, own(dstate_t), d_norm_end, table],
        scratch=[pltpu.VMEM((2, heads, lanes), F32)],
    )
    early = lax.optimization_barrier((pieces[keys[-1]], grad, base, base_after, wa, wb, ba, bb))
    pieces[keys[-1]], grad, base, base_after, wa, wb, ba, bb = early

    block = ((mine, packed, LANES), BF16)
    all_blocks = pltpu.VMEM((local,) + block[0], BF16)
    held = [pltpu.VMEM((3, ranks, depth, width), BF16), pltpu.SemaphoreType.DMA((3, ranks))]
    slots = call(
        partial(project_kernel, hd, local, len(keys)),
        "project",
        [block] * local,
        [here, where],
        [pieces[at] for at in keys],
        [w_value, w_key, w_query],
        scratch=[all_blocks] + held,
    )
    slots = exchange(slots)

    def key_side(start_state):
        return call(
            partial(key_kernel, sk, hd, local),
            "key_side",
            [
                ((local, mine, packed, LANES), BF16),
                ((mine, local, LANES, lanes), BF16),
                ((mine, local, rows, lanes), BF16),
                ((mine, local, rows, LANES), BF16),
                ((mine, LANES, lanes), F32),
            ],
            [here],
            [*slots, start_state, wb],
        )

    def of_groups(x, wanted):
        everything = lax.all_gather(x.astype(BF16), "group").astype(F32)
        chosen = wanted(jnp.arange(groups))
        return jnp.where(chosen.reshape((groups,) + (1,) * x.ndim), everything, 0.0).sum(0)

    if groups > 1:
        sums = key_side(jnp.zeros_like(base))[4]
        base = base + of_groups(sums, lambda at: at < group)
    qkv, states, key_feats, kdot, _ = key_side(base)

    dq, qdot, dn, cots, window = call(
        partial(query_kernel, sk, hd),
        "query_side",
        [
            ((mine, local, half, LANES), BF16),
            ((mine, local, rows, LANES), BF16),
            ((mine, local, rows, LANES), BF16),
            ((mine, local, LANES, lanes), F32),
            ((mine, hd + 16, lanes), BF16),
        ],
        [],
        [qkv, grad, kdot, states, wa, wb, ba, bb],
    )
    if groups > 1:
        later = of_groups(cots.sum(1), lambda at: at > group)
        base_after = base_after + later * lane_weights(sk, lanes)

    gradients = call(
        partial(reverse_kernel, sk, hd),
        "key_gradients",
        [block] * local,
        [here],
        [qkv, dq, key_feats, kdot, qdot, dn, cots, base_after, wb, bb],
        scratch=[all_blocks],
    )
    gradients = exchange(gradients)

    if groups > 1:
        window = lax.psum(window, "group")
    spread = {0: window}
    distance = local // 2
    while distance:
        both = jnp.stack([spread[at] for at in sorted(spread)])
        both = hop(both, "local", distance)
        spread.update({at ^ distance: both[n] for n, at in enumerate(sorted(spread))})
        distance //= 2

    order = sorted(range(ranks), key=lambda at: [-(at >> bit & 1) for bit in range(ranks.bit_length() - 1)])
    order_of = jnp.stack([rank ^ at for at in order]).astype(jnp.int32)
    d_query, d_key, d_value, sums = call(
        partial(input_kernel, hd, local),
        "input_gradient",
        [((rows, width), BF16)] * 3 + [((ranks, rows, depth), BF16)],
        [here, order_of],
        gradients,
        [w_query, w_key, w_value],
        scratch=[all_blocks] + held,
    )
    distance = 1
    while distance < ranks:
        count = sums.shape[0] // 2
        came = hop(sums[:count], "head", distance)
        sums = (sums[count:].astype(F32) + came.astype(F32)).astype(BF16)
        distance *= 2

    state_out, d_prefix_norm = call(
        partial(expand_kernel, hd, local),
        "prefix_gradients",
        [((heads, hd, feat), F32), ((heads, feat), F32)],
        [here],
        [*[spread[k] for k in range(local)], dstate_t, d_norm_end, table],
        scratch=[pltpu.VMEM((local,) + window.shape, BF16)],
    )
    d_prefix_state = state_out.transpose(0, 2, 1)
    return sums[0], d_query, d_key, d_value, d_prefix_state, d_prefix_norm


def solution(mesh):
    seq, head = mesh.shape["seq"], mesh.shape["head"]

    def run(*args):
        heads = args[5].shape[0] // head
        local = math.gcd(heads, seq)
        groups = seq // local
        inner = Mesh(mesh.devices.reshape(groups, local, head), ("group", "local", "head"))
        tokens = ("group", "local")
        return jax.shard_map(
            partial(body, groups, local),
            mesh=inner,
            in_specs=(
                P(tokens, "head"),
                P(None, "head"),
                P(None, "head"),
                P(None, "head"),
                P(),
                P("head", None, None),
                P("head", None),
                P(tokens, "head"),
                P("head", None, None),
                P("head", None),
            ),
            out_specs=(
                P(tokens, "head"),
                P(tokens, "head"),
                P(tokens, "head"),
                P(tokens, "head"),
                P("head", None, None),
                P("head", None),
            ),
            check_vma=False,
        )(*args)

    return run
```

time: 161 us -> 114 us (0.71)
  blocking collectives: 32.2 us -> 0 us
  local copies, waits for them, and re-layouts: 34.8 us -> 12.8 us
  starting transfers between devices: 29.7 us -> 45.2 us
  waiting for transfers between devices: 24.1 us -> 20.7 us
  Pallas kernels: 36.1 us -> 33.2 us
    all_gather x1 -> x0, blocking collectives: 32.2 us -> none  [body(): window = lax.all_gather(window, 'local', axis=0, tiled=True)]
    ppermute x0 -> x14, starting transfers between devices: none -> 23.7 us  [send(): lax.ppermute(x, 'local', [(i, (i + shift) % local) for i in range(local)])]
    all_to_all x5 -> x1, waiting for transfers between devices: 20.9 us -> 0.01 us  [body(): grad = lax.all_to_all(grad, 'local', 0, 0, tiled=True)]
    all_to_all x5 -> x1, starting transfers between devices: 25.4 us -> 5.83 us  [body(): grad = lax.all_to_all(grad, 'local', 0, 0, tiled=True)]
    unnamed x77 -> x48, local copies, waits for them, and re-layouts: 30.7 us -> 11.6 us
    ppermute x0 -> x14, waiting for transfers between devices: none -> 11.6 us  [send(): lax.ppermute(x, 'local', [(i, (i + shift) % local) for i in range(local)])]
    ppermute x5 -> x8, starting transfers between devices: 4.32 us -> 15.6 us  [hop(): return lax.ppermute(x, axis, [(i, i ^ distance) for i in range(count)])]
    ppermute x5 -> x8, waiting for transfers between devices: 3.22 us -> 9.06 us  [hop(): return lax.ppermute(x, axis, [(i, i ^ distance) for i in range(count)])]
  transfers between devices with their start and end apart: 10 -> 23, of which waited for: 6 -> 7; matrix products, arithmetic and copies ran while one was open for 4% -> 1% of each run, Pallas kernels for 14% -> 14%
where the time goes in v2:
time: 114 us
  starting transfers between devices  45.2 us (40%)
  Pallas kernels  33.2 us (29%)
  waiting for transfers between devices  20.7 us (18%)
  local copies, waits for them, and re-layouts  12.8 us (11%)
  other arithmetic  1.15 us (1%)
    pallas_call x8, Pallas kernels, call(): pl.pallas_call(kernel, in_specs=[smem] * len(scalars) + [vmem] * len(arra...  33.2 us
    ppermute x14, starting transfers between devices, send(): lax.ppermute(x, 'local', [(i, (i + shift) % local) for i in range(local)])  23.7 us
    ppermute x8, starting transfers between devices, hop(): return lax.ppermute(x, axis, [(i, i ^ distance) for i in range(count)])  15.6 us
    ppermute x14, waiting for transfers between devices, send(): lax.ppermute(x, 'local', [(i, (i + shift) % local) for i in range(local)])  11.6 us
    unnamed x48, local copies, waits for them, and re-layouts  11.6 us
    ppermute x8, waiting for transfers between devices, hop(): return lax.ppermute(x, axis, [(i, i ^ distance) for i in range(count)])  9.06 us
    all_to_all x1, starting transfers between devices, body(): grad = lax.all_to_all(grad, 'local', 0, 0, tiled=True)  5.83 us
  transfers between devices with their start and end apart: 23, of which 7 were waited for; matrix products, arithmetic and copies ran while one was open for 1% of the time, Pallas kernels for 14%

profile of v2, /device:TPU:0, one launch (start us, length us, event | category | flops | bytes accessed | tf_op | source)
XLA Modules:
  0.0 113.9 jit_solution(16516810482717963187)
XLA Ops:
  0.7 3.0 %collective-permute-start.1 = (bf16[256,512]{1,0:T(8,128)(2,1)}, bf16[256,512]{1,0:T(8,128)(2,1)}, u32[]{:S(2)}, u32[]{:S(2)}) collective-permute-start(bf16[256,512]{1,0:T(8,128)(2,1)} %refs_0_.1), channel_id=1, source_target_pairs={{0,2},{1,3},{2,0},{3,1},{4,6},{5,7},{6,4},{7,5},{8,10},{9,11},{10,... | collective-permute-start | bytes 786440 | tf_op jit(solution)/shard_map/ppermute | solution.py:410
  3.7 0.9 copy-done.17
  5.5 5.8 %all-to-all-start = ((bf16[8,1,128,128]{3,2,1,0:T(8,128)(2,1)}), bf16[8,1,128,128]{3,2,1,0:T(8,128)(2,1)}, u32[]{:S(2)}, u32[]{:S(2)}) async-start(bf16[8,1,128,128]{3,2,1,0:T(8,128)(2,1)} %copy-done.9), calls=%async_computation | async-start | bytes 524288 | tf_op jit(solution)/shard_map/all_to_all | solution.py:449
  11.9 1.1 dynamic-slice_bitcast_fusion
  15.2 1.7 %prepare.1 = (f32[1,128,640]{2,1,0:T(8,128)S(1)}, f32[1,128,640]{2,1,0:T(8,128)S(1)}, bf16[256,512]{1,0:T(8,128)(2,1)S(1)}, bf16[256,512]{1,0:T(8,128)(2,1)S(1)}...) custom-call(s32[1]{0:T(128)} %bitcast.place_ref, f32[2,32,64]{2,1,0:T(8,128)S(1)} %bitcast.33, ...), custom_call_target="tpu_custom_call" | custom-call | tf_op jit(solution)/shard_map/prepare/pallas_call | solution.py:397
  20.6 1.6 %copy-done.1 = bf16[2048,512]{1,0:T(8,128)(2,1)S(1)} copy-done((bf16[2048,512]{1,0:T(8,128)(2,1)S(1)}, bf16[2048,512]{1,0:T(8,128)(2,1)}, u32[]{:S(2)}) %copy-start.1) | copy-done | bytes 2097176
  22.2 1.6 %copy-done.3 = bf16[2048,512]{1,0:T(8,128)(2,1)S(1)} copy-done((bf16[2048,512]{1,0:T(8,128)(2,1)S(1)}, bf16[2048,512]{1,0:T(8,128)(2,1)}, u32[]{:S(2)}) %copy-start.3) | copy-done | bytes 2097176
  24.7 4.6 %project.1 = (bf16[1,384,128]{2,1,0:T(8,128)(2,1)S(1)}, bf16[1,384,128]{2,1,0:T(8,128)(2,1)S(1)}, bf16[1,384,128]{2,1,0:T(8,128)(2,1)S(1)}, bf16[1,384,128]{2,1,...) custom-call(s32[1]{0:T(128)} %bitcast.place_ref, ...), custom_call_target="tpu_custom_call" | custom-call | tf_op jit(solution)/shard_map/project/pallas_call | solution.py:397
  29.3 2.0 %collective-permute-start.3 = (bf16[1,384,128]{2,1,0:T(8,128)(2,1)S(1)}, bf16[1,384,128]{2,1,0:T(8,128)(2,1)S(1)}, u32[]{:S(2)}, u32[]{:S(2)}) collective-permute-start(bf16[1,384,128]{2,1,0:T(8,128)(2,1)S(1)} %get-tuple-element.59), channel_id=1, source_target_pairs={{0,4},{4,8},{8,12},{12,16},{16,20},{20,24},{24,28},{28,0},{1,5},{5... | collective-permute-start | bytes 294920 | tf_op jit(solution)/shard_map/ppermute | solution.py:430
  31.3 1.5 %collective-permute-start.4 = (bf16[1,384,128]{2,1,0:T(8,128)(2,1)S(1)}, bf16[1,384,128]{2,1,0:T(8,128)(2,1)S(1)}, u32[]{:S(2)}, u32[]{:S(2)}) collective-permute-start(bf16[1,384,128]{2,1,0:T(8,128)(2,1)S(1)} %get-tuple-element.60), channel_id=1, source_target_pairs={{0,8},{4,12},{8,16},{12,20},{16,24},{20,28},{24,0},{28,4},{1,9},{5... | collective-permute-start | bytes 294920 | tf_op jit(solution)/shard_map/ppermute | solution.py:430
  32.7 2.4 %collective-permute-start.5 = (bf16[1,384,128]{2,1,0:T(8,128)(2,1)S(1)}, bf16[1,384,128]{2,1,0:T(8,128)(2,1)S(1)}, u32[]{:S(2)}, u32[]{:S(2)}) collective-permute-start(bf16[1,384,128]{2,1,0:T(8,128)(2,1)S(1)} %get-tuple-element.61), channel_id=1, source_target_pairs={{0,12},{4,16},{8,20},{12,24},{16,28},{20,0},{24,4},{28,8},{1,13},{... | collective-permute-start | bytes 294920 | tf_op jit(solution)/shard_map/ppermute | solution.py:430
  35.1 1.5 %collective-permute-start.6 = (bf16[1,384,128]{2,1,0:T(8,128)(2,1)S(1)}, bf16[1,384,128]{2,1,0:T(8,128)(2,1)S(1)}, u32[]{:S(2)}, u32[]{:S(2)}) collective-permute-start(bf16[1,384,128]{2,1,0:T(8,128)(2,1)S(1)} %get-tuple-element.62), channel_id=1, source_target_pairs={{0,16},{4,20},{8,24},{12,28},{16,0},{20,4},{24,8},{28,12},{1,17},{... | collective-permute-start | bytes 294920 | tf_op jit(solution)/shard_map/ppermute | solution.py:430
  36.6 2.4 %collective-permute-start.7 = (bf16[1,384,128]{2,1,0:T(8,128)(2,1)S(1)}, bf16[1,384,128]{2,1,0:T(8,128)(2,1)S(1)}, u32[]{:S(2)}, u32[]{:S(2)}) collective-permute-start(bf16[1,384,128]{2,1,0:T(8,128)(2,1)S(1)} %get-tuple-element.63), channel_id=1, source_target_pairs={{0,20},{4,24},{8,28},{12,0},{16,4},{20,8},{24,12},{28,16},{1,21},{... | collective-permute-start | bytes 294920 | tf_op jit(solution)/shard_map/ppermute | solution.py:430
  38.9 1.5 %collective-permute-start.8 = (bf16[1,384,128]{2,1,0:T(8,128)(2,1)S(1)}, bf16[1,384,128]{2,1,0:T(8,128)(2,1)S(1)}, u32[]{:S(2)}, u32[]{:S(2)}) collective-permute-start(bf16[1,384,128]{2,1,0:T(8,128)(2,1)S(1)} %get-tuple-element.64), channel_id=1, source_target_pairs={{0,24},{4,28},{8,0},{12,4},{16,8},{20,12},{24,16},{28,20},{1,25},{... | collective-permute-start | bytes 294920 | tf_op jit(solution)/shard_map/ppermute | solution.py:430
  40.4 1.5 %collective-permute-start.9 = (bf16[1,384,128]{2,1,0:T(8,128)(2,1)S(1)}, bf16[1,384,128]{2,1,0:T(8,128)(2,1)S(1)}, u32[]{:S(2)}, u32[]{:S(2)}) collective-permute-start(bf16[1,384,128]{2,1,0:T(8,128)(2,1)S(1)} %get-tuple-element.65), channel_id=1, source_target_pairs={{0,28},{4,0},{8,4},{12,8},{16,12},{20,16},{24,20},{28,24},{1,29},{... | collective-permute-start | bytes 294920 | tf_op jit(solution)/shard_map/ppermute | solution.py:430
  41.9 3.8 %collective-permute-done.5.refs_3_ = bf16[1,384,128]{2,1,0:T(8,128)(2,1)S(1)} collective-permute-done((bf16[1,384,128]{2,1,0:T(8,128)(2,1)S(1)}, bf16[1,384,128]{2,1,0:T(8,128)(2,1)S(1)}, u32[]{:S(2)}, u32[]{:S(2)}) %collective-permute-start.5) | collective-permute-done | bytes 98336 | tf_op jit(solution)/shard_map/ppermute | solution.py:430
  46.5 3.7 %key_side.1 = (bf16[8,1,384,128]{3,2,1,0:T(8,128)(2,1)S(1)}, bf16[1,8,128,640]{3,2,1,0:T(8,128)(2,1)S(1)}, bf16[1,8,256,640]{3,2,1,0:T(8,128)(2,1)S(1)}, bf16[1,...) custom-call(s32[1]{0:T(128)} %bitcast.place_ref, bf16[1,384,128]{2,1,0:T(8,128)(2,1)S(1)} %get-tuple-element.58.refs_0_, ...), custom_call_target="tpu_custom_call" | custom-call | tf_op jit(solution)/shard_map/key_side/pallas_call | solution.py:397
  50.2 9.5 %query_side.1 = (bf16[1,8,128,128]{3,2,1,0:T(8,128)(2,1)S(1)}, bf16[1,8,256,128]{3,2,1,0:T(8,128)(2,1)S(1)}, bf16[1,8,256,128]{3,2,1,0:T(8,128)(2,1)S(1)}, f32[1...) custom-call(bf16[8,1,384,128]{3,2,1,0:T(8,128)(2,1)S(1)} %get-tuple-element.68.qkv_ref, ...), custom_call_target="tpu_custom_call" | custom-call | tf_op jit(solution)/shard_map/query_side/pallas_call | solution.py:397
  59.7 6.0 %collective-permute-start.19 = (bf16[1,1,80,640]{3,2,1,0:T(8,128)(2,1)S(1)}, bf16[1,1,80,640]{3,2,1,0:T(8,128)(2,1)S(1)}, u32[]{:S(2)}, u32[]{:S(2)}) collective-permute-start(bf16[1,1,80,640]{3,2,1,0:T(8,128)(2,1)S(1)} %bitcast.29), channel_id=1, source_target_pairs={{0,16},{4,20},{8,24},{12,28},{16,0},{20,4},{24,8},{28,12},{1,17},{... | collective-permute-start | bytes 307208 | tf_op jit(solution)/shard_map/ppermute | solution.py:410
  65.7 6.0 %key_gradients.1 = (bf16[1,384,128]{2,1,0:T(8,128)(2,1)S(1)}, bf16[1,384,128]{2,1,0:T(8,128)(2,1)S(1)}, bf16[1,384,128]{2,1,0:T(8,128)(2,1)S(1)}, bf16[1,384,128...) custom-call(s32[1]{0:T(128)} %bitcast.place_ref, ...), custom_call_target="tpu_custom_call" | custom-call | tf_op jit(solution)/shard_map/key_gradients/pallas_call | solution.py:397
  71.8 3.0 %collective-permute-start.10 = (bf16[1,384,128]{2,1,0:T(8,128)(2,1)S(1)}, bf16[1,384,128]{2,1,0:T(8,128)(2,1)S(1)}, u32[]{:S(2)}, u32[]{:S(2)}) collective-permute-start(bf16[1,384,128]{2,1,0:T(8,128)(2,1)S(1)} %get-tuple-element.82), channel_id=1, source_target_pairs={{0,4},{4,8},{8,12},{12,16},{16,20},{20,24},{24,28},{28,0},{1,5},{5... | collective-permute-start | bytes 294920 | tf_op jit(solution)/shard_map/ppermute | solution.py:430
  75.3 2.5 %collective-permute-start.20 = (bf16[2,1,80,640]{3,2,1,0:T(8,128)(2,1)S(1)}, bf16[2,1,80,640]{3,2,1,0:T(8,128)(2,1)S(1)}, u32[]{:S(2)}, u32[]{:S(2)}) collective-permute-start(bf16[2,1,80,640]{3,2,1,0:T(8,128)(2,1)S(1)} %pad_maximum_fusion.1), channel_id=1, source_target_pairs={{0,8},{4,12},{8,0},{12,4},{16,24},{20,28},{24,16},{28,20},{1,9},{5... | collective-permute-start | bytes 614408 | tf_op jit(solution)/shard_map/ppermute | solution.py:410
  77.8 1.5 %collective-permute-start.13 = (bf16[1,384,128]{2,1,0:T(8,128)(2,1)S(1)}, bf16[1,384,128]{2,1,0:T(8,128)(2,1)S(1)}, u32[]{:S(2)}, u32[]{:S(2)}) collective-permute-start(bf16[1,384,128]{2,1,0:T(8,128)(2,1)S(1)} %get-tuple-element.85), channel_id=1, source_target_pairs={{0,16},{4,20},{8,24},{12,28},{16,0},{20,4},{24,8},{28,12},{1,17},{... | collective-permute-start | bytes 294920 | tf_op jit(solution)/shard_map/ppermute | solution.py:430
  79.3 1.1 collective-permute-done.10.refs_1_
  80.4 2.7 %collective-permute-start.14 = (bf16[1,384,128]{2,1,0:T(8,128)(2,1)S(1)}, bf16[1,384,128]{2,1,0:T(8,128)(2,1)S(1)}, u32[]{:S(2)}, u32[]{:S(2)}) collective-permute-start(bf16[1,384,128]{2,1,0:T(8,128)(2,1)S(1)} %get-tuple-element.86), channel_id=1, source_target_pairs={{0,20},{4,24},{8,28},{12,0},{16,4},{20,8},{24,12},{28,16},{1,21},{... | collective-permute-start | bytes 294920 | tf_op jit(solution)/shard_map/ppermute | solution.py:430
  83.6 1.5 %collective-permute-done.12.refs_3_ = bf16[1,384,128]{2,1,0:T(8,128)(2,1)S(1)} collective-permute-done((bf16[1,384,128]{2,1,0:T(8,128)(2,1)S(1)}, bf16[1,384,128]{2,1,0:T(8,128)(2,1)S(1)}, u32[]{:S(2)}, u32[]{:S(2)}) %collective-permute-start.12) | collective-permute-done | bytes 98336 | tf_op jit(solution)/shard_map/ppermute | solution.py:430
  85.1 3.0 %collective-permute-start.16 = (bf16[1,384,128]{2,1,0:T(8,128)(2,1)S(1)}, bf16[1,384,128]{2,1,0:T(8,128)(2,1)S(1)}, u32[]{:S(2)}, u32[]{:S(2)}) collective-permute-start(bf16[1,384,128]{2,1,0:T(8,128)(2,1)S(1)} %get-tuple-element.88), channel_id=1, source_target_pairs={{0,28},{4,0},{8,4},{12,8},{16,12},{20,16},{24,20},{28,24},{1,29},{... | collective-permute-start | bytes 294920 | tf_op jit(solution)/shard_map/ppermute | solution.py:430
  88.2 4.4 %collective-permute-done.14.refs_5_ = bf16[1,384,128]{2,1,0:T(8,128)(2,1)S(1)} collective-permute-done((bf16[1,384,128]{2,1,0:T(8,128)(2,1)S(1)}, bf16[1,384,128]{2,1,0:T(8,128)(2,1)S(1)}, u32[]{:S(2)}, u32[]{:S(2)}) %collective-permute-start.14) | collective-permute-done | bytes 98336 | tf_op jit(solution)/shard_map/ppermute | solution.py:430
  92.6 5.0 %input_gradient.1 = (bf16[256,512]{1,0:T(8,128)(2,1)}, bf16[256,512]{1,0:T(8,128)(2,1)}, bf16[256,512]{1,0:T(8,128)(2,1)}, bf16[4,256,512]{2,1,0:T(8,128)(2,1)S(1)}) custom-call(s32[1]{0:T(128)} %bitcast.place_ref, s32[4]{0:T(128)S(1)} %pad_add_fusion.order_ref, bf16[1,384,128]{2,1,0:T(8,128)(2,1)S(1)} %get-tuple-element.81.refs_0_, ...), custom_call_target="tpu_custom_call" | custom-call | tf_op jit(solution)/shard_map/input_gradient/pallas_call | solution.py:397
  97.8 2.5 %collective-permute-start.21 = (bf16[4,1,80,640]{3,2,1,0:T(8,128)(2,1)S(1)}, bf16[4,1,80,640]{3,2,1,0:T(8,128)(2,1)S(1)}, u32[]{:S(2)}, u32[]{:S(2)}) collective-permute-start(bf16[4,1,80,640]{3,2,1,0:T(8,128)(2,1)S(1)} %pad_maximum_fusion), channel_id=1, source_target_pairs={{0,4},{4,0},{8,12},{12,8},{16,20},{20,16},{24,28},{28,24},{1,5},{5... | collective-permute-start | bytes 1228808 | tf_op jit(solution)/shard_map/ppermute | solution.py:410
  101.4 9.0 %collective-permute-done.21 = bf16[4,1,80,640]{3,2,1,0:T(8,128)(2,1)S(1)} collective-permute-done((bf16[4,1,80,640]{3,2,1,0:T(8,128)(2,1)S(1)}, bf16[4,1,80,640]{3,2,1,0:T(8,128)(2,1)S(1)}, u32[]{:S(2)}, u32[]{:S(2)}) %collective-permute-start.21) | collective-permute-done | bytes 409632 | tf_op jit(solution)/shard_map/ppermute | solution.py:410
  110.5 2.6 %prefix_gradients.1 = (f32[8,64,1024]{2,1,0:T(8,128)}, f32[8,1024]{1,0:T(8,128)}) custom-call(s32[1]{0:T(128)} %bitcast.place_ref, bf16[1,80,640]{2,1,0:T(8,128)(2,1)S(1)} %get-tuple-element.93.refs_0_, bf16[1,80,640]{2,1,0:T(8,128)(2,1)S(1)} %get-tuple-element.99.refs_1_, bf16[1,80,640]{2,1,0:T(8,128)(2,1)S(1)} %get-tuple-element.101.refs_2_, ...), custom_call_target="tpu_custom_call" | custom-call | tf_op jit(solution)/shard_map/prefix_gradients/pallas_call | solution.py:397
  (81 shorter events, 12.3 us)
Async XLA Ops:
  0.6 19.9 %copy-start = (bf16[2048,512]{1,0:T(8,128)(2,1)S(1)}, bf16[2048,512]{1,0:T(8,128)(2,1)}, u32[]{:S(2)}) copy-start(bf16[2048,512]{1,0:T(8,128)(2,1)} %refs_10_.2) | copy-start | bytes 6291460
  0.7 10.6 %collective-permute-start.1 = (bf16[256,512]{1,0:T(8,128)(2,1)}, bf16[256,512]{1,0:T(8,128)(2,1)}, u32[]{:S(2)}, u32[]{:S(2)}) collective-permute-start(bf16[256,512]{1,0:T(8,128)(2,1)} %refs_0_.1), channel_id=1, source_target_pairs={{0,2},{1,3},{2,0},{3,1},{4,6},{5,7},{6,4},{7,5},{8,10},{9,11},{10,... | collective-permute-start | bytes 786440 | tf_op jit(solution)/shard_map/ppermute | solution.py:410
  5.5 15.1 %all-to-all-start = ((bf16[8,1,128,128]{3,2,1,0:T(8,128)(2,1)}), bf16[8,1,128,128]{3,2,1,0:T(8,128)(2,1)}, u32[]{:S(2)}, u32[]{:S(2)}) async-start(bf16[8,1,128,128]{3,2,1,0:T(8,128)(2,1)} %copy-done.9), calls=%async_computation | async-start | bytes 524288 | tf_op jit(solution)/shard_map/all_to_all | solution.py:449
  11.3 9.3 %collective-permute-start.2 = (bf16[256,512]{1,0:T(8,128)(2,1)}, bf16[256,512]{1,0:T(8,128)(2,1)}, u32[]{:S(2)}, u32[]{:S(2)}) collective-permute-start(bf16[256,512]{1,0:T(8,128)(2,1)} %collective-permute-done.1.refs_2_), channel_id=1, source_target_pairs={{0,1},{1,0},{2,3},{3,2},{4,5},{5,4},{6,7},{7,6},{8,9},{9,8},{10,11... | collective-permute-start | bytes 786440 | tf_op jit(solution)/shard_map/ppermute | solution.py:410
  11.4 9.2 %collective-permute-start = (bf16[256,512]{1,0:T(8,128)(2,1)}, bf16[256,512]{1,0:T(8,128)(2,1)}, u32[]{:S(2)}, u32[]{:S(2)}) collective-permute-start(bf16[256,512]{1,0:T(8,128)(2,1)} %refs_0_.1), channel_id=1, source_target_pairs={{0,1},{1,0},{2,3},{3,2},{4,5},{5,4},{6,7},{7,6},{8,9},{9,8},{10,11... | collective-permute-start | bytes 786440 | tf_op jit(solution)/shard_map/ppermute | solution.py:410
  24.7 21.8 %copy-start.8 = (bf16[256,512]{1,0:T(8,128)(2,1)S(1)}, bf16[256,512]{1,0:T(8,128)(2,1)}, u32[]{:S(2)}) copy-start(bf16[256,512]{1,0:T(8,128)(2,1)} %copy-done.7) | copy-start | bytes 786436
  24.7 21.8 %copy-start.13 = (f32[1,128,640]{2,1,0:T(8,128)S(1)}, f32[1,128,640]{2,1,0:T(8,128)}, u32[]{:S(2)}) copy-start(f32[1,128,640]{2,1,0:T(8,128)} %copy-done.12) | copy-start | bytes 983044
  24.7 25.5 %copy-start.15 = (bf16[256,512]{1,0:T(8,128)(2,1)S(1)}, bf16[256,512]{1,0:T(8,128)(2,1)}, u32[]{:S(2)}) copy-start(bf16[256,512]{1,0:T(8,128)(2,1)} %copy-done.14) | copy-start | bytes 786436
  24.7 25.5 %copy-start.21 = (bf16[512,128]{1,0:T(8,128)(2,1)S(1)}, bf16[512,128]{1,0:T(8,128)(2,1)}, u32[]{:S(2)}) copy-start(bf16[512,128]{1,0:T(8,128)(2,1)} %copy-done.20) | copy-start | bytes 393220
  29.3 9.7 %collective-permute-start.3 = (bf16[1,384,128]{2,1,0:T(8,128)(2,1)S(1)}, bf16[1,384,128]{2,1,0:T(8,128)(2,1)S(1)}, u32[]{:S(2)}, u32[]{:S(2)}) collective-permute-start(bf16[1,384,128]{2,1,0:T(8,128)(2,1)S(1)} %get-tuple-element.59), channel_id=1, source_target_pairs={{0,4},{4,8},{8,12},{12,16},{16,20},{20,24},{24,28},{28,0},{1,5},{5... | collective-permute-start | bytes 294920 | tf_op jit(solution)/shard_map/ppermute | solution.py:430
  31.3 9.1 %collective-permute-start.4 = (bf16[1,384,128]{2,1,0:T(8,128)(2,1)S(1)}, bf16[1,384,128]{2,1,0:T(8,128)(2,1)S(1)}, u32[]{:S(2)}, u32[]{:S(2)}) collective-permute-start(bf16[1,384,128]{2,1,0:T(8,128)(2,1)S(1)} %get-tuple-element.60), channel_id=1, source_target_pairs={{0,8},{4,12},{8,16},{12,20},{16,24},{20,28},{24,0},{28,4},{1,9},{5... | collective-permute-start | bytes 294920 | tf_op jit(solution)/shard_map/ppermute | solution.py:430
  32.7 12.9 %collective-permute-start.5 = (bf16[1,384,128]{2,1,0:T(8,128)(2,1)S(1)}, bf16[1,384,128]{2,1,0:T(8,128)(2,1)S(1)}, u32[]{:S(2)}, u32[]{:S(2)}) collective-permute-start(bf16[1,384,128]{2,1,0:T(8,128)(2,1)S(1)} %get-tuple-element.61), channel_id=1, source_target_pairs={{0,12},{4,16},{8,20},{12,24},{16,28},{20,0},{24,4},{28,8},{1,13},{... | collective-permute-start | bytes 294920 | tf_op jit(solution)/shard_map/ppermute | solution.py:430
  35.1 11.2 %collective-permute-start.6 = (bf16[1,384,128]{2,1,0:T(8,128)(2,1)S(1)}, bf16[1,384,128]{2,1,0:T(8,128)(2,1)S(1)}, u32[]{:S(2)}, u32[]{:S(2)}) collective-permute-start(bf16[1,384,128]{2,1,0:T(8,128)(2,1)S(1)} %get-tuple-element.62), channel_id=1, source_target_pairs={{0,16},{4,20},{8,24},{12,28},{16,0},{20,4},{24,8},{28,12},{1,17},{... | collective-permute-start | bytes 294920 | tf_op jit(solution)/shard_map/ppermute | solution.py:430
  36.6 9.7 %collective-permute-start.7 = (bf16[1,384,128]{2,1,0:T(8,128)(2,1)S(1)}, bf16[1,384,128]{2,1,0:T(8,128)(2,1)S(1)}, u32[]{:S(2)}, u32[]{:S(2)}) collective-permute-start(bf16[1,384,128]{2,1,0:T(8,128)(2,1)S(1)} %get-tuple-element.63), channel_id=1, source_target_pairs={{0,20},{4,24},{8,28},{12,0},{16,4},{20,8},{24,12},{28,16},{1,21},{... | collective-permute-start | bytes 294920 | tf_op jit(solution)/shard_map/ppermute | solution.py:430
  38.9 7.4 %collective-permute-start.8 = (bf16[1,384,128]{2,1,0:T(8,128)(2,1)S(1)}, bf16[1,384,128]{2,1,0:T(8,128)(2,1)S(1)}, u32[]{:S(2)}, u32[]{:S(2)}) collective-permute-start(bf16[1,384,128]{2,1,0:T(8,128)(2,1)S(1)} %get-tuple-element.64), channel_id=1, source_target_pairs={{0,24},{4,28},{8,0},{12,4},{16,8},{20,12},{24,16},{28,20},{1,25},{... | collective-permute-start | bytes 294920 | tf_op jit(solution)/shard_map/ppermute | solution.py:430
  40.4 6.1 %collective-permute-start.9 = (bf16[1,384,128]{2,1,0:T(8,128)(2,1)S(1)}, bf16[1,384,128]{2,1,0:T(8,128)(2,1)S(1)}, u32[]{:S(2)}, u32[]{:S(2)}) collective-permute-start(bf16[1,384,128]{2,1,0:T(8,128)(2,1)S(1)} %get-tuple-element.65), channel_id=1, source_target_pairs={{0,28},{4,0},{8,4},{12,8},{16,12},{20,16},{24,20},{28,24},{1,29},{... | collective-permute-start | bytes 294920 | tf_op jit(solution)/shard_map/ppermute | solution.py:430
  50.2 15.6 %copy-start.11 = (f32[1,128,640]{2,1,0:T(8,128)S(1)}, f32[1,128,640]{2,1,0:T(8,128)}, u32[]{:S(2)}) copy-start(f32[1,128,640]{2,1,0:T(8,128)} %copy-done.10) | copy-start | bytes 983044
  59.7 15.6 %collective-permute-start.19 = (bf16[1,1,80,640]{3,2,1,0:T(8,128)(2,1)S(1)}, bf16[1,1,80,640]{3,2,1,0:T(8,128)(2,1)S(1)}, u32[]{:S(2)}, u32[]{:S(2)}) collective-permute-start(bf16[1,1,80,640]{3,2,1,0:T(8,128)(2,1)S(1)} %bitcast.29), channel_id=1, source_target_pairs={{0,16},{4,20},{8,24},{12,28},{16,0},{20,4},{24,8},{28,12},{1,17},{... | collective-permute-start | bytes 307208 | tf_op jit(solution)/shard_map/ppermute | solution.py:410
  65.7 26.8 %copy-start.2 = (bf16[2048,512]{1,0:T(8,128)(2,1)S(1)}, bf16[2048,512]{1,0:T(8,128)(2,1)}, u32[]{:S(2)}) copy-start(bf16[2048,512]{1,0:T(8,128)(2,1)} %refs_9_.2) | copy-start | bytes 6291460
  65.7 26.8 %copy-start.4 = (bf16[2048,512]{1,0:T(8,128)(2,1)S(1)}, bf16[2048,512]{1,0:T(8,128)(2,1)}, u32[]{:S(2)}) copy-start(bf16[2048,512]{1,0:T(8,128)(2,1)} %refs_8_.1) | copy-start | bytes 6291460
  71.8 8.6 %collective-permute-start.10 = (bf16[1,384,128]{2,1,0:T(8,128)(2,1)S(1)}, bf16[1,384,128]{2,1,0:T(8,128)(2,1)S(1)}, u32[]{:S(2)}, u32[]{:S(2)}) collective-permute-start(bf16[1,384,128]{2,1,0:T(8,128)(2,1)S(1)} %get-tuple-element.82), channel_id=1, source_target_pairs={{0,4},{4,8},{8,12},{12,16},{16,20},{20,24},{24,28},{28,0},{1,5},{5... | collective-permute-start | bytes 294920 | tf_op jit(solution)/shard_map/ppermute | solution.py:430
  74.8 8.3 %collective-permute-start.11 = (bf16[1,384,128]{2,1,0:T(8,128)(2,1)S(1)}, bf16[1,384,128]{2,1,0:T(8,128)(2,1)S(1)}, u32[]{:S(2)}, u32[]{:S(2)}) collective-permute-start(bf16[1,384,128]{2,1,0:T(8,128)(2,1)S(1)} %get-tuple-element.83), channel_id=1, source_target_pairs={{0,8},{4,12},{8,16},{12,20},{16,24},{20,28},{24,0},{28,4},{1,9},{5... | collective-permute-start | bytes 294920 | tf_op jit(solution)/shard_map/ppermute | solution.py:430
  75.3 9.8 %collective-permute-start.12 = (bf16[1,384,128]{2,1,0:T(8,128)(2,1)S(1)}, bf16[1,384,128]{2,1,0:T(8,128)(2,1)S(1)}, u32[]{:S(2)}, u32[]{:S(2)}) collective-permute-start(bf16[1,384,128]{2,1,0:T(8,128)(2,1)S(1)} %get-tuple-element.84), channel_id=1, source_target_pairs={{0,12},{4,16},{8,20},{12,24},{16,28},{20,0},{24,4},{28,8},{1,13},{... | collective-permute-start | bytes 294920 | tf_op jit(solution)/shard_map/ppermute | solution.py:430
  75.3 22.4 %collective-permute-start.20 = (bf16[2,1,80,640]{3,2,1,0:T(8,128)(2,1)S(1)}, bf16[2,1,80,640]{3,2,1,0:T(8,128)(2,1)S(1)}, u32[]{:S(2)}, u32[]{:S(2)}) collective-permute-start(bf16[2,1,80,640]{3,2,1,0:T(8,128)(2,1)S(1)} %pad_maximum_fusion.1), channel_id=1, source_target_pairs={{0,8},{4,12},{8,0},{12,4},{16,24},{20,28},{24,16},{28,20},{1,9},{5... | collective-permute-start | bytes 614408 | tf_op jit(solution)/shard_map/ppermute | solution.py:410
  77.8 10.4 %collective-permute-start.13 = (bf16[1,384,128]{2,1,0:T(8,128)(2,1)S(1)}, bf16[1,384,128]{2,1,0:T(8,128)(2,1)S(1)}, u32[]{:S(2)}, u32[]{:S(2)}) collective-permute-start(bf16[1,384,128]{2,1,0:T(8,128)(2,1)S(1)} %get-tuple-element.85), channel_id=1, source_target_pairs={{0,16},{4,20},{8,24},{12,28},{16,0},{20,4},{24,8},{28,12},{1,17},{... | collective-permute-start | bytes 294920 | tf_op jit(solution)/shard_map/ppermute | solution.py:430
  80.4 12.2 %collective-permute-start.14 = (bf16[1,384,128]{2,1,0:T(8,128)(2,1)S(1)}, bf16[1,384,128]{2,1,0:T(8,128)(2,1)S(1)}, u32[]{:S(2)}, u32[]{:S(2)}) collective-permute-start(bf16[1,384,128]{2,1,0:T(8,128)(2,1)S(1)} %get-tuple-element.86), channel_id=1, source_target_pairs={{0,20},{4,24},{8,28},{12,0},{16,4},{20,8},{24,12},{28,16},{1,21},{... | collective-permute-start | bytes 294920 | tf_op jit(solution)/shard_map/ppermute | solution.py:430
  83.1 9.5 %collective-permute-start.15 = (bf16[1,384,128]{2,1,0:T(8,128)(2,1)S(1)}, bf16[1,384,128]{2,1,0:T(8,128)(2,1)S(1)}, u32[]{:S(2)}, u32[]{:S(2)}) collective-permute-start(bf16[1,384,128]{2,1,0:T(8,128)(2,1)S(1)} %get-tuple-element.87), channel_id=1, source_target_pairs={{0,24},{4,28},{8,0},{12,4},{16,8},{20,12},{24,16},{28,20},{1,25},{... | collective-permute-start | bytes 294920 | tf_op jit(solution)/shard_map/ppermute | solution.py:430
  85.1 7.5 %collective-permute-start.16 = (bf16[1,384,128]{2,1,0:T(8,128)(2,1)S(1)}, bf16[1,384,128]{2,1,0:T(8,128)(2,1)S(1)}, u32[]{:S(2)}, u32[]{:S(2)}) collective-permute-start(bf16[1,384,128]{2,1,0:T(8,128)(2,1)S(1)} %get-tuple-element.88), channel_id=1, source_target_pairs={{0,28},{4,0},{8,4},{12,8},{16,12},{20,16},{24,20},{28,24},{1,29},{... | collective-permute-start | bytes 294920 | tf_op jit(solution)/shard_map/ppermute | solution.py:430
  97.6 12.9 %copy-start.6 = (f32[8,1024,64]{1,2,0:T(8,128)S(1)}, f32[8,1024,64]{1,2,0:T(8,128)}, u32[]{:S(2)}) copy-start(f32[8,1024,64]{1,2,0:T(8,128)} %param.19) | copy-start | bytes 6291460
  97.6 2.8 %collective-permute-start.17 = (bf16[2,256,512]{2,1,0:T(8,128)(2,1)S(1)}, bf16[2,256,512]{2,1,0:T(8,128)(2,1)S(1)}, u32[]{:S(2)}, u32[]{:S(2)}) collective-permute-start(bf16[2,256,512]{2,1,0:T(8,128)(2,1)S(1)} %slice.31), channel_id=1, source_target_pairs={{0,1},{1,0},{2,3},{3,2},{4,5},{5,4},{6,7},{7,6},{8,9},{9,8},{10,11... | collective-permute-start | bytes 1572872 | tf_op jit(solution)/shard_map/ppermute | solution.py:410
  97.8 12.7 %collective-permute-start.21 = (bf16[4,1,80,640]{3,2,1,0:T(8,128)(2,1)S(1)}, bf16[4,1,80,640]{3,2,1,0:T(8,128)(2,1)S(1)}, u32[]{:S(2)}, u32[]{:S(2)}) collective-permute-start(bf16[4,1,80,640]{3,2,1,0:T(8,128)(2,1)S(1)} %pad_maximum_fusion), channel_id=1, source_target_pairs={{0,4},{4,0},{8,12},{12,8},{16,20},{20,16},{24,28},{28,24},{1,5},{5... | collective-permute-start | bytes 1228808 | tf_op jit(solution)/shard_map/ppermute | solution.py:410
  100.5 12.6 %collective-permute-start.18 = (bf16[1,256,512]{2,1,0:T(8,128)(2,1)S(1)}, bf16[1,256,512]{2,1,0:T(8,128)(2,1)S(1)}, u32[]{:S(2)}, u32[]{:S(2)}) collective-permute-start(bf16[1,256,512]{2,1,0:T(8,128)(2,1)S(1)} %slice.41), channel_id=1, source_target_pairs={{0,2},{1,3},{2,0},{3,1},{4,6},{5,7},{6,4},{7,5},{8,10},{9,11},{10,... | collective-permute-start | bytes 786440 | tf_op jit(solution)/shard_map/ppermute | solution.py:410
  (15 other events, 36.8 us)

commit v3 on v2

--- a/solution.py
+++ b/solution.py
@@ -103,11 +103,18 @@
 
 
 def prepare_kernel(
-    sk, place_ref, sketch_ref, state_ref, norm_ref, dstate_ref, dnorm_ref, map_ref,
-    fwd_ref, bwd_ref, wa_ref, wb_ref, ba_ref, bb_ref, rows_ref,
+    sk, sketch_ref, norm_ref, dnorm_ref, map_ref, states_ref, dstates_ref,
+    fwd_ref, bwd_ref, wb_ref, ba_ref, bb_ref, rows_ref, state_ref, dstate_ref, done_ref,
 ):
+    mine, half, _ = state_ref.shape
+    own = pl.ds(lax.axis_index("local") * mine, mine)
+    copies = [
+        pltpu.make_async_copy(states_ref.at[own], state_ref, done_ref.at[0]),
+        pltpu.make_async_copy(dstates_ref.at[own], dstate_ref, done_ref.at[1]),
+    ]
+    for copy in copies:
+        copy.start()
     table = map_ref[...]
-    mine, half, _ = state_ref.shape
     step = LANES // sk
     left, right = sketch_ref[0], sketch_ref[1] * sk ** (-0.5)
 
@@ -121,7 +128,6 @@
     bb_ref[...] = jnp.concatenate([none, hi.astype(F32)], axis=1).astype(BF16)
     hi, lo = hi.astype(F32).T, lo.astype(F32).T
     none = jnp.zeros_like(hi)
-    wa_ref[...] = jnp.concatenate([hi, none, lo, none], axis=0).astype(BF16)
     wb_ref[...] = jnp.concatenate([none, hi, none, lo], axis=0).astype(BF16)
 
     def mapped(x):
@@ -132,81 +138,92 @@
         ((state_ref, norm_ref, fwd_ref, 1.0), (dstate_ref, dnorm_ref, bwd_ref, 1.0 / half))
     ):
         rows_ref[which] = mapped(n_ref[...]) * scale
+        copies[which].wait()
         for m in range(mine):
             o_ref[m, :half] = mapped(s_ref[m])
             o_ref[m, half:] = jnp.broadcast_to(
-                rows_ref[which, pl.ds(place_ref[0] * mine + m, 1), :], (LANES - half, o_ref.shape[2])
+                rows_ref[which, pl.ds(lax.axis_index("local") * mine + m, 1), :], (LANES - half, o_ref.shape[2])
             )
 
 
-def gradient_kernel(hd, local, grad_ref, out_ref):
-    rows = grad_ref.shape[0]
-    half = rows // 2
-    low = lane_of(half) < hd
-    mine = out_ref.shape[1]
-    for pair in range(local * mine // 2):
-        both = grad_ref[:, pair * LANES : (pair + 1) * LANES].astype(F32)
-        top, bottom = both[:half], both[half:]
-        for at, block in (
-            (2 * pair, jnp.where(low, top, pltpu.roll(bottom, hd, 1))),
-            (2 * pair + 1, jnp.where(low, pltpu.roll(top, hd, 1), bottom)),
-        ):
-            out_ref[at // mine, at % mine] = block.astype(BF16)
-
-
-def bring(weights, where_ref, depth, held_ref, done_ref):
-    copies = [
-        [
-            pltpu.make_async_copy(
-                w.at[pl.ds(pl.multiple_of(where_ref[i] * depth, depth), depth)], held_ref.at[k, i], done_ref.at[k, i]
-            )
-            for i in range(held_ref.shape[1])
-        ]
-        for k, w in enumerate(weights)
-    ]
-    for i in range(held_ref.shape[1]):
-        for k in range(len(weights)):
-            copies[k][i].start()
-    return copies
-
-
-def project_kernel(hd, local, count, place_ref, where_ref, *refs):
+def project_kernel(hd, local, count, *refs):
     pieces = refs[:count]
     weights = refs[count : count + 3]
-    out_refs = refs[count + 3 : -3]
-    blocks_ref, held_ref, done_ref = refs[-3:]
+    grad_ref = refs[count + 3]
+    out_refs = refs[count + 4 : -1]
+    blocks_ref = refs[-1]
     depth = pieces[0].shape[1]
     rows = pieces[0].shape[0]
-    half = rows // 2
     mine = blocks_ref.shape[1]
-    copies = bring(weights, where_ref, depth, held_ref, done_ref)
     sums = []
-    for k in range(len(weights)):
+    for w in weights:
         total = None
         for i, x in enumerate(pieces):
-            copies[k][i].wait()
-            part = mm(x[...], held_ref[k, i])
+            part = mm(x[...], w[pl.ds(pl.multiple_of(lax.bitwise_xor(lax.axis_index("head"), i) * depth, depth), depth), :])
             total = part if total is None else total + part
         sums.append(total)
     value, key, query = sums
     for h in range(local * mine):
         cols = slice(h * hd, (h + 1) * hd)
-        slot = slot_of(place_ref[0], h // mine, local)
+        slot = slot_of(lax.axis_index("local"), h // mine, local)
         blocks_ref[slot, h % mine, :rows] = jnp.concatenate([value[:, cols], key[:, cols]], axis=1).astype(BF16)
         blocks_ref[slot, h % mine, rows:] = jnp.concatenate(
-            [query[:half, cols], query[half:, cols]], axis=1
+            [grad_ref[:, cols].astype(F32), query[:, cols]], axis=1
         ).astype(BF16)
     for s, out_ref in enumerate(out_refs):
         out_ref[...] = blocks_ref[s]
 
 
-def key_kernel(sk, hd, local, place_ref, *refs):
+def window_rows(hd, sk):
+    tiles = tile_count(sk)
+    return (tiles - 1) * hd + hd // (2 * LANES // sk) + 8
+
+
+def pack_window(total, hd, sk):
+    tiles = tile_count(sk)
+    used = sk // 2
+    short = hd // (LANES // used)
+    lane = lane_of(short)
+    row = lax.broadcasted_iota(jnp.int32, (8, LANES), 0)
+    last = total[:hd, LANES * (tiles - 1) :]
+    tail = jnp.zeros((short, LANES), F32)
+    for i in range(LANES // used):
+        part = last[short * i : short * (i + 1)]
+        tail = jnp.where(lane // used == i, pltpu.roll(part, used * i, 1) if i else part, tail)
+    sums = jnp.zeros((8, LANES), F32)
+    for t in range(tiles):
+        sums = jnp.where(row == t, total[hd : hd + 8, LANES * t : LANES * (t + 1)], sums)
+    full = [total[:hd, LANES * t : LANES * (t + 1)] for t in range(tiles - 1)]
+    return jnp.concatenate(full + [tail, sums], axis=0).astype(BF16)
+
+
+def unpack_window(packed, hd, sk):
+    tiles = tile_count(sk)
+    used = sk // 2
+    short = hd // (LANES // used)
+    lane = lane_of(short)
+    end = (tiles - 1) * hd
+    rest = packed[end:].astype(F32)
+    tail, sums = rest[:short], rest[short:]
+    parts = []
+    for i in range(LANES // used):
+        part = jnp.where(lane < used, pltpu.roll(tail, LANES - used * i, 1) if i else tail, 0.0)
+        parts.append(part + pltpu.roll(part, used, 1))
+    last = jnp.concatenate(parts, axis=0).astype(BF16)
+    state = jnp.concatenate([packed[hd * t : hd * (t + 1)] for t in range(tiles - 1)] + [last], axis=1)
+    norm = jnp.concatenate(
+        [jnp.broadcast_to(sums[t : t + 1], (16, LANES)) for t in range(tiles)], axis=1
+    ).astype(BF16)
+    return jnp.concatenate([state, norm], axis=0)
+
+
+def key_kernel(sk, hd, local, *refs):
     slots = refs[:local]
     base_ref, wb_ref, qkv_ref, state_ref, feat_ref, kdot_ref, total_ref = refs[local:]
     blocks, mine, packed, _ = qkv_ref.shape
     for s, slot in enumerate(slots):
-        qkv_ref[came_in(place_ref[0], s, blocks)] = slot[...]
-    rows = packed * 2 // 3
+        qkv_ref[came_in(lax.axis_index("local"), s, blocks)] = slot[...]
+    rows = packed // 2
     width = base_ref.shape[2]
     tiles = width // LANES
     weights = lane_weights(sk, width)
@@ -230,11 +247,11 @@
 
 
 def query_kernel(
-    sk, hd, qkv_ref, g_ref, kdot_ref, state_ref, wa_ref, wb_ref, ba_ref, bb_ref,
+    sk, hd, qkv_ref, kdot_ref, state_ref, wb_ref, ba_ref, bb_ref,
     dq_ref, qdot_ref, dn_ref, cot_ref, total_ref,
 ):
     blocks, mine, packed, _ = qkv_ref.shape
-    rows = packed * 2 // 3
+    rows = packed // 2
     half = rows // 2
     width = state_ref.shape[3]
     tiles = width // LANES
@@ -249,10 +266,8 @@
     for m in range(mine):
         total = jnp.zeros((LANES, width), F32)
         for c in range(blocks):
-            q = qkv_ref[c, m, rows:]
-            top = sketched(q, wa_ref[...])
-            bottom = sketched(q, wb_ref[...])
-            e0, e1, d0, d1 = tuple(jnp.concatenate([a, b], axis=0) for a, b in zip(top, bottom))
+            gq = qkv_ref[c, m, rows:]
+            e0, e1, d0, d1 = sketched(gq, wb_ref[...])
             e, d = e0 * e1, d0 * d1
             feat = features(e, d, sk, tiles)
             hi, lo = split(e)
@@ -269,8 +284,7 @@
             num = mm(feat, state, NT) + mm((dots * dots).astype(BF16), ones)
             inv = 1.0 / (1.0 + num)
             inv = jnp.where(low, pltpu.roll(inv, hd, 1), inv)
-            g = g_ref[c, m].astype(F32)
-            g = jnp.concatenate([g, pltpu.roll(g, hd, 1)], axis=0)
+            g = gq.astype(F32)
             g_hi, g_lo = split(jnp.where(low, g * num, 0.0))
             den = mm(jnp.concatenate([g_hi, g_lo], axis=1), adder)
             dn = (jnp.where(low, g, den * inv) * inv).astype(BF16)
@@ -293,16 +307,16 @@
             here = mm(dn, feat, TN)
             cot_ref[m, c] = here
             total = total + here
-        total_ref[m] = total[: total_ref.shape[1]].astype(BF16)
+        total_ref[m] = pack_window(total, hd, sk)
 
 
 def reverse_kernel(
-    sk, hd, place_ref, qkv_ref, dq_ref, feat_ref, kdot_ref, qdot_ref, dn_ref, cot_ref, base_ref, wb_ref, bb_ref, *refs
+    sk, hd, window_ref, qkv_ref, dq_ref, feat_ref, kdot_ref, qdot_ref, dn_ref, cot_ref, base_ref, wb_ref, bb_ref, *refs
 ):
     out_refs = refs[:-1]
     blocks_ref = refs[-1]
-    blocks, mine, packed, _ = qkv_ref.shape
-    rows = packed * 2 // 3
+    mine, blocks, rows, _ = dn_ref.shape
+    packed = rows + rows // 2
     width = base_ref.shape[2]
     tiles = width // LANES
     weights = lane_weights(sk, width)
@@ -337,22 +351,23 @@
                 ],
                 axis=1,
             )
-            slot = slot_of(place_ref[0], c, blocks)
+            slot = slot_of(lax.axis_index("local"), c, blocks)
             blocks_ref[slot, m, :rows] = (jnp.where(low, dv, 0.0) + mm(back, bb_ref[...])).astype(BF16)
             blocks_ref[slot, m, rows:] = dq_ref[m, c]
             state = state + cot_ref[m, c] * weights
     for s, out_ref in enumerate(out_refs):
-        out_ref[...] = blocks_ref[s]
-
-
-def input_kernel(hd, local, place_ref, order_ref, *refs):
+        out_ref[:, :packed] = blocks_ref[s]
+        out_ref[:, packed:] = window_ref[...]
+
+
+def input_kernel(hd, local, order, *refs):
     slots = refs[:local]
     weights = refs[local : local + 3]
-    dq_ref, dk_ref, dv_ref, out_ref, all_ref, held_ref, done_ref = refs[local + 3 :]
-    copies = bring(weights, order_ref, dk_ref.shape[1], held_ref, done_ref)
+    dq_ref, dk_ref, dv_ref, out_ref, all_ref = refs[local + 3 :]
+    depth = dk_ref.shape[1]
     _, mine, packed, _ = all_ref.shape
     for s, slot in enumerate(slots):
-        all_ref[came_in(place_ref[0], s, local)] = slot[...]
+        all_ref[came_in(lax.axis_index("local"), s, local)] = slot[:, :packed]
     rows = packed * 2 // 3
     half = rows // 2
     low = lane_of(rows) < hd
@@ -371,38 +386,38 @@
     dq, dk, dv = dq_ref[...], dk_ref[...], dv_ref[...]
     for i in range(out_ref.shape[0]):
         total = None
-        for k, x in enumerate((dq, dk, dv)):
-            copies[k][i].wait()
-            part = mm(x, held_ref[k, i], NT)
+        for w, x in zip(weights, (dq, dk, dv)):
+            part = mm(x, w[pl.ds(pl.multiple_of(lax.bitwise_xor(lax.axis_index("head"), order[i]) * depth, depth), depth), :], NT)
             total = part if total is None else total + part
         out_ref[i] = total.astype(BF16)
 
 
-def expand_kernel(hd, local, place_ref, *refs):
-    pieces = refs[:local]
+def expand_kernel(hd, sk, local, *refs):
+    slots = refs[:local]
     dstate_ref, dnorm_ref, map_ref, state_ref, norm_ref, all_ref = refs[local:]
-    mine, rows, width = pieces[0].shape
-    for k, piece in enumerate(pieces):
-        all_ref[lax.bitwise_xor(place_ref[0], k)] = piece[...]
-    heads = local * mine
+    mine = slots[0].shape[0]
+    first = slots[0].shape[1] - window_rows(hd, sk)
+    heads, rows, width = all_ref.shape
+    for s, slot in enumerate(slots):
+        for m in range(mine):
+            all_ref[came_in(lax.axis_index("local"), s, local) * mine + m] = unpack_window(slot[m, first:], hd, sk)
     spread = mm(all_ref[...].reshape(heads * rows, width), map_ref[...], NT)
     for h in range(heads):
         state_ref[h] = dstate_ref[h] + spread[h * rows : h * rows + hd]
         norm_ref[h : h + 1] = dnorm_ref[h : h + 1] + spread[h * rows + hd : h * rows + hd + 1] * float(LANES - hd)
 
 
-def call(kernel, name, out_shape, scalars, arrays, stay=(), mib=16, scratch=()):
-    smem = pl.BlockSpec(memory_space=pltpu.SMEM)
+def call(kernel, name, out_shape, arrays, stay=(), mib=16, scratch=()):
     vmem = pl.BlockSpec(memory_space=pltpu.VMEM)
     return pl.pallas_call(
         kernel,
-        in_specs=[smem] * len(scalars) + [vmem] * len(arrays) + [pl.BlockSpec(memory_space=pl.ANY)] * len(stay),
+        in_specs=[vmem] * len(arrays) + [pl.BlockSpec(memory_space=pltpu.HBM)] * len(stay),
         out_specs=[vmem] * len(out_shape),
         out_shape=[jax.ShapeDtypeStruct(dims, kind) for dims, kind in out_shape],
         scratch_shapes=list(scratch),
         compiler_params=pltpu.CompilerParams(vmem_limit_bytes=mib * MIB),
         name=name,
-    )(*scalars, *arrays, *stay)
+    )(*arrays, *stay)
 
 
 def hop(x, axis, distance):
@@ -421,10 +436,7 @@
     packed = rows + half
     mine = heads // local
     ranks = lax.axis_size("head")
-    rank = lax.axis_index("head")
-    place = lax.axis_index("local")
     group = lax.axis_index("group")
-    here = place.astype(jnp.int32)[None]
 
     def send(x, shift):
         return lax.ppermute(x, "local", [(i, (i + shift) % local) for i in range(local)])
@@ -436,45 +448,42 @@
         return [came[s] for s in range(local)]
 
     pieces = {0: inputs}
-    distance = ranks // 2
+    far = {ranks // 2: hop(inputs, "head", ranks // 2)} if ranks > 1 else {}
+
+    table = jnp.asarray(pair_map(sk), BF16)
+
+    state_t = prefix_state.transpose(0, 2, 1)
+    dstate_t = d_state_end.transpose(0, 2, 1)
+    base, base_after, wb, ba, bb = call(
+        partial(prepare_kernel, sk),
+        "prepare",
+        [((mine, LANES, lanes), F32)] * 2 + [((4 * hd, 4 * LANES), BF16)] + [((4 * LANES, 2 * hd), BF16)] * 2,
+        [sketch.transpose(0, 2, 1), prefix_norm, d_norm_end, table],
+        [state_t, dstate_t],
+        scratch=[
+            pltpu.VMEM((2, heads, lanes), F32),
+            pltpu.VMEM((mine, hd, feat), F32),
+            pltpu.VMEM((mine, hd, feat), F32),
+            pltpu.SemaphoreType.DMA((2,)),
+        ],
+    )
+    far, base, base_after, wb, ba, bb = lax.optimization_barrier((far, base, base_after, wb, ba, bb))
+    pieces.update(far)
+    distance = ranks // 4
     while distance:
         pieces.update({at ^ distance: hop(x, "head", distance) for at, x in list(pieces.items())})
         distance //= 2
-    keys = sorted(pieces)
-    where = jnp.stack([rank ^ at for at in keys]).astype(jnp.int32)
-
-    (grad,) = call(
-        partial(gradient_kernel, hd, local), "gather_cotangents", [((local, mine, half, LANES), BF16)], [], [d_attn]
-    )
-    grad = lax.all_to_all(grad, "local", 0, 0, tiled=True)
-
-    table = jnp.asarray(pair_map(sk), BF16)
-
-    state_t = prefix_state.transpose(0, 2, 1)
-    dstate_t = d_state_end.transpose(0, 2, 1)
-    own = lambda x: lax.dynamic_slice_in_dim(x, place * mine, mine, 0)
-    base, base_after, wa, wb, ba, bb = call(
-        partial(prepare_kernel, sk),
-        "prepare",
-        [((mine, LANES, lanes), F32)] * 2 + [((4 * hd, 4 * LANES), BF16)] * 2 + [((4 * LANES, 2 * hd), BF16)] * 2,
-        [here],
-        [sketch.transpose(0, 2, 1), own(state_t), prefix_norm, own(dstate_t), d_norm_end, table],
-        scratch=[pltpu.VMEM((2, heads, lanes), F32)],
-    )
-    early = lax.optimization_barrier((pieces[keys[-1]], grad, base, base_after, wa, wb, ba, bb))
-    pieces[keys[-1]], grad, base, base_after, wa, wb, ba, bb = early
-
-    block = ((mine, packed, LANES), BF16)
+    keys = range(ranks)
+
+    block = ((mine, 2 * rows, LANES), BF16)
     all_blocks = pltpu.VMEM((local,) + block[0], BF16)
-    held = [pltpu.VMEM((3, ranks, depth, width), BF16), pltpu.SemaphoreType.DMA((3, ranks))]
+    back_blocks = pltpu.VMEM((local, mine, packed, LANES), BF16)
     slots = call(
         partial(project_kernel, hd, local, len(keys)),
         "project",
         [block] * local,
-        [here, where],
-        [pieces[at] for at in keys],
-        [w_value, w_key, w_query],
-        scratch=[all_blocks] + held,
+        [pieces[at] for at in keys] + [w_value, w_key, w_query, d_attn],
+        scratch=[all_blocks],
     )
     slots = exchange(slots)
 
@@ -483,13 +492,12 @@
             partial(key_kernel, sk, hd, local),
             "key_side",
             [
-                ((local, mine, packed, LANES), BF16),
+                ((local, mine, 2 * rows, LANES), BF16),
                 ((mine, local, LANES, lanes), BF16),
                 ((mine, local, rows, lanes), BF16),
                 ((mine, local, rows, LANES), BF16),
                 ((mine, LANES, lanes), F32),
             ],
-            [here],
             [*slots, start_state, wb],
         )
 
@@ -511,45 +519,32 @@
             ((mine, local, rows, LANES), BF16),
             ((mine, local, rows, LANES), BF16),
             ((mine, local, LANES, lanes), F32),
-            ((mine, hd + 16, lanes), BF16),
+            ((mine, window_rows(hd, sk), LANES), BF16),
         ],
-        [],
-        [qkv, grad, kdot, states, wa, wb, ba, bb],
+        [qkv, kdot, states, wb, ba, bb],
     )
     if groups > 1:
         later = of_groups(cots.sum(1), lambda at: at > group)
         base_after = base_after + later * lane_weights(sk, lanes)
 
+    if groups > 1:
+        window = lax.psum(window, "group")
     gradients = call(
         partial(reverse_kernel, sk, hd),
         "key_gradients",
-        [block] * local,
-        [here],
-        [qkv, dq, key_feats, kdot, qdot, dn, cots, base_after, wb, bb],
-        scratch=[all_blocks],
+        [((mine, packed + window_rows(hd, sk), LANES), BF16)] * local,
+        [window, qkv, dq, key_feats, kdot, qdot, dn, cots, base_after, wb, bb],
+        scratch=[back_blocks],
     )
     gradients = exchange(gradients)
 
-    if groups > 1:
-        window = lax.psum(window, "group")
-    spread = {0: window}
-    distance = local // 2
-    while distance:
-        both = jnp.stack([spread[at] for at in sorted(spread)])
-        both = hop(both, "local", distance)
-        spread.update({at ^ distance: both[n] for n, at in enumerate(sorted(spread))})
-        distance //= 2
-
     order = sorted(range(ranks), key=lambda at: [-(at >> bit & 1) for bit in range(ranks.bit_length() - 1)])
-    order_of = jnp.stack([rank ^ at for at in order]).astype(jnp.int32)
     d_query, d_key, d_value, sums = call(
-        partial(input_kernel, hd, local),
+        partial(input_kernel, hd, local, order),
         "input_gradient",
         [((rows, width), BF16)] * 3 + [((ranks, rows, depth), BF16)],
-        [here, order_of],
-        gradients,
-        [w_query, w_key, w_value],
-        scratch=[all_blocks] + held,
+        [*gradients, w_query, w_key, w_value],
+        scratch=[back_blocks],
     )
     distance = 1
     while distance < ranks:
@@ -559,12 +554,11 @@
         distance *= 2
 
     state_out, d_prefix_norm = call(
-        partial(expand_kernel, hd, local),
+        partial(expand_kernel, hd, sk, local),
         "prefix_gradients",
         [((heads, hd, feat), F32), ((heads, feat), F32)],
-        [here],
-        [*[spread[k] for k in range(local)], dstate_t, d_norm_end, table],
-        scratch=[pltpu.VMEM((local,) + window.shape, BF16)],
+        [*gradients, dstate_t, d_norm_end, table],
+        scratch=[pltpu.VMEM((heads, hd + 16, lanes), BF16)],
     )
     d_prefix_state = state_out.transpose(0, 2, 1)
     return sums[0], d_query, d_key, d_value, d_prefix_state, d_prefix_norm

time: 114 us -> 108 us (0.947)
  the two profiles are of different devices: /device:TPU:0 before, /device:TPU:12 now
where the time goes in v3:
time: 108 us
  waiting for transfers between devices  51.8 us (48%)
  Pallas kernels  27.7 us (26%)
  starting transfers between devices  18.5 us (17%)
  local copies, waits for them, and re-layouts  8.44 us (8%)
    ppermute x14, waiting for transfers between devices, send(): lax.ppermute(x, 'local', [(i, (i + shift) % local) for i in range(local)])  43.6 us
    pallas_call x7, Pallas kernels, call(): pl.pallas_call(kernel, in_specs=[vmem] * len(arrays) + [pl.BlockSpec(memo...  27.7 us
    ppermute x14, starting transfers between devices, send(): lax.ppermute(x, 'local', [(i, (i + shift) % local) for i in range(local)])  15.7 us
    unnamed x30, local copies, waits for them, and re-layouts  8.39 us
    ppermute x5, waiting for transfers between devices, hop(): return lax.ppermute(x, axis, [(i, i ^ distance) for i in range(count)])  8.15 us
    ppermute x5, starting transfers between devices, hop(): return lax.ppermute(x, axis, [(i, i ^ distance) for i in range(count)])  2.81 us
  transfers between devices with their start and end apart: 19, of which 14 were waited for; matrix products, arithmetic and copies ran while one was open for 0% of the time, Pallas kernels for 4%

profile of v3, /device:TPU:12, one launch (start us, length us, event | category | flops | bytes accessed | tf_op | source)
XLA Modules:
  0.0 108.0 jit_solution(7748307348297595883)
XLA Ops:
  0.6 1.6 %collective-permute-start.1 = (bf16[256,512]{1,0:T(8,128)(2,1)}, bf16[256,512]{1,0:T(8,128)(2,1)S(1)}, u32[]{:S(2)}, u32[]{:S(2)}) collective-permute-start(bf16[256,512]{1,0:T(8,128)(2,1)} %refs_0_.1), channel_id=1, source_target_pairs={{0,2},{1,3},{2,0},{3,1},{4,6},{5,7},{6,4},{7,5},{8,10},{9,11},{10,... | collective-permute-start | bytes 786440 | tf_op jit(solution)/shard_map/ppermute | solution.py:425
  2.2 1.6 %copy-done = f32[8,1024,64]{1,2,0:T(8,128)S(1)} copy-done((f32[8,1024,64]{1,2,0:T(8,128)S(1)}, f32[8,1024,64]{1,2,0:T(8,128)}, u32[]{:S(2)}) %copy-start) | copy-done | bytes 2097176
  3.8 1.3 %copy-done.6 = bf16[1024,640]{1,0:T(8,128)(2,1)S(1)} copy-done((bf16[1024,640]{1,0:T(8,128)(2,1)S(1)}, bf16[1024,640]{1,0:T(8,128)(2,1)}, u32[]{:S(2)}) %copy-start.6) | copy-done | bytes 1310744
  5.1 1.6 %copy-done.8 = f32[8,1024,64]{1,2,0:T(8,128)S(1)} copy-done((f32[8,1024,64]{1,2,0:T(8,128)S(1)}, f32[8,1024,64]{1,2,0:T(8,128)}, u32[]{:S(2)}) %copy-start.8) | copy-done | bytes 2097176
  9.0 2.0 %prepare.1 = (f32[1,128,640]{2,1,0:T(8,128)S(1)}, f32[1,128,640]{2,1,0:T(8,128)S(1)}, bf16[256,512]{1,0:T(8,128)(2,1)S(1)}, bf16[512,128]{1,0:T(8,128)(2,1)S(1)}, bf16[512,128]{1,0:T(8,128)(2,1)S(1)}) custom-call(f32[2,32,64]{2,1,0:T(8,128)S(1)} %bitcast.9, f32[8,1024]{1,0:T(8,128)S(1)} %copy-done.14, f32[8,1024]{1,0:T(8,128)S(1)} %copy-done.11, ...), custom_call_target="tpu_custom_call" | custom-call | tf_op jit(solution)/shard_map/prepare/pallas_call | solution.py:412
  11.6 1.2 %collective-permute-done.2.refs_3_ = bf16[256,512]{1,0:T(8,128)(2,1)S(1)} collective-permute-done((bf16[256,512]{1,0:T(8,128)(2,1)S(1)}, bf16[256,512]{1,0:T(8,128)(2,1)S(1)}, u32[]{:S(2)}, u32[]{:S(2)}) %collective-permute-start.2) | collective-permute-done | bytes 262176 | tf_op jit(solution)/shard_map/ppermute | solution.py:425
  12.8 1.6 %copy-done.4 = bf16[2048,512]{1,0:T(8,128)(2,1)S(1)} copy-done((bf16[2048,512]{1,0:T(8,128)(2,1)S(1)}, bf16[2048,512]{1,0:T(8,128)(2,1)}, u32[]{:S(2)}) %copy-start.4) | copy-done | bytes 2097176
  14.4 2.0 %project.1 = (bf16[1,512,128]{2,1,0:T(8,128)(2,1)S(1)}, bf16[1,512,128]{2,1,0:T(8,128)(2,1)S(1)}, bf16[1,512,128]{2,1,0:T(8,128)(2,1)S(1)}, bf16[1,512,128]{2,1,...) custom-call(bf16[256,512]{1,0:T(8,128)(2,1)S(1)} %copy-done.9, ...), custom_call_target="tpu_custom_call" | custom-call | tf_op jit(solution)/shard_map/project/pallas_call | solution.py:412
  16.4 1.6 %collective-permute-start.3 = (bf16[1,512,128]{2,1,0:T(8,128)(2,1)S(1)}, bf16[1,512,128]{2,1,0:T(8,128)(2,1)S(1)}, u32[]{:S(2)}, u32[]{:S(2)}) collective-permute-start(bf16[1,512,128]{2,1,0:T(8,128)(2,1)S(1)} %get-tuple-element.55), channel_id=1, source_target_pairs={{0,4},{4,8},{8,12},{12,16},{16,20},{20,24},{24,28},{28,0},{1,5},{5... | collective-permute-start | bytes 393224 | tf_op jit(solution)/shard_map/ppermute | solution.py:442
  18.0 1.6 %collective-permute-start.4 = (bf16[1,512,128]{2,1,0:T(8,128)(2,1)S(1)}, bf16[1,512,128]{2,1,0:T(8,128)(2,1)S(1)}, u32[]{:S(2)}, u32[]{:S(2)}) collective-permute-start(bf16[1,512,128]{2,1,0:T(8,128)(2,1)S(1)} %get-tuple-element.56), channel_id=1, source_target_pairs={{0,8},{4,12},{8,16},{12,20},{16,24},{20,28},{24,0},{28,4},{1,9},{5... | collective-permute-start | bytes 393224 | tf_op jit(solution)/shard_map/ppermute | solution.py:442
  19.6 1.2 %collective-permute-start.5 = (bf16[1,512,128]{2,1,0:T(8,128)(2,1)S(1)}, bf16[1,512,128]{2,1,0:T(8,128)(2,1)S(1)}, u32[]{:S(2)}, u32[]{:S(2)}) collective-permute-start(bf16[1,512,128]{2,1,0:T(8,128)(2,1)S(1)} %get-tuple-element.57), channel_id=1, source_target_pairs={{0,12},{4,16},{8,20},{12,24},{16,28},{20,0},{24,4},{28,8},{1,13},{... | collective-permute-start | bytes 393224 | tf_op jit(solution)/shard_map/ppermute | solution.py:442
  20.7 1.7 %collective-permute-start.6 = (bf16[1,512,128]{2,1,0:T(8,128)(2,1)S(1)}, bf16[1,512,128]{2,1,0:T(8,128)(2,1)S(1)}, u32[]{:S(2)}, u32[]{:S(2)}) collective-permute-start(bf16[1,512,128]{2,1,0:T(8,128)(2,1)S(1)} %get-tuple-element.58), channel_id=1, source_target_pairs={{0,16},{4,20},{8,24},{12,28},{16,0},{20,4},{24,8},{28,12},{1,17},{... | collective-permute-start | bytes 393224 | tf_op jit(solution)/shard_map/ppermute | solution.py:442
  22.4 1.3 %collective-permute-start.7 = (bf16[1,512,128]{2,1,0:T(8,128)(2,1)S(1)}, bf16[1,512,128]{2,1,0:T(8,128)(2,1)S(1)}, u32[]{:S(2)}, u32[]{:S(2)}) collective-permute-start(bf16[1,512,128]{2,1,0:T(8,128)(2,1)S(1)} %get-tuple-element.59), channel_id=1, source_target_pairs={{0,20},{4,24},{8,28},{12,0},{16,4},{20,8},{24,12},{28,16},{1,21},{... | collective-permute-start | bytes 393224 | tf_op jit(solution)/shard_map/ppermute | solution.py:442
  23.7 1.3 %collective-permute-start.8 = (bf16[1,512,128]{2,1,0:T(8,128)(2,1)S(1)}, bf16[1,512,128]{2,1,0:T(8,128)(2,1)S(1)}, u32[]{:S(2)}, u32[]{:S(2)}) collective-permute-start(bf16[1,512,128]{2,1,0:T(8,128)(2,1)S(1)} %get-tuple-element.60), channel_id=1, source_target_pairs={{0,24},{4,28},{8,0},{12,4},{16,8},{20,12},{24,16},{28,20},{1,25},{... | collective-permute-start | bytes 393224 | tf_op jit(solution)/shard_map/ppermute | solution.py:442
  25.1 10.6 %collective-permute-done.4.refs_2_ = bf16[1,512,128]{2,1,0:T(8,128)(2,1)S(1)} collective-permute-done((bf16[1,512,128]{2,1,0:T(8,128)(2,1)S(1)}, bf16[1,512,128]{2,1,0:T(8,128)(2,1)S(1)}, u32[]{:S(2)}, u32[]{:S(2)}) %collective-permute-start.4) | collective-permute-done | bytes 131104 | tf_op jit(solution)/shard_map/ppermute | solution.py:442
  35.7 2.9 %collective-permute-done.5.refs_3_ = bf16[1,512,128]{2,1,0:T(8,128)(2,1)S(1)} collective-permute-done((bf16[1,512,128]{2,1,0:T(8,128)(2,1)S(1)}, bf16[1,512,128]{2,1,0:T(8,128)(2,1)S(1)}, u32[]{:S(2)}, u32[]{:S(2)}) %collective-permute-start.5) | collective-permute-done | bytes 131104 | tf_op jit(solution)/shard_map/ppermute | solution.py:442
  38.7 2.3 %collective-permute-done.6.refs_4_ = bf16[1,512,128]{2,1,0:T(8,128)(2,1)S(1)} collective-permute-done((bf16[1,512,128]{2,1,0:T(8,128)(2,1)S(1)}, bf16[1,512,128]{2,1,0:T(8,128)(2,1)S(1)}, u32[]{:S(2)}, u32[]{:S(2)}) %collective-permute-start.6) | collective-permute-done | bytes 131104 | tf_op jit(solution)/shard_map/ppermute | solution.py:442
  40.9 1.9 %collective-permute-done.8.refs_6_ = bf16[1,512,128]{2,1,0:T(8,128)(2,1)S(1)} collective-permute-done((bf16[1,512,128]{2,1,0:T(8,128)(2,1)S(1)}, bf16[1,512,128]{2,1,0:T(8,128)(2,1)S(1)}, u32[]{:S(2)}, u32[]{:S(2)}) %collective-permute-start.8) | collective-permute-done | bytes 131104 | tf_op jit(solution)/shard_map/ppermute | solution.py:442
  43.9 3.7 %key_side.1 = (bf16[8,1,512,128]{3,2,1,0:T(8,128)(2,1)S(1)}, bf16[1,8,128,640]{3,2,1,0:T(8,128)(2,1)S(1)}, bf16[1,8,256,640]{3,2,1,0:T(8,128)(2,1)S(1)}, bf16[1,...) custom-call(bf16[1,512,128]{2,1,0:T(8,128)(2,1)S(1)} %get-tuple-element.54.refs_0_, ...), custom_call_target="tpu_custom_call" | custom-call | tf_op jit(solution)/shard_map/key_side/pallas_call | solution.py:412
  47.6 8.5 %query_side.1 = (bf16[1,8,128,128]{3,2,1,0:T(8,128)(2,1)S(1)}, bf16[1,8,256,128]{3,2,1,0:T(8,128)(2,1)S(1)}, bf16[1,8,256,128]{3,2,1,0:T(8,128)(2,1)S(1)}, f32[1...) custom-call(bf16[8,1,512,128]{3,2,1,0:T(8,128)(2,1)S(1)} %get-tuple-element.64.qkv_ref, ...), custom_call_target="tpu_custom_call" | custom-call | tf_op jit(solution)/shard_map/query_side/pallas_call | solution.py:412
  56.2 6.1 %key_gradients.1 = (bf16[1,656,128]{2,1,0:T(8,128)(2,1)S(1)}, bf16[1,656,128]{2,1,0:T(8,128)(2,1)S(1)}, bf16[1,656,128]{2,1,0:T(8,128)(2,1)S(1)}, bf16[1,656,128...) custom-call(bf16[1,272,128]{2,1,0:T(8,128)(2,1)S(1)} %get-tuple-elem, ...), custom_call_target="tpu_custom_call" | custom-call | tf_op jit(solution)/shard_map/key_gradients/pallas_call | solution.py:412
  62.7 2.8 %collective-permute-start.12 = (bf16[1,656,128]{2,1,0:T(8,128)(2,1)S(1)}, bf16[1,656,128]{2,1,0:T(8,128)(2,1)S(1)}, u32[]{:S(2)}, u32[]{:S(2)}) collective-permute-start(bf16[1,656,128]{2,1,0:T(8,128)(2,1)S(1)} %get-tuple-element.79), channel_id=1, source_target_pairs={{0,12},{4,16},{8,20},{12,24},{16,28},{20,0},{24,4},{28,8},{1,13},{... | collective-permute-start | bytes 503816 | tf_op jit(solution)/shard_map/ppermute | solution.py:442
  65.4 1.6 %collective-permute-start.13 = (bf16[1,656,128]{2,1,0:T(8,128)(2,1)S(1)}, bf16[1,656,128]{2,1,0:T(8,128)(2,1)S(1)}, u32[]{:S(2)}, u32[]{:S(2)}) collective-permute-start(bf16[1,656,128]{2,1,0:T(8,128)(2,1)S(1)} %get-tuple-element.80), channel_id=1, source_target_pairs={{0,16},{4,20},{8,24},{12,28},{16,0},{20,4},{24,8},{28,12},{1,17},{... | collective-permute-start | bytes 503816 | tf_op jit(solution)/shard_map/ppermute | solution.py:442
  68.6 1.3 %collective-permute-start.15 = (bf16[1,656,128]{2,1,0:T(8,128)(2,1)S(1)}, bf16[1,656,128]{2,1,0:T(8,128)(2,1)S(1)}, u32[]{:S(2)}, u32[]{:S(2)}) collective-permute-start(bf16[1,656,128]{2,1,0:T(8,128)(2,1)S(1)} %get-tuple-element.82), channel_id=1, source_target_pairs={{0,24},{4,28},{8,0},{12,4},{16,8},{20,12},{24,16},{28,20},{1,25},{... | collective-permute-start | bytes 503816 | tf_op jit(solution)/shard_map/ppermute | solution.py:442
  69.9 15.1 %collective-permute-done.11.refs_2_ = bf16[1,656,128]{2,1,0:T(8,128)(2,1)S(1)} collective-permute-done((bf16[1,656,128]{2,1,0:T(8,128)(2,1)S(1)}, bf16[1,656,128]{2,1,0:T(8,128)(2,1)S(1)}, u32[]{:S(2)}, u32[]{:S(2)}) %collective-permute-start.11) | collective-permute-done | bytes 167968 | tf_op jit(solution)/shard_map/ppermute | solution.py:442
  84.9 3.6 %collective-permute-done.12.refs_3_ = bf16[1,656,128]{2,1,0:T(8,128)(2,1)S(1)} collective-permute-done((bf16[1,656,128]{2,1,0:T(8,128)(2,1)S(1)}, bf16[1,656,128]{2,1,0:T(8,128)(2,1)S(1)}, u32[]{:S(2)}, u32[]{:S(2)}) %collective-permute-start.12) | collective-permute-done | bytes 167968 | tf_op jit(solution)/shard_map/ppermute | solution.py:442
  88.5 3.0 %collective-permute-done.13.refs_4_ = bf16[1,656,128]{2,1,0:T(8,128)(2,1)S(1)} collective-permute-done((bf16[1,656,128]{2,1,0:T(8,128)(2,1)S(1)}, bf16[1,656,128]{2,1,0:T(8,128)(2,1)S(1)}, u32[]{:S(2)}, u32[]{:S(2)}) %collective-permute-start.13) | collective-permute-done | bytes 167968 | tf_op jit(solution)/shard_map/ppermute | solution.py:442
  91.5 1.4 %collective-permute-done.15.refs_6_ = bf16[1,656,128]{2,1,0:T(8,128)(2,1)S(1)} collective-permute-done((bf16[1,656,128]{2,1,0:T(8,128)(2,1)S(1)}, bf16[1,656,128]{2,1,0:T(8,128)(2,1)S(1)}, u32[]{:S(2)}, u32[]{:S(2)}) %collective-permute-start.15) | collective-permute-done | bytes 167968 | tf_op jit(solution)/shard_map/ppermute | solution.py:442
  94.0 2.6 %input_gradient.1 = (bf16[256,512]{1,0:T(8,128)(2,1)}, bf16[256,512]{1,0:T(8,128)(2,1)}, bf16[256,512]{1,0:T(8,128)(2,1)}, bf16[4,256,512]{2,1,0:T(8,128)(2,1)S(1)}) custom-call(bf16[1,656,128]{2,1,0:T(8,128)(2,1)S(1)} %get-tuple-element.76.refs_0_, bf16[1,656,128]{2,1,0:T(8,128)(2,1)S(1)} %collective-permute-done.10.refs_1_, ...), custom_call_target="tpu_custom_call" | custom-call | tf_op jit(solution)/shard_map/input_gradient/pallas_call | solution.py:412
  96.8 1.9 %collective-permute-done.17 = bf16[2,256,512]{2,1,0:T(8,128)(2,1)S(1)} collective-permute-done((bf16[2,256,512]{2,1,0:T(8,128)(2,1)S(1)}, bf16[2,256,512]{2,1,0:T(8,128)(2,1)S(1)}, u32[]{:S(2)}, u32[]{:S(2)}) %collective-permute-start.17) | collective-permute-done | bytes 524320 | tf_op jit(solution)/shard_map/ppermute | solution.py:425
  99.4 2.7 %prefix_gradients.1 = (f32[8,64,1024]{2,1,0:T(8,128)}, f32[8,1024]{1,0:T(8,128)}) custom-call(bf16[1,656,128]{2,1,0:T(8,128)(2,1)S(1)} %get-tuple-element.76.refs_0_, bf16[1,656,128]{2,1,0:T(8,128)(2,1)S(1)} %collective-permute-done.10.refs_1_, bf16[1,656,128]{2,1,0:T(8,128)(2,1)S(1)} %collective-permute-done.11.refs_2_, ...), custom_call_target="tpu_custom_call" | custom-call | tf_op jit(solution)/shard_map/prefix_gradients/pallas_call | solution.py:412
  102.2 5.1 %collective-permute-done.18 = bf16[1,256,512]{2,1,0:T(8,128)(2,1)S(1)} collective-permute-done((bf16[1,256,512]{2,1,0:T(8,128)(2,1)S(1)}, bf16[1,256,512]{2,1,0:T(8,128)(2,1)S(1)}, u32[]{:S(2)}, u32[]{:S(2)}) %collective-permute-start.18) | collective-permute-done | bytes 262176 | tf_op jit(solution)/shard_map/ppermute | solution.py:425
  (47 shorter events, 8.8 us)
Async XLA Ops:
  0.6 10.4 %collective-permute-start.1 = (bf16[256,512]{1,0:T(8,128)(2,1)}, bf16[256,512]{1,0:T(8,128)(2,1)S(1)}, u32[]{:S(2)}, u32[]{:S(2)}) collective-permute-start(bf16[256,512]{1,0:T(8,128)(2,1)} %refs_0_.1), channel_id=1, source_target_pairs={{0,2},{1,3},{2,0},{3,1},{4,6},{5,7},{6,4},{7,5},{8,10},{9,11},{10,... | collective-permute-start | bytes 786440 | tf_op jit(solution)/shard_map/ppermute | solution.py:425
  2.2 9.4 %collective-permute-start = (bf16[256,512]{1,0:T(8,128)(2,1)}, bf16[256,512]{1,0:T(8,128)(2,1)S(1)}, u32[]{:S(2)}, u32[]{:S(2)}) collective-permute-start(bf16[256,512]{1,0:T(8,128)(2,1)} %refs_0_.1), channel_id=1, source_target_pairs={{0,1},{1,0},{2,3},{3,2},{4,5},{5,4},{6,7},{7,6},{8,9},{9,8},{10,11... | collective-permute-start | bytes 786440 | tf_op jit(solution)/shard_map/ppermute | solution.py:425
  2.2 1.6 %copy-start = (f32[8,1024,64]{1,2,0:T(8,128)S(1)}, f32[8,1024,64]{1,2,0:T(8,128)}, u32[]{:S(2)}) copy-start(f32[8,1024,64]{1,2,0:T(8,128)} %param.19) | copy-start | bytes 6291460
  3.8 1.3 %copy-start.6 = (bf16[1024,640]{1,0:T(8,128)(2,1)S(1)}, bf16[1024,640]{1,0:T(8,128)(2,1)}, u32[]{:S(2)}) copy-start(bf16[1024,640]{1,0:T(8,128)(2,1)} %constant.2.clone.map_ref.refs_10_) | copy-start | bytes 3932164
  5.1 1.6 %copy-start.8 = (f32[8,1024,64]{1,2,0:T(8,128)S(1)}, f32[8,1024,64]{1,2,0:T(8,128)}, u32[]{:S(2)}) copy-start(f32[8,1024,64]{1,2,0:T(8,128)} %param.16) | copy-start | bytes 6291460
  6.7 0.8 copy-start.11
  9.0 3.8 %copy-start.2 = (bf16[2048,512]{1,0:T(8,128)(2,1)S(1)}, bf16[2048,512]{1,0:T(8,128)(2,1)}, u32[]{:S(2)}) copy-start(bf16[2048,512]{1,0:T(8,128)(2,1)} %refs_10_.2) | copy-start | bytes 6291460
  9.0 3.8 %copy-start.3 = (bf16[2048,512]{1,0:T(8,128)(2,1)S(1)}, bf16[2048,512]{1,0:T(8,128)(2,1)}, u32[]{:S(2)}) copy-start(bf16[2048,512]{1,0:T(8,128)(2,1)} %refs_9_.2) | copy-start | bytes 6291460
  9.0 3.8 %copy-start.9 = (bf16[256,512]{1,0:T(8,128)(2,1)S(1)}, bf16[256,512]{1,0:T(8,128)(2,1)}, u32[]{:S(2)}) copy-start(bf16[256,512]{1,0:T(8,128)(2,1)} %refs_0_.1) | copy-start | bytes 786436
  9.0 3.8 %copy-start.10 = (bf16[256,512]{1,0:T(8,128)(2,1)S(1)}, bf16[256,512]{1,0:T(8,128)(2,1)}, u32[]{:S(2)}) copy-start(bf16[256,512]{1,0:T(8,128)(2,1)} %refs_7_.1) | copy-start | bytes 786436
  11.0 1.7 %collective-permute-start.2 = (bf16[256,512]{1,0:T(8,128)(2,1)S(1)}, bf16[256,512]{1,0:T(8,128)(2,1)S(1)}, u32[]{:S(2)}, u32[]{:S(2)}) collective-permute-start(bf16[256,512]{1,0:T(8,128)(2,1)S(1)} %collective-permute-done.1.refs_2_), channel_id=1, source_target_pairs={{0,1},{1,0},{2,3},{3,2},{4,5},{5,4},{6,7},{7,6},{8,9},{9,8},{10,11... | collective-permute-start | bytes 786440 | tf_op jit(solution)/shard_map/ppermute | solution.py:425
  12.8 1.6 %copy-start.4 = (bf16[2048,512]{1,0:T(8,128)(2,1)S(1)}, bf16[2048,512]{1,0:T(8,128)(2,1)}, u32[]{:S(2)}) copy-start(bf16[2048,512]{1,0:T(8,128)(2,1)} %refs_8_.1) | copy-start | bytes 6291460
  16.4 7.3 %collective-permute-start.3 = (bf16[1,512,128]{2,1,0:T(8,128)(2,1)S(1)}, bf16[1,512,128]{2,1,0:T(8,128)(2,1)S(1)}, u32[]{:S(2)}, u32[]{:S(2)}) collective-permute-start(bf16[1,512,128]{2,1,0:T(8,128)(2,1)S(1)} %get-tuple-element.55), channel_id=1, source_target_pairs={{0,4},{4,8},{8,12},{12,16},{16,20},{20,24},{24,28},{28,0},{1,5},{5... | collective-permute-start | bytes 393224 | tf_op jit(solution)/shard_map/ppermute | solution.py:442
  18.0 17.7 %collective-permute-start.4 = (bf16[1,512,128]{2,1,0:T(8,128)(2,1)S(1)}, bf16[1,512,128]{2,1,0:T(8,128)(2,1)S(1)}, u32[]{:S(2)}, u32[]{:S(2)}) collective-permute-start(bf16[1,512,128]{2,1,0:T(8,128)(2,1)S(1)} %get-tuple-element.56), channel_id=1, source_target_pairs={{0,8},{4,12},{8,16},{12,20},{16,24},{20,28},{24,0},{28,4},{1,9},{5... | collective-permute-start | bytes 393224 | tf_op jit(solution)/shard_map/ppermute | solution.py:442
  19.6 19.1 %collective-permute-start.5 = (bf16[1,512,128]{2,1,0:T(8,128)(2,1)S(1)}, bf16[1,512,128]{2,1,0:T(8,128)(2,1)S(1)}, u32[]{:S(2)}, u32[]{:S(2)}) collective-permute-start(bf16[1,512,128]{2,1,0:T(8,128)(2,1)S(1)} %get-tuple-element.57), channel_id=1, source_target_pairs={{0,12},{4,16},{8,20},{12,24},{16,28},{20,0},{24,4},{28,8},{1,13},{... | collective-permute-start | bytes 393224 | tf_op jit(solution)/shard_map/ppermute | solution.py:442
  20.7 20.2 %collective-permute-start.6 = (bf16[1,512,128]{2,1,0:T(8,128)(2,1)S(1)}, bf16[1,512,128]{2,1,0:T(8,128)(2,1)S(1)}, u32[]{:S(2)}, u32[]{:S(2)}) collective-permute-start(bf16[1,512,128]{2,1,0:T(8,128)(2,1)S(1)} %get-tuple-element.58), channel_id=1, source_target_pairs={{0,16},{4,20},{8,24},{12,28},{16,0},{20,4},{24,8},{28,12},{1,17},{... | collective-permute-start | bytes 393224 | tf_op jit(solution)/shard_map/ppermute | solution.py:442
  22.4 18.5 %collective-permute-start.7 = (bf16[1,512,128]{2,1,0:T(8,128)(2,1)S(1)}, bf16[1,512,128]{2,1,0:T(8,128)(2,1)S(1)}, u32[]{:S(2)}, u32[]{:S(2)}) collective-permute-start(bf16[1,512,128]{2,1,0:T(8,128)(2,1)S(1)} %get-tuple-element.59), channel_id=1, source_target_pairs={{0,20},{4,24},{8,28},{12,0},{16,4},{20,8},{24,12},{28,16},{1,21},{... | collective-permute-start | bytes 393224 | tf_op jit(solution)/shard_map/ppermute | solution.py:442
  23.7 19.1 %collective-permute-start.8 = (bf16[1,512,128]{2,1,0:T(8,128)(2,1)S(1)}, bf16[1,512,128]{2,1,0:T(8,128)(2,1)S(1)}, u32[]{:S(2)}, u32[]{:S(2)}) collective-permute-start(bf16[1,512,128]{2,1,0:T(8,128)(2,1)S(1)} %get-tuple-element.60), channel_id=1, source_target_pairs={{0,24},{4,28},{8,0},{12,4},{16,8},{20,12},{24,16},{28,20},{1,25},{... | collective-permute-start | bytes 393224 | tf_op jit(solution)/shard_map/ppermute | solution.py:442
  35.7 8.2 %collective-permute-start.9 = (bf16[1,512,128]{2,1,0:T(8,128)(2,1)S(1)}, bf16[1,512,128]{2,1,0:T(8,128)(2,1)S(1)}, u32[]{:S(2)}, u32[]{:S(2)}) collective-permute-start(bf16[1,512,128]{2,1,0:T(8,128)(2,1)S(1)} %get-tuple-element.61), channel_id=1, source_target_pairs={{0,28},{4,0},{8,4},{12,8},{16,12},{20,16},{24,20},{28,24},{1,29},{... | collective-permute-start | bytes 393224 | tf_op jit(solution)/shard_map/ppermute | solution.py:442
  56.2 37.8 %copy-start.5 = (bf16[2048,512]{1,0:T(8,128)(2,1)S(1)}, bf16[2048,512]{1,0:T(8,128)(2,1)}, u32[]{:S(2)}) copy-start(bf16[2048,512]{1,0:T(8,128)(2,1)} %refs_8_.1) | copy-start | bytes 6291460
  62.3 6.3 %collective-permute-start.10 = (bf16[1,656,128]{2,1,0:T(8,128)(2,1)S(1)}, bf16[1,656,128]{2,1,0:T(8,128)(2,1)S(1)}, u32[]{:S(2)}, u32[]{:S(2)}) collective-permute-start(bf16[1,656,128]{2,1,0:T(8,128)(2,1)S(1)} %get-tuple-element.77), channel_id=1, source_target_pairs={{0,4},{4,8},{8,12},{12,16},{16,20},{20,24},{24,28},{28,0},{1,5},{5... | collective-permute-start | bytes 503816 | tf_op jit(solution)/shard_map/ppermute | solution.py:442
  62.3 22.6 %collective-permute-start.11 = (bf16[1,656,128]{2,1,0:T(8,128)(2,1)S(1)}, bf16[1,656,128]{2,1,0:T(8,128)(2,1)S(1)}, u32[]{:S(2)}, u32[]{:S(2)}) collective-permute-start(bf16[1,656,128]{2,1,0:T(8,128)(2,1)S(1)} %get-tuple-element.78), channel_id=1, source_target_pairs={{0,8},{4,12},{8,16},{12,20},{16,24},{20,28},{24,0},{28,4},{1,9},{5... | collective-permute-start | bytes 503816 | tf_op jit(solution)/shard_map/ppermute | solution.py:442
  62.7 25.9 %collective-permute-start.12 = (bf16[1,656,128]{2,1,0:T(8,128)(2,1)S(1)}, bf16[1,656,128]{2,1,0:T(8,128)(2,1)S(1)}, u32[]{:S(2)}, u32[]{:S(2)}) collective-permute-start(bf16[1,656,128]{2,1,0:T(8,128)(2,1)S(1)} %get-tuple-element.79), channel_id=1, source_target_pairs={{0,12},{4,16},{8,20},{12,24},{16,28},{20,0},{24,4},{28,8},{1,13},{... | collective-permute-start | bytes 503816 | tf_op jit(solution)/shard_map/ppermute | solution.py:442
  65.4 26.1 %collective-permute-start.13 = (bf16[1,656,128]{2,1,0:T(8,128)(2,1)S(1)}, bf16[1,656,128]{2,1,0:T(8,128)(2,1)S(1)}, u32[]{:S(2)}, u32[]{:S(2)}) collective-permute-start(bf16[1,656,128]{2,1,0:T(8,128)(2,1)S(1)} %get-tuple-element.80), channel_id=1, source_target_pairs={{0,16},{4,20},{8,24},{12,28},{16,0},{20,4},{24,8},{28,12},{1,17},{... | collective-permute-start | bytes 503816 | tf_op jit(solution)/shard_map/ppermute | solution.py:442
  67.0 24.5 %collective-permute-start.14 = (bf16[1,656,128]{2,1,0:T(8,128)(2,1)S(1)}, bf16[1,656,128]{2,1,0:T(8,128)(2,1)S(1)}, u32[]{:S(2)}, u32[]{:S(2)}) collective-permute-start(bf16[1,656,128]{2,1,0:T(8,128)(2,1)S(1)} %get-tuple-element.81), channel_id=1, source_target_pairs={{0,20},{4,24},{8,28},{12,0},{16,4},{20,8},{24,12},{28,16},{1,21},{... | collective-permute-start | bytes 503816 | tf_op jit(solution)/shard_map/ppermute | solution.py:442
  68.6 24.3 %collective-permute-start.15 = (bf16[1,656,128]{2,1,0:T(8,128)(2,1)S(1)}, bf16[1,656,128]{2,1,0:T(8,128)(2,1)S(1)}, u32[]{:S(2)}, u32[]{:S(2)}) collective-permute-start(bf16[1,656,128]{2,1,0:T(8,128)(2,1)S(1)} %get-tuple-element.82), channel_id=1, source_target_pairs={{0,24},{4,28},{8,0},{12,4},{16,8},{20,12},{24,16},{28,20},{1,25},{... | collective-permute-start | bytes 503816 | tf_op jit(solution)/shard_map/ppermute | solution.py:442
  84.9 9.1 %collective-permute-start.16 = (bf16[1,656,128]{2,1,0:T(8,128)(2,1)S(1)}, bf16[1,656,128]{2,1,0:T(8,128)(2,1)S(1)}, u32[]{:S(2)}, u32[]{:S(2)}) collective-permute-start(bf16[1,656,128]{2,1,0:T(8,128)(2,1)S(1)} %get-tuple-element.83), channel_id=1, source_target_pairs={{0,28},{4,0},{8,4},{12,8},{16,12},{20,16},{24,20},{28,24},{1,29},{... | collective-permute-start | bytes 503816 | tf_op jit(solution)/shard_map/ppermute | solution.py:442
  94.0 5.4 %copy-start.7 = (bf16[1024,640]{1,0:T(8,128)(2,1)S(1)}, bf16[1024,640]{1,0:T(8,128)(2,1)}, u32[]{:S(2)}) copy-start(bf16[1024,640]{1,0:T(8,128)(2,1)} %constant.2.clone.map_ref.refs_10_) | copy-start | bytes 3932164
  96.6 2.8 %copy-start.1 = (f32[8,1024,64]{1,2,0:T(8,128)S(1)}, f32[8,1024,64]{1,2,0:T(8,128)}, u32[]{:S(2)}) copy-start(f32[8,1024,64]{1,2,0:T(8,128)} %param.19) | copy-start | bytes 6291460
  96.6 2.8 %copy-start.12 = (f32[8,1024]{1,0:T(8,128)S(1)}, f32[8,1024]{1,0:T(8,128)}, u32[]{:S(2)}) copy-start(f32[8,1024]{1,0:T(8,128)} %refs_9_.3) | copy-start | bytes 98308
  96.7 2.0 %collective-permute-start.17 = (bf16[2,256,512]{2,1,0:T(8,128)(2,1)S(1)}, bf16[2,256,512]{2,1,0:T(8,128)(2,1)S(1)}, u32[]{:S(2)}, u32[]{:S(2)}) collective-permute-start(bf16[2,256,512]{2,1,0:T(8,128)(2,1)S(1)} %slice.13), channel_id=1, source_target_pairs={{0,1},{1,0},{2,3},{3,2},{4,5},{5,4},{6,7},{7,6},{8,9},{9,8},{10,11... | collective-permute-start | bytes 1572872 | tf_op jit(solution)/shard_map/ppermute | solution.py:425
  98.8 8.4 %collective-permute-start.18 = (bf16[1,256,512]{2,1,0:T(8,128)(2,1)S(1)}, bf16[1,256,512]{2,1,0:T(8,128)(2,1)S(1)}, u32[]{:S(2)}, u32[]{:S(2)}) collective-permute-start(bf16[1,256,512]{2,1,0:T(8,128)(2,1)S(1)} %slice.17), channel_id=1, source_target_pairs={{0,2},{1,3},{2,0},{3,1},{4,6},{5,7},{6,4},{7,5},{8,10},{9,11},{10,... | collective-permute-start | bytes 786440 | tf_op jit(solution)/shard_map/ppermute | solution.py:425
  (2 other events, 1.5 us)

commit v4 on v3

--- a/solution.py
+++ b/solution.py
@@ -14,6 +14,7 @@
 LANES = 128
 VMEM = pltpu.VMEM
 MIB = 1024 * 1024
+GROUP = 4
 
 NN = (((1,), (0,)), ((), ()))
 NT = (((1,), (1,)), ((), ()))
@@ -144,6 +145,17 @@
             o_ref[m, half:] = jnp.broadcast_to(
                 rows_ref[which, pl.ds(lax.axis_index("local") * mine + m, 1), :], (LANES - half, o_ref.shape[2])
             )
+
+
+def load_kernel(count, *refs):
+    sources, targets, done_ref = refs[:count], refs[count:-1], refs[-1]
+    copies = [
+        pltpu.make_async_copy(source, target, done_ref.at[i]) for i, (source, target) in enumerate(zip(sources, targets))
+    ]
+    for copy in copies:
+        copy.start()
+    for copy in copies:
+        copy.wait()
 
 
 def project_kernel(hd, local, count, *refs):
@@ -217,21 +229,26 @@
     return jnp.concatenate([state, norm], axis=0)
 
 
+def whole_state(packed, hd, sk):
+    both = unpack_window(packed, hd, sk).astype(F32)
+    return jnp.concatenate([both[:hd]] + [both[hd:]] * ((LANES - hd) // 16), axis=0)
+
+
 def key_kernel(sk, hd, local, *refs):
     slots = refs[:local]
-    base_ref, wb_ref, qkv_ref, state_ref, feat_ref, kdot_ref, total_ref = refs[local:]
+    wb_ref, qkv_ref, state_ref, feat_ref, kdot_ref, total_ref = refs[local:]
     blocks, mine, packed, _ = qkv_ref.shape
     for s, slot in enumerate(slots):
         qkv_ref[came_in(lax.axis_index("local"), s, blocks)] = slot[...]
     rows = packed // 2
-    width = base_ref.shape[2]
+    width = state_ref.shape[3]
     tiles = width // LANES
     weights = lane_weights(sk, width)
     lane = lane_of(rows)
     for m in range(mine):
-        state = base_ref[m]
+        state = jnp.zeros((LANES, width), F32)
         for c in range(blocks):
-            state_ref[m, c] = state.astype(BF16)
+            state_ref[m, c] = state
             vk = qkv_ref[c, m, :rows]
             e0, e1, d0, d1 = sketched(vk, wb_ref[...])
             e, d = e0 * e1, d0 * d1
@@ -243,11 +260,11 @@
             ).astype(BF16)
             ones = jnp.where(lane < hd, vk.astype(F32), 1.0).astype(BF16)
             state = state + mm(ones, feat, TN) * weights
-        total_ref[m] = state
+        total_ref[m] = pack_window(state, hd, sk)
 
 
 def query_kernel(
-    sk, hd, qkv_ref, kdot_ref, state_ref, wb_ref, ba_ref, bb_ref,
+    sk, hd, carry_ref, base_ref, qkv_ref, kdot_ref, state_ref, wb_ref, ba_ref, bb_ref,
     dq_ref, qdot_ref, dn_ref, cot_ref, total_ref,
 ):
     blocks, mine, packed, _ = qkv_ref.shape
@@ -265,6 +282,7 @@
     adder = jnp.where((r_i < hd) & (c_i >= hd), -1.0 / (LANES - hd), 0.0).astype(BF16)
     for m in range(mine):
         total = jnp.zeros((LANES, width), F32)
+        base = base_ref[m] if carry_ref is None else base_ref[m] + whole_state(carry_ref[m], hd, sk)
         for c in range(blocks):
             gq = qkv_ref[c, m, rows:]
             e0, e1, d0, d1 = sketched(gq, wb_ref[...])
@@ -278,7 +296,7 @@
             ).astype(BF16)
             qdot_ref[m, c] = qdot
             kdot = kdot_ref[m, c]
-            state = state_ref[m, c]
+            state = (base + state_ref[m, c]).astype(BF16)
             ones = jnp.where(low, qkv_ref[c, m, :rows].astype(F32), 1.0).astype(BF16)
             dots = jnp.where(causal, mm(qdot, kdot, NT), 0.0)
             num = mm(feat, state, NT) + mm((dots * dots).astype(BF16), ones)
@@ -311,10 +329,18 @@
 
 
 def reverse_kernel(
-    sk, hd, window_ref, qkv_ref, dq_ref, feat_ref, kdot_ref, qdot_ref, dn_ref, cot_ref, base_ref, wb_ref, bb_ref, *refs
+    sk, hd, others, window_ref, qkv_ref, dq_ref, feat_ref, kdot_ref, qdot_ref, dn_ref, cot_ref, base_ref, wb_ref, bb_ref, *refs
 ):
-    out_refs = refs[:-1]
+    other_refs = refs[:others]
+    out_refs = refs[others:-1]
     blocks_ref = refs[-1]
+    window, later = window_ref[...].astype(F32), None
+    for d, other_ref in enumerate(other_refs, 1):
+        other = other_ref[...].astype(F32)
+        window = window + other
+        other = jnp.where(lax.axis_index("group") < d, other, 0.0)
+        later = other if later is None else later + other
+    window = window.astype(BF16)
     mine, blocks, rows, _ = dn_ref.shape
     packed = rows + rows // 2
     width = base_ref.shape[2]
@@ -327,6 +353,8 @@
     )
     for m in range(mine):
         state = base_ref[m]
+        if later is not None:
+            state = state + whole_state(later[m].astype(BF16), hd, sk) * weights
         for c in reversed(range(blocks)):
             after = state.astype(BF16)
             vk = qkv_ref[c, m, :rows]
@@ -357,7 +385,7 @@
             state = state + cot_ref[m, c] * weights
     for s, out_ref in enumerate(out_refs):
         out_ref[:, :packed] = blocks_ref[s]
-        out_ref[:, packed:] = window_ref[...]
+        out_ref[:, packed:] = window
 
 
 def input_kernel(hd, local, order, *refs):
@@ -454,6 +482,36 @@
 
     state_t = prefix_state.transpose(0, 2, 1)
     dstate_t = d_state_end.transpose(0, 2, 1)
+    loads = (w_value, w_key, w_query, d_attn, inputs)
+    loaded = call(
+        partial(load_kernel, len(loads)),
+        "load",
+        [(x.shape, x.dtype) for x in loads],
+        [],
+        loads,
+        mib=48,
+        scratch=[pltpu.SemaphoreType.DMA((len(loads),))],
+    )
+    far, loaded = lax.optimization_barrier((far, list(loaded)))
+    pieces.update(far)
+    distance = ranks // 4
+    while distance:
+        pieces.update({at ^ distance: hop(x, "head", distance) for at, x in list(pieces.items())})
+        distance //= 2
+    keys = list(range(ranks))
+
+    block = ((mine, 2 * rows, LANES), BF16)
+    all_blocks = pltpu.VMEM((local,) + block[0], BF16)
+    back_blocks = pltpu.VMEM((local, mine, packed, LANES), BF16)
+    slots = call(
+        partial(project_kernel, hd, local, len(keys)),
+        "project",
+        [block] * local,
+        [loaded[4]] + [pieces[at] for at in keys[1:]] + loaded[:4],
+        scratch=[all_blocks],
+    )
+    sketch, first = lax.optimization_barrier((sketch, slots[0]))
+    slots = exchange([first, *slots[1:]])
     base, base_after, wb, ba, bb = call(
         partial(prepare_kernel, sk),
         "prepare",
@@ -467,73 +525,45 @@
             pltpu.SemaphoreType.DMA((2,)),
         ],
     )
-    far, base, base_after, wb, ba, bb = lax.optimization_barrier((far, base, base_after, wb, ba, bb))
-    pieces.update(far)
-    distance = ranks // 4
-    while distance:
-        pieces.update({at ^ distance: hop(x, "head", distance) for at, x in list(pieces.items())})
-        distance //= 2
-    keys = range(ranks)
-
-    block = ((mine, 2 * rows, LANES), BF16)
-    all_blocks = pltpu.VMEM((local,) + block[0], BF16)
-    back_blocks = pltpu.VMEM((local, mine, packed, LANES), BF16)
-    slots = call(
-        partial(project_kernel, hd, local, len(keys)),
-        "project",
-        [block] * local,
-        [pieces[at] for at in keys] + [w_value, w_key, w_query, d_attn],
-        scratch=[all_blocks],
-    )
-    slots = exchange(slots)
-
-    def key_side(start_state):
-        return call(
-            partial(key_kernel, sk, hd, local),
-            "key_side",
-            [
-                ((local, mine, 2 * rows, LANES), BF16),
-                ((mine, local, LANES, lanes), BF16),
-                ((mine, local, rows, lanes), BF16),
-                ((mine, local, rows, LANES), BF16),
-                ((mine, LANES, lanes), F32),
-            ],
-            [*slots, start_state, wb],
-        )
-
-    def of_groups(x, wanted):
-        everything = lax.all_gather(x.astype(BF16), "group").astype(F32)
-        chosen = wanted(jnp.arange(groups))
-        return jnp.where(chosen.reshape((groups,) + (1,) * x.ndim), everything, 0.0).sum(0)
-
-    if groups > 1:
-        sums = key_side(jnp.zeros_like(base))[4]
-        base = base + of_groups(sums, lambda at: at < group)
-    qkv, states, key_feats, kdot, _ = key_side(base)
-
+
+    small = ((mine, window_rows(hd, sk), LANES), BF16)
+    qkv, states, key_feats, kdot, total = call(
+        partial(key_kernel, sk, hd, local),
+        "key_side",
+        [
+            ((local, mine, 2 * rows, LANES), BF16),
+            ((mine, local, LANES, lanes), F32),
+            ((mine, local, rows, lanes), BF16),
+            ((mine, local, rows, LANES), BF16),
+            small,
+        ],
+        [*slots, wb],
+    )
+
+    carry = []
+    for d in range(1, groups):
+        carry.append(lax.ppermute(total, "group", [(i, i + d) for i in range(groups - d)]))
+    carry = carry[:1] if len(carry) < 2 else [sum(x.astype(F32) for x in carry).astype(BF16)]
+    side = partial(query_kernel, sk, hd) if carry else partial(query_kernel, sk, hd, None)
     dq, qdot, dn, cots, window = call(
-        partial(query_kernel, sk, hd),
+        side,
         "query_side",
         [
             ((mine, local, half, LANES), BF16),
             ((mine, local, rows, LANES), BF16),
             ((mine, local, rows, LANES), BF16),
             ((mine, local, LANES, lanes), F32),
-            ((mine, window_rows(hd, sk), LANES), BF16),
+            small,
         ],
-        [qkv, kdot, states, wb, ba, bb],
-    )
-    if groups > 1:
-        later = of_groups(cots.sum(1), lambda at: at > group)
-        base_after = base_after + later * lane_weights(sk, lanes)
-
-    if groups > 1:
-        window = lax.psum(window, "group")
+        [*carry, base, qkv, kdot, states, wb, ba, bb],
+    )
+
+    others = [lax.ppermute(window, "group", [(i, (i + d) % groups) for i in range(groups)]) for d in range(1, groups)]
     gradients = call(
-        partial(reverse_kernel, sk, hd),
+        partial(reverse_kernel, sk, hd, len(others)),
         "key_gradients",
         [((mine, packed + window_rows(hd, sk), LANES), BF16)] * local,
-        [window, qkv, dq, key_feats, kdot, qdot, dn, cots, base_after, wb, bb],
+        [window, qkv, dq, key_feats, kdot, qdot, dn, cots, base_after, wb, bb, *others],
         scratch=[back_blocks],
     )
     gradients = exchange(gradients)
@@ -570,6 +600,7 @@
     def run(*args):
         heads = args[5].shape[0] // head
         local = math.gcd(heads, seq)
+        local = min(local & -local, GROUP)
         groups = seq // local
         inner = Mesh(mesh.devices.reshape(groups, local, head), ("group", "local", "head"))
         tokens = ("group", "local")

time: 108 us -> 96.2 us (0.89)
  the two profiles are of different devices: /device:TPU:12 before, /device:TPU:0 now
where the time goes in v4:
time: 96.2 us; the launch traced here: 95.7 us
  Pallas kernels  32.1 us (33%)
  waiting for transfers between devices  32.1 us (33%)
  starting transfers between devices  26.1 us (27%)
  local copies, waits for them, and re-layouts  3.68 us (4%)
    pallas_call x8, Pallas kernels, call(): pl.pallas_call(kernel, in_specs=[vmem] * len(arrays) + [pl.BlockSpec(memo...  32.1 us
    ppermute x6, waiting for transfers between devices, send(): lax.ppermute(x, 'local', [(i, (i + shift) % local) for i in range(local)])  18.3 us
    ppermute x6, starting transfers between devices, send(): lax.ppermute(x, 'local', [(i, (i + shift) % local) for i in range(local)])  13 us
    ppermute x5, waiting for transfers between devices, hop(): return lax.ppermute(x, axis, [(i, i ^ distance) for i in range(count)])  7.85 us
    ppermute x5, starting transfers between devices, hop(): return lax.ppermute(x, axis, [(i, i ^ distance) for i in range(count)])  4.88 us
    ppermute x1, starting transfers between devices, body(): lax.ppermute(total, 'group', [(i, i + d) for i in range(groups - d)])  4.76 us
    unnamed x24, local copies, waits for them, and re-layouts  3.62 us
    ppermute x1, starting transfers between devices, body(): lax.ppermute(window, 'group', [(i, (i + d) % groups) for i in range(group...  3.51 us
  transfers between devices with their start and end apart: 13, of which 12 were waited for; matrix products, arithmetic and copies ran while one was open for 0% of the time, Pallas kernels for 10%

profile of v4, /device:TPU:0, one launch (start us, length us, event | category | flops | bytes accessed | tf_op | source)
XLA Modules:
  0.0 95.7 jit_solution(18375349321291194189)
XLA Ops:
  0.6 3.0 %collective-permute-start = (bf16[256,512]{1,0:T(8,128)(2,1)}, bf16[256,512]{1,0:T(8,128)(2,1)S(1)}, u32[]{:S(2)}, u32[]{:S(2)}) collective-permute-start(bf16[256,512]{1,0:T(8,128)(2,1)} %refs_4_.2), channel_id=1, source_target_pairs={{0,2},{1,3},{2,0},{3,1},{4,6},{5,7},{6,4},{7,5},{8,10},{9,11},{10,... | collective-permute-start | bytes 786440 | tf_op jit(solution)/shard_map/ppermute | solution.py:453
  3.6 0.9 copy-done.7
  4.6 0.9 copy-done.8
  5.5 4.2 %load.1 = (bf16[2048,512]{1,0:T(8,128)(2,1)S(1)}, bf16[2048,512]{1,0:T(8,128)(2,1)S(1)}, bf16[2048,512]{1,0:T(8,128)(2,1)}, bf16[256,512]{1,0:T(8,128)(2,1)S(1)}, bf16[256,512]{1,0:T(8,128)(2,1)S(1)}) custom-call(bf16[2048,512]{1,0:T(8,128)(2,1)} %refs_6_.2, bf16[2048,512]{1,0:T(8,128)(2,1)} %refs_5_.2, bf16[2048,512]{1,0:T(8,128)(2,1)} %refs_4_.3, ...), custom_call_target="tpu_custom_call" | custom-call | tf_op jit(solution)/shard_map/load/pallas_call | solution.py:440
  10.4 1.3 %collective-permute-done.2.refs_3_ = bf16[256,512]{1,0:T(8,128)(2,1)S(1)} collective-permute-done((bf16[256,512]{1,0:T(8,128)(2,1)S(1)}, bf16[256,512]{1,0:T(8,128)(2,1)S(1)}, u32[]{:S(2)}, u32[]{:S(2)}) %collective-permute-start.2) | collective-permute-done | bytes 262176 | tf_op jit(solution)/shard_map/ppermute | solution.py:453
  11.7 1.7 %copy-done.6 = bf16[2048,512]{1,0:T(8,128)(2,1)S(1)} copy-done((bf16[2048,512]{1,0:T(8,128)(2,1)S(1)}, bf16[2048,512]{1,0:T(8,128)(2,1)}, u32[]{:S(2)}) %copy-start.6) | copy-done | bytes 2097176
  13.4 2.2 %project.1 = (bf16[2,512,128]{2,1,0:T(8,128)(2,1)S(1)}, bf16[2,512,128]{2,1,0:T(8,128)(2,1)S(1)}, bf16[2,512,128]{2,1,0:T(8,128)(2,1)S(1)}, bf16[2,512,128]{2,1,0:T(8,128)(2,1)S(1)}) custom-call(bf16[256,512]{1,0:T(8,128)(2,1)S(1)} %get-tuple-element.53.refs_0_, bf16[256,512]{1,0:T(8,128)(2,1)S(1)} %collective-permute-done.1.refs_1_, ...), custom_call_target="tpu_custom_call" | custom-call | tf_op jit(solution)/shard_map/project/pallas_call | solution.py:440
  15.6 1.8 %collective-permute-start.3 = (bf16[2,512,128]{2,1,0:T(8,128)(2,1)S(1)}, bf16[2,512,128]{2,1,0:T(8,128)(2,1)S(1)}, u32[]{:S(2)}, u32[]{:S(2)}) collective-permute-start(bf16[2,512,128]{2,1,0:T(8,128)(2,1)S(1)} %get-tuple-element.61), channel_id=1, source_target_pairs={{0,4},{4,8},{8,12},{12,0},{1,5},{5,9},{9,13},{13,1},{2,6},{6,10},{... | collective-permute-start | bytes 786440 | tf_op jit(solution)/shard_map/ppermute | solution.py:470
  17.4 1.6 %collective-permute-start.4 = (bf16[2,512,128]{2,1,0:T(8,128)(2,1)S(1)}, bf16[2,512,128]{2,1,0:T(8,128)(2,1)S(1)}, u32[]{:S(2)}, u32[]{:S(2)}) collective-permute-start(bf16[2,512,128]{2,1,0:T(8,128)(2,1)S(1)} %get-tuple-element.62), channel_id=1, source_target_pairs={{0,8},{4,12},{8,0},{12,4},{1,9},{5,13},{9,1},{13,5},{2,10},{6,14},... | collective-permute-start | bytes 786440 | tf_op jit(solution)/shard_map/ppermute | solution.py:470
  19.0 1.4 %collective-permute-start.5 = (bf16[2,512,128]{2,1,0:T(8,128)(2,1)S(1)}, bf16[2,512,128]{2,1,0:T(8,128)(2,1)S(1)}, u32[]{:S(2)}, u32[]{:S(2)}) collective-permute-start(bf16[2,512,128]{2,1,0:T(8,128)(2,1)S(1)} %get-tuple-element.63), channel_id=1, source_target_pairs={{0,12},{4,0},{8,4},{12,8},{1,13},{5,1},{9,5},{13,9},{2,14},{6,2},{... | collective-permute-start | bytes 786440 | tf_op jit(solution)/shard_map/ppermute | solution.py:470
  20.4 3.0 %prepare.1 = (f32[2,128,640]{2,1,0:T(8,128)S(1)}, f32[2,128,640]{2,1,0:T(8,128)S(1)}, bf16[256,512]{1,0:T(8,128)(2,1)S(1)}, bf16[512,128]{1,0:T(8,128)(2,1)S(1)}, bf16[512,128]{1,0:T(8,128)(2,1)S(1)}) custom-call(f32[2,32,64]{2,1,0:T(8,128)S(1)} %bitcast.9, f32[8,1024]{1,0:T(8,128)S(1)} %copy-done.11, f32[8,1024]{1,0:T(8,128)S(1)} %copy-done.9, ...), custom_call_target="tpu_custom_call" | custom-call | tf_op jit(solution)/shard_map/prepare/pallas_call | solution.py:440
  23.4 2.3 %collective-permute-done.3.refs_1_ = bf16[2,512,128]{2,1,0:T(8,128)(2,1)S(1)} collective-permute-done((bf16[2,512,128]{2,1,0:T(8,128)(2,1)S(1)}, bf16[2,512,128]{2,1,0:T(8,128)(2,1)S(1)}, u32[]{:S(2)}, u32[]{:S(2)}) %collective-permute-start.3) | collective-permute-done | bytes 262176 | tf_op jit(solution)/shard_map/ppermute | solution.py:470
  25.7 0.9 collective-permute-done.4.refs_2_
  26.6 4.0 %collective-permute-done.5.refs_3_ = bf16[2,512,128]{2,1,0:T(8,128)(2,1)S(1)} collective-permute-done((bf16[2,512,128]{2,1,0:T(8,128)(2,1)S(1)}, bf16[2,512,128]{2,1,0:T(8,128)(2,1)S(1)}, u32[]{:S(2)}, u32[]{:S(2)}) %collective-permute-start.5) | collective-permute-done | bytes 262176 | tf_op jit(solution)/shard_map/ppermute | solution.py:470
  30.5 3.0 %key_side.1 = (bf16[4,2,512,128]{3,2,1,0:T(8,128)(2,1)S(1)}, f32[2,4,128,640]{3,2,1,0:T(8,128)S(1)}, bf16[2,4,256,640]{3,2,1,0:T(8,128)(2,1)S(1)}, bf16[2,4,256,...) custom-call(bf16[2,512,128]{2,1,0:T(8,128)(2,1)S(1)} %get-tuple-element.60.refs_0_, ...), custom_call_target="tpu_custom_call" | custom-call | tf_op jit(solution)/shard_map/key_side/pallas_call | solution.py:440
  33.6 4.8 %collective-permute-start.6 = (bf16[2,272,128]{2,1,0:T(8,128)(2,1)S(1)}, bf16[2,272,128]{2,1,0:T(8,128)(2,1)S(1)}, u32[]{:S(2)}, u32[]{:S(2)}) collective-permute-start(bf16[2,272,128]{2,1,0:T(8,128)(2,1)S(1)} %get-tuple-element.66), channel_id=1, source_target_pairs={{0,16},{1,17},{2,18},{3,19},{4,20},{5,21},{6,22},{7,23},{8,24},{9,... | collective-permute-start | bytes 417800 | tf_op jit(solution)/shard_map/ppermute | solution.py:545
  38.3 2.9 %collective-permute-done.6.carry_ref = bf16[2,272,128]{2,1,0:T(8,128)(2,1)S(1)} collective-permute-done((bf16[2,272,128]{2,1,0:T(8,128)(2,1)S(1)}, bf16[2,272,128]{2,1,0:T(8,128)(2,1)S(1)}, u32[]{:S(2)}, u32[]{:S(2)}) %collective-permute-start.6) | collective-permute-done | bytes 139296 | tf_op jit(solution)/shard_map/ppermute | solution.py:545
  41.3 8.5 %query_side.1 = (bf16[2,4,128,128]{3,2,1,0:T(8,128)(2,1)S(1)}, bf16[2,4,256,128]{3,2,1,0:T(8,128)(2,1)S(1)}, bf16[2,4,256,128]{3,2,1,0:T(8,128)(2,1)S(1)}, f32[2...) custom-call(bf16[2,272,128]{2,1,0:T(8,128)(2,1)S(1)} %collective-permute-done.6.carry_ref, ...), custom_call_target="tpu_custom_call" | custom-call | tf_op jit(solution)/shard_map/query_side/pallas_call | solution.py:440
  49.8 3.5 %collective-permute-start.7 = (bf16[2,272,128]{2,1,0:T(8,128)(2,1)S(1)}, bf16[2,272,128]{2,1,0:T(8,128)(2,1)S(1)}, u32[]{:S(2)}, u32[]{:S(2)}) collective-permute-start(bf16[2,272,128]{2,1,0:T(8,128)(2,1)S(1)} %get-tuple-element.73.window_ref), channel_id=1, source_target_pairs={{0,16},{16,0},{1,17},{17,1},{2,18},{18,2},{3,19},{19,3},{4,20},{20... | collective-permute-start | bytes 417800 | tf_op jit(solution)/shard_map/ppermute | solution.py:561
  53.3 3.0 %collective-permute-done.7.refs_0_ = bf16[2,272,128]{2,1,0:T(8,128)(2,1)S(1)} collective-permute-done((bf16[2,272,128]{2,1,0:T(8,128)(2,1)S(1)}, bf16[2,272,128]{2,1,0:T(8,128)(2,1)S(1)}, u32[]{:S(2)}, u32[]{:S(2)}) %collective-permute-start.7) | collective-permute-done | bytes 139296 | tf_op jit(solution)/shard_map/ppermute | solution.py:561
  56.4 6.1 %key_gradients.1 = (bf16[2,656,128]{2,1,0:T(8,128)(2,1)S(1)}, bf16[2,656,128]{2,1,0:T(8,128)(2,1)S(1)}, bf16[2,656,128]{2,1,0:T(8,128)(2,1)S(1)}, bf16[2,656,128]{2,1,0:T(8,128)(2,1)S(1)}) custom-call(bf16[2,272,128]{2,1,0:T(8,128)(2,1)S(1)} %get-tuple-element.73.window_ref, bf16[4,2,512,128]{3,2,1,0:T(8,128)(2,1)S(1)} %get-tuple-element.68.qkv_ref, ...), custom_call_target="tpu_custom_call" | custom-call | tf_op jit(solution)/shard_map/key_gradients/pallas_call | solution.py:440
  62.4 1.3 %collective-permute-start.8 = (bf16[2,656,128]{2,1,0:T(8,128)(2,1)S(1)}, bf16[2,656,128]{2,1,0:T(8,128)(2,1)S(1)}, u32[]{:S(2)}, u32[]{:S(2)}) collective-permute-start(bf16[2,656,128]{2,1,0:T(8,128)(2,1)S(1)} %get-tuple-element.81), channel_id=1, source_target_pairs={{0,4},{4,8},{8,12},{12,0},{1,5},{5,9},{9,13},{13,1},{2,6},{6,10},{... | collective-permute-start | bytes 1007624 | tf_op jit(solution)/shard_map/ppermute | solution.py:470
  63.7 4.0 %collective-permute-start.9 = (bf16[2,656,128]{2,1,0:T(8,128)(2,1)S(1)}, bf16[2,656,128]{2,1,0:T(8,128)(2,1)S(1)}, u32[]{:S(2)}, u32[]{:S(2)}) collective-permute-start(bf16[2,656,128]{2,1,0:T(8,128)(2,1)S(1)} %get-tuple-element.82), channel_id=1, source_target_pairs={{0,8},{4,12},{8,0},{12,4},{1,9},{5,13},{9,1},{13,5},{2,10},{6,14},... | collective-permute-start | bytes 1007624 | tf_op jit(solution)/shard_map/ppermute | solution.py:470
  67.7 2.8 %collective-permute-start.10 = (bf16[2,656,128]{2,1,0:T(8,128)(2,1)S(1)}, bf16[2,656,128]{2,1,0:T(8,128)(2,1)S(1)}, u32[]{:S(2)}, u32[]{:S(2)}) collective-permute-start(bf16[2,656,128]{2,1,0:T(8,128)(2,1)S(1)} %get-tuple-element.83), channel_id=1, source_target_pairs={{0,12},{4,0},{8,4},{12,8},{1,13},{5,1},{9,5},{13,9},{2,14},{6,2},{... | collective-permute-start | bytes 1007624 | tf_op jit(solution)/shard_map/ppermute | solution.py:470
  70.6 5.4 %collective-permute-done.8.refs_1_ = bf16[2,656,128]{2,1,0:T(8,128)(2,1)S(1)} collective-permute-done((bf16[2,656,128]{2,1,0:T(8,128)(2,1)S(1)}, bf16[2,656,128]{2,1,0:T(8,128)(2,1)S(1)}, u32[]{:S(2)}, u32[]{:S(2)}) %collective-permute-start.8) | collective-permute-done | bytes 335904 | tf_op jit(solution)/shard_map/ppermute | solution.py:470
  76.5 5.2 %collective-permute-done.10.refs_3_ = bf16[2,656,128]{2,1,0:T(8,128)(2,1)S(1)} collective-permute-done((bf16[2,656,128]{2,1,0:T(8,128)(2,1)S(1)}, bf16[2,656,128]{2,1,0:T(8,128)(2,1)S(1)}, u32[]{:S(2)}, u32[]{:S(2)}) %collective-permute-start.10) | collective-permute-done | bytes 335904 | tf_op jit(solution)/shard_map/ppermute | solution.py:470
  81.7 2.6 %input_gradient.1 = (bf16[256,512]{1,0:T(8,128)(2,1)}, bf16[256,512]{1,0:T(8,128)(2,1)}, bf16[256,512]{1,0:T(8,128)(2,1)}, bf16[4,256,512]{2,1,0:T(8,128)(2,1)S(1)}) custom-call(bf16[2,656,128]{2,1,0:T(8,128)(2,1)S(1)} %get-tuple-element.80.refs_0_, bf16[2,656,128]{2,1,0:T(8,128)(2,1)S(1)} %collective-permute-done.8.refs_1_, ...), custom_call_target="tpu_custom_call" | custom-call | tf_op jit(solution)/shard_map/input_gradient/pallas_call | solution.py:440
  84.4 1.9 %collective-permute-done.11 = bf16[2,256,512]{2,1,0:T(8,128)(2,1)S(1)} collective-permute-done((bf16[2,256,512]{2,1,0:T(8,128)(2,1)S(1)}, bf16[2,256,512]{2,1,0:T(8,128)(2,1)S(1)}, u32[]{:S(2)}, u32[]{:S(2)}) %collective-permute-start.11) | collective-permute-done | bytes 524320 | tf_op jit(solution)/shard_map/ppermute | solution.py:453
  86.5 1.6 %collective-permute-start.12 = (bf16[1,256,512]{2,1,0:T(8,128)(2,1)S(1)}, bf16[1,256,512]{2,1,0:T(8,128)(2,1)S(1)}, u32[]{:S(2)}, u32[]{:S(2)}) collective-permute-start(bf16[1,256,512]{2,1,0:T(8,128)(2,1)S(1)} %slice.17), channel_id=1, source_target_pairs={{0,2},{1,3},{2,0},{3,1},{4,6},{5,7},{6,4},{7,5},{8,10},{9,11},{10,... | collective-permute-start | bytes 786440 | tf_op jit(solution)/shard_map/ppermute | solution.py:453
  88.1 2.6 %prefix_gradients.1 = (f32[8,64,1024]{2,1,0:T(8,128)}, f32[8,1024]{1,0:T(8,128)}) custom-call(bf16[2,656,128]{2,1,0:T(8,128)(2,1)S(1)} %get-tuple-element.80.refs_0_, bf16[2,656,128]{2,1,0:T(8,128)(2,1)S(1)} %collective-permute-done.8.refs_1_, bf16[2,656,128]{2,1,0:T(8,128)(2,1)S(1)} %collective-permute-done.9.refs_2_, ...), custom_call_target="tpu_custom_call" | custom-call | tf_op jit(solution)/shard_map/prefix_gradients/pallas_call | solution.py:440
  90.6 4.3 %collective-permute-done.12 = bf16[1,256,512]{2,1,0:T(8,128)(2,1)S(1)} collective-permute-done((bf16[1,256,512]{2,1,0:T(8,128)(2,1)S(1)}, bf16[1,256,512]{2,1,0:T(8,128)(2,1)S(1)}, u32[]{:S(2)}, u32[]{:S(2)}) %collective-permute-start.12) | collective-permute-done | bytes 262176 | tf_op jit(solution)/shard_map/ppermute | solution.py:453
  94.9 0.8 fusion
  (30 shorter events, 1.4 us)
Async XLA Ops:
  0.6 9.5 %collective-permute-start = (bf16[256,512]{1,0:T(8,128)(2,1)}, bf16[256,512]{1,0:T(8,128)(2,1)S(1)}, u32[]{:S(2)}, u32[]{:S(2)}) collective-permute-start(bf16[256,512]{1,0:T(8,128)(2,1)} %refs_4_.2), channel_id=1, source_target_pairs={{0,2},{1,3},{2,0},{3,1},{4,6},{5,7},{6,4},{7,5},{8,10},{9,11},{10,... | collective-permute-start | bytes 786440 | tf_op jit(solution)/shard_map/ppermute | solution.py:453
  3.6 6.8 %collective-permute-start.1 = (bf16[256,512]{1,0:T(8,128)(2,1)}, bf16[256,512]{1,0:T(8,128)(2,1)S(1)}, u32[]{:S(2)}, u32[]{:S(2)}) collective-permute-start(bf16[256,512]{1,0:T(8,128)(2,1)} %refs_4_.2), channel_id=1, source_target_pairs={{0,1},{1,0},{2,3},{3,2},{4,5},{5,4},{6,7},{7,6},{8,9},{9,8},{10,11... | collective-permute-start | bytes 786440 | tf_op jit(solution)/shard_map/ppermute | solution.py:453
  3.6 1.0 copy-start.7
  4.6 0.9 copy-start.8
  10.2 10.2 %copy-start = (f32[8,1024,64]{1,2,0:T(8,128)S(1)}, f32[8,1024,64]{1,2,0:T(8,128)}, u32[]{:S(2)}) copy-start(f32[8,1024,64]{1,2,0:T(8,128)} %param.19) | copy-start | bytes 6291460
  10.2 10.2 %copy-start.4 = (bf16[1024,640]{1,0:T(8,128)(2,1)S(1)}, bf16[1024,640]{1,0:T(8,128)(2,1)}, u32[]{:S(2)}) copy-start(bf16[1024,640]{1,0:T(8,128)(2,1)} %constant.2.clone.map_ref.refs_6_) | copy-start | bytes 3932164
  10.2 10.2 %copy-start.5 = (f32[8,1024,64]{1,2,0:T(8,128)S(1)}, f32[8,1024,64]{1,2,0:T(8,128)}, u32[]{:S(2)}) copy-start(f32[8,1024,64]{1,2,0:T(8,128)} %param.16) | copy-start | bytes 6291460
  10.2 1.5 %collective-permute-start.2 = (bf16[256,512]{1,0:T(8,128)(2,1)S(1)}, bf16[256,512]{1,0:T(8,128)(2,1)S(1)}, u32[]{:S(2)}, u32[]{:S(2)}) collective-permute-start(bf16[256,512]{1,0:T(8,128)(2,1)S(1)} %collective-permute-done.refs_2_), channel_id=1, source_target_pairs={{0,1},{1,0},{2,3},{3,2},{4,5},{5,4},{6,7},{7,6},{8,9},{9,8},{10,11... | collective-permute-start | bytes 786440 | tf_op jit(solution)/shard_map/ppermute | solution.py:453
  11.7 1.7 %copy-start.6 = (bf16[2048,512]{1,0:T(8,128)(2,1)S(1)}, bf16[2048,512]{1,0:T(8,128)(2,1)}, u32[]{:S(2)}) copy-start(bf16[2048,512]{1,0:T(8,128)(2,1)} %get-tuple-element.57.refs_6_) | copy-start | bytes 6291460
  13.4 7.0 %copy-start.9 = (f32[8,1024]{1,0:T(8,128)S(1)}, f32[8,1024]{1,0:T(8,128)}, u32[]{:S(2)}) copy-start(f32[8,1024]{1,0:T(8,128)} %refs_5_.3) | copy-start | bytes 98308
  13.4 7.0 %copy-start.10 = (f32[2,64,32]{1,2,0:T(8,128)S(1)}, f32[2,64,32]{1,2,0:T(8,128)}, u32[]{:S(2)}) copy-start(f32[2,64,32]{1,2,0:T(8,128)} %param.15) | copy-start | bytes 49156
  13.4 7.0 %copy-start.11 = (f32[8,1024]{1,0:T(8,128)S(1)}, f32[8,1024]{1,0:T(8,128)}, u32[]{:S(2)}) copy-start(f32[8,1024]{1,0:T(8,128)} %norm_ref.1) | copy-start | bytes 98308
  15.6 10.1 %collective-permute-start.3 = (bf16[2,512,128]{2,1,0:T(8,128)(2,1)S(1)}, bf16[2,512,128]{2,1,0:T(8,128)(2,1)S(1)}, u32[]{:S(2)}, u32[]{:S(2)}) collective-permute-start(bf16[2,512,128]{2,1,0:T(8,128)(2,1)S(1)} %get-tuple-element.61), channel_id=1, source_target_pairs={{0,4},{4,8},{8,12},{12,0},{1,5},{5,9},{9,13},{13,1},{2,6},{6,10},{... | collective-permute-start | bytes 786440 | tf_op jit(solution)/shard_map/ppermute | solution.py:470
  17.4 9.2 %collective-permute-start.4 = (bf16[2,512,128]{2,1,0:T(8,128)(2,1)S(1)}, bf16[2,512,128]{2,1,0:T(8,128)(2,1)S(1)}, u32[]{:S(2)}, u32[]{:S(2)}) collective-permute-start(bf16[2,512,128]{2,1,0:T(8,128)(2,1)S(1)} %get-tuple-element.62), channel_id=1, source_target_pairs={{0,8},{4,12},{8,0},{12,4},{1,9},{5,13},{9,1},{13,5},{2,10},{6,14},... | collective-permute-start | bytes 786440 | tf_op jit(solution)/shard_map/ppermute | solution.py:470
  19.0 11.6 %collective-permute-start.5 = (bf16[2,512,128]{2,1,0:T(8,128)(2,1)S(1)}, bf16[2,512,128]{2,1,0:T(8,128)(2,1)S(1)}, u32[]{:S(2)}, u32[]{:S(2)}) collective-permute-start(bf16[2,512,128]{2,1,0:T(8,128)(2,1)S(1)} %get-tuple-element.63), channel_id=1, source_target_pairs={{0,12},{4,0},{8,4},{12,8},{1,13},{5,1},{9,5},{13,9},{2,14},{6,2},{... | collective-permute-start | bytes 786440 | tf_op jit(solution)/shard_map/ppermute | solution.py:470
  33.6 7.7 %collective-permute-start.6 = (bf16[2,272,128]{2,1,0:T(8,128)(2,1)S(1)}, bf16[2,272,128]{2,1,0:T(8,128)(2,1)S(1)}, u32[]{:S(2)}, u32[]{:S(2)}) collective-permute-start(bf16[2,272,128]{2,1,0:T(8,128)(2,1)S(1)} %get-tuple-element.66), channel_id=1, source_target_pairs={{0,16},{1,17},{2,18},{3,19},{4,20},{5,21},{6,22},{7,23},{8,24},{9,... | collective-permute-start | bytes 417800 | tf_op jit(solution)/shard_map/ppermute | solution.py:545
  49.8 6.5 %collective-permute-start.7 = (bf16[2,272,128]{2,1,0:T(8,128)(2,1)S(1)}, bf16[2,272,128]{2,1,0:T(8,128)(2,1)S(1)}, u32[]{:S(2)}, u32[]{:S(2)}) collective-permute-start(bf16[2,272,128]{2,1,0:T(8,128)(2,1)S(1)} %get-tuple-element.73.window_ref), channel_id=1, source_target_pairs={{0,16},{16,0},{1,17},{17,1},{2,18},{18,2},{3,19},{19,3},{4,20},{20... | collective-permute-start | bytes 417800 | tf_op jit(solution)/shard_map/ppermute | solution.py:561
  56.3 25.4 %copy-start.1 = (bf16[2048,512]{1,0:T(8,128)(2,1)S(1)}, bf16[2048,512]{1,0:T(8,128)(2,1)}, u32[]{:S(2)}) copy-start(bf16[2048,512]{1,0:T(8,128)(2,1)} %refs_6_.2) | copy-start | bytes 6291460
  56.3 25.4 %copy-start.2 = (bf16[2048,512]{1,0:T(8,128)(2,1)S(1)}, bf16[2048,512]{1,0:T(8,128)(2,1)}, u32[]{:S(2)}) copy-start(bf16[2048,512]{1,0:T(8,128)(2,1)} %refs_5_.2) | copy-start | bytes 6291460
  56.3 25.4 %copy-start.3 = (bf16[2048,512]{1,0:T(8,128)(2,1)S(1)}, bf16[2048,512]{1,0:T(8,128)(2,1)}, u32[]{:S(2)}) copy-start(bf16[2048,512]{1,0:T(8,128)(2,1)} %refs_4_.3) | copy-start | bytes 6291460
  62.4 13.6 %collective-permute-start.8 = (bf16[2,656,128]{2,1,0:T(8,128)(2,1)S(1)}, bf16[2,656,128]{2,1,0:T(8,128)(2,1)S(1)}, u32[]{:S(2)}, u32[]{:S(2)}) collective-permute-start(bf16[2,656,128]{2,1,0:T(8,128)(2,1)S(1)} %get-tuple-element.81), channel_id=1, source_target_pairs={{0,4},{4,8},{8,12},{12,0},{1,5},{5,9},{9,13},{13,1},{2,6},{6,10},{... | collective-permute-start | bytes 1007624 | tf_op jit(solution)/shard_map/ppermute | solution.py:470
  63.7 12.8 %collective-permute-start.9 = (bf16[2,656,128]{2,1,0:T(8,128)(2,1)S(1)}, bf16[2,656,128]{2,1,0:T(8,128)(2,1)S(1)}, u32[]{:S(2)}, u32[]{:S(2)}) collective-permute-start(bf16[2,656,128]{2,1,0:T(8,128)(2,1)S(1)} %get-tuple-element.82), channel_id=1, source_target_pairs={{0,8},{4,12},{8,0},{12,4},{1,9},{5,13},{9,1},{13,5},{2,10},{6,14},... | collective-permute-start | bytes 1007624 | tf_op jit(solution)/shard_map/ppermute | solution.py:470
  67.7 14.0 %collective-permute-start.10 = (bf16[2,656,128]{2,1,0:T(8,128)(2,1)S(1)}, bf16[2,656,128]{2,1,0:T(8,128)(2,1)S(1)}, u32[]{:S(2)}, u32[]{:S(2)}) collective-permute-start(bf16[2,656,128]{2,1,0:T(8,128)(2,1)S(1)} %get-tuple-element.83), channel_id=1, source_target_pairs={{0,12},{4,0},{8,4},{12,8},{1,13},{5,1},{9,5},{13,9},{2,14},{6,2},{... | collective-permute-start | bytes 1007624 | tf_op jit(solution)/shard_map/ppermute | solution.py:470
  84.4 2.0 %collective-permute-start.11 = (bf16[2,256,512]{2,1,0:T(8,128)(2,1)S(1)}, bf16[2,256,512]{2,1,0:T(8,128)(2,1)S(1)}, u32[]{:S(2)}, u32[]{:S(2)}) collective-permute-start(bf16[2,256,512]{2,1,0:T(8,128)(2,1)S(1)} %slice.13), channel_id=1, source_target_pairs={{0,1},{1,0},{2,3},{3,2},{4,5},{5,4},{6,7},{7,6},{8,9},{9,8},{10,11... | collective-permute-start | bytes 1572872 | tf_op jit(solution)/shard_map/ppermute | solution.py:453
  86.5 8.4 %collective-permute-start.12 = (bf16[1,256,512]{2,1,0:T(8,128)(2,1)S(1)}, bf16[1,256,512]{2,1,0:T(8,128)(2,1)S(1)}, u32[]{:S(2)}, u32[]{:S(2)}) collective-permute-start(bf16[1,256,512]{2,1,0:T(8,128)(2,1)S(1)} %slice.17), channel_id=1, source_target_pairs={{0,2},{1,3},{2,0},{3,1},{4,6},{5,7},{6,4},{7,5},{8,10},{9,11},{10,... | collective-permute-start | bytes 786440 | tf_op jit(solution)/shard_map/ppermute | solution.py:453

commit v5 on v4

--- a/solution.py
+++ b/solution.py
@@ -332,15 +332,15 @@
     sk, hd, others, window_ref, qkv_ref, dq_ref, feat_ref, kdot_ref, qdot_ref, dn_ref, cot_ref, base_ref, wb_ref, bb_ref, *refs
 ):
     other_refs = refs[:others]
-    out_refs = refs[others:-1]
-    blocks_ref = refs[-1]
+    out_refs = refs[others:-2]
+    sum_ref, blocks_ref = refs[-2:]
     window, later = window_ref[...].astype(F32), None
     for d, other_ref in enumerate(other_refs, 1):
         other = other_ref[...].astype(F32)
         window = window + other
         other = jnp.where(lax.axis_index("group") < d, other, 0.0)
         later = other if later is None else later + other
-    window = window.astype(BF16)
+    sum_ref[...] = window.astype(BF16)
     mine, blocks, rows, _ = dn_ref.shape
     packed = rows + rows // 2
     width = base_ref.shape[2]
@@ -384,18 +384,16 @@
             blocks_ref[slot, m, rows:] = dq_ref[m, c]
             state = state + cot_ref[m, c] * weights
     for s, out_ref in enumerate(out_refs):
-        out_ref[:, :packed] = blocks_ref[s]
-        out_ref[:, packed:] = window
+        out_ref[...] = blocks_ref[s]
 
 
 def input_kernel(hd, local, order, *refs):
     slots = refs[:local]
     weights = refs[local : local + 3]
-    dq_ref, dk_ref, dv_ref, out_ref, all_ref = refs[local + 3 :]
-    depth = dk_ref.shape[1]
+    dq_ref, dk_ref, dv_ref, out_ref, again_ref, all_ref = refs[local + 3 :]
     _, mine, packed, _ = all_ref.shape
     for s, slot in enumerate(slots):
-        all_ref[came_in(lax.axis_index("local"), s, local)] = slot[:, :packed]
+        all_ref[came_in(lax.axis_index("local"), s, local)] = slot[...]
     rows = packed * 2 // 3
     half = rows // 2
     low = lane_of(rows) < hd
@@ -411,13 +409,24 @@
         a, b = a[rows:], b[rows:]
         dq_ref[:half, cols] = jnp.where(low[:half], a, pltpu.roll(b, hd, 1)).astype(BF16)
         dq_ref[half:, cols] = jnp.where(low[:half], pltpu.roll(a, hd, 1), b).astype(BF16)
-    dq, dk, dv = dq_ref[...], dk_ref[...], dv_ref[...]
+    for k, ref in enumerate((dq_ref, dk_ref, dv_ref)):
+        again_ref[k] = ref[...]
+    head_terms(order, again_ref, weights, out_ref)
+
+
+def head_terms(order, gradients, weights, out_ref):
+    depth = gradients.shape[2]
+    dq, dk, dv = (gradients[k] for k in range(3))
     for i in range(out_ref.shape[0]):
         total = None
         for w, x in zip(weights, (dq, dk, dv)):
             part = mm(x, w[pl.ds(pl.multiple_of(lax.bitwise_xor(lax.axis_index("head"), order[i]) * depth, depth), depth), :], NT)
             total = part if total is None else total + part
         out_ref[i] = total.astype(BF16)
+
+
+def rest_kernel(order, *refs):
+    head_terms(order, refs[0], refs[1:4], refs[4])
 
 
 def expand_kernel(hd, sk, local, *refs):
@@ -489,7 +498,7 @@
         [(x.shape, x.dtype) for x in loads],
         [],
         loads,
-        mib=48,
+        mib=8,
         scratch=[pltpu.SemaphoreType.DMA((len(loads),))],
     )
     far, loaded = lax.optimization_barrier((far, list(loaded)))
@@ -559,24 +568,35 @@
     )
 
     others = [lax.ppermute(window, "group", [(i, (i + d) % groups) for i in range(groups)]) for d in range(1, groups)]
-    gradients = call(
+    *gradients, window = call(
         partial(reverse_kernel, sk, hd, len(others)),
         "key_gradients",
-        [((mine, packed + window_rows(hd, sk), LANES), BF16)] * local,
+        [((mine, packed, LANES), BF16)] * local + [small],
         [window, qkv, dq, key_feats, kdot, qdot, dn, cots, base_after, wb, bb, *others],
         scratch=[back_blocks],
     )
     gradients = exchange(gradients)
 
+    window, gradients = lax.optimization_barrier((window, gradients))
+    spread = exchange([window] * local)
+
     order = sorted(range(ranks), key=lambda at: [-(at >> bit & 1) for bit in range(ranks.bit_length() - 1)])
-    d_query, d_key, d_value, sums = call(
-        partial(input_kernel, hd, local, order),
+    d_query, d_key, d_value, sums, again = call(
+        partial(input_kernel, hd, local, order[: ranks // 2]),
         "input_gradient",
-        [((rows, width), BF16)] * 3 + [((ranks, rows, depth), BF16)],
+        [((rows, width), BF16)] * 3 + [((ranks // 2, rows, depth), BF16), ((3, rows, width), BF16)],
         [*gradients, w_query, w_key, w_value],
         scratch=[back_blocks],
     )
-    distance = 1
+    came = hop(sums, "head", 1)
+    (sums,) = call(
+        partial(rest_kernel, order[ranks // 2 :]),
+        "input_gradient_rest",
+        [((ranks // 2, rows, depth), BF16)],
+        [again, w_query, w_key, w_value],
+    )
+    sums = (sums.astype(F32) + came.astype(F32)).astype(BF16)
+    distance = 2
     while distance < ranks:
         count = sums.shape[0] // 2
         came = hop(sums[:count], "head", distance)
@@ -587,7 +607,7 @@
         partial(expand_kernel, hd, sk, local),
         "prefix_gradients",
         [((heads, hd, feat), F32), ((heads, feat), F32)],
-        [*gradients, dstate_t, d_norm_end, table],
+        [*spread, dstate_t, d_norm_end, table],
         scratch=[pltpu.VMEM((heads, hd + 16, lanes), BF16)],
     )
     d_prefix_state = state_out.transpose(0, 2, 1)

time: 96.2 us -> 94.7 us (0.984)
  waiting for transfers between devices: 32.1 us -> 27.5 us
  starting transfers between devices: 26.1 us -> 29.7 us
  Pallas kernels: 32.1 us -> 28.8 us
  local copies, waits for them, and re-layouts: 3.68 us -> 6.74 us
    ppermute x5, waiting for transfers between devices: 7.85 us -> 2.06 us  [hop(): return lax.ppermute(x, axis, [(i, i ^ distance) for i in range(count)])]
    ppermute x6 -> x9, starting transfers between devices: 13 us -> 17.8 us  [send(): lax.ppermute(x, 'local', [(i, (i + shift) % local) for i in range(local)])]
    pallas_call x8 -> x9, Pallas kernels: 32.1 us -> 28.8 us  [call(): pl.pallas_call(kernel, in_specs=[vmem] * len(arrays) + [pl.BlockSpec(memo...]
    unnamed x24 -> x28, local copies, waits for them, and re-layouts: 3.62 us -> 6.72 us
    ppermute x5, starting transfers between devices: 4.88 us -> 3.65 us  [hop(): return lax.ppermute(x, axis, [(i, i ^ distance) for i in range(count)])]
    ppermute x6 -> x9, waiting for transfers between devices: 18.3 us -> 19.4 us  [send(): lax.ppermute(x, 'local', [(i, (i + shift) % local) for i in range(local)])]
  transfers between devices with their start and end apart: 13 -> 16, of which waited for: 12 -> 13; matrix products, arithmetic and copies ran while one was open for 0% -> 0% of each run, Pallas kernels for 10% -> 7%
where the time goes in v5:
time: 94.7 us; the launch traced here: 94.4 us
  starting transfers between devices  29.7 us (31%)
  Pallas kernels  28.8 us (30%)
  waiting for transfers between devices  27.5 us (29%)
  local copies, waits for them, and re-layouts  6.74 us (7%)
    pallas_call x9, Pallas kernels, call(): pl.pallas_call(kernel, in_specs=[vmem] * len(arrays) + [pl.BlockSpec(memo...  28.8 us
    ppermute x9, waiting for transfers between devices, send(): lax.ppermute(x, 'local', [(i, (i + shift) % local) for i in range(local)])  19.4 us
    ppermute x9, starting transfers between devices, send(): lax.ppermute(x, 'local', [(i, (i + shift) % local) for i in range(local)])  17.8 us
    unnamed x28, local copies, waits for them, and re-layouts  6.72 us
    ppermute x1, starting transfers between devices, body(): lax.ppermute(total, 'group', [(i, i + d) for i in range(groups - d)])  4.68 us
    ppermute x5, starting transfers between devices, hop(): return lax.ppermute(x, axis, [(i, i ^ distance) for i in range(count)])  3.65 us
    ppermute x1, starting transfers between devices, body(): lax.ppermute(window, 'group', [(i, (i + d) % groups) for i in range(group...  3.5 us
    ppermute x1, waiting for transfers between devices, body(): lax.ppermute(window, 'group', [(i, (i + d) % groups) for i in range(group...  3.04 us
  transfers between devices with their start and end apart: 16, of which 13 were waited for; matrix products, arithmetic and copies ran while one was open for 0% of the time, Pallas kernels for 7%

profile of v5, /device:TPU:0, one launch (start us, length us, event | category | flops | bytes accessed | tf_op | source)
XLA Modules:
  0.0 94.4 jit_solution(16245917943931894287)
XLA Ops:
  0.6 3.0 %collective-permute-start = (bf16[256,512]{1,0:T(8,128)(2,1)}, bf16[256,512]{1,0:T(8,128)(2,1)S(1)}, u32[]{:S(2)}, u32[]{:S(2)}) collective-permute-start(bf16[256,512]{1,0:T(8,128)(2,1)} %refs_4_.2), channel_id=1, source_target_pairs={{0,2},{1,3},{2,0},{3,1},{4,6},{5,7},{6,4},{7,5},{8,10},{9,11},{10,... | collective-permute-start | bytes 786440 | tf_op jit(solution)/shard_map/ppermute | solution.py:462
  3.6 1.6 %copy-done = bf16[2048,512]{1,0:T(8,128)(2,1)S(1)} copy-done((bf16[2048,512]{1,0:T(8,128)(2,1)S(1)}, bf16[2048,512]{1,0:T(8,128)(2,1)}, u32[]{:S(2)}) %copy-start) | copy-done | bytes 2097176
  5.2 1.6 %copy-done.2 = bf16[2048,512]{1,0:T(8,128)(2,1)S(1)} copy-done((bf16[2048,512]{1,0:T(8,128)(2,1)S(1)}, bf16[2048,512]{1,0:T(8,128)(2,1)}, u32[]{:S(2)}) %copy-start.2) | copy-done | bytes 2097176
  6.8 1.6 %copy-done.4 = bf16[2048,512]{1,0:T(8,128)(2,1)S(1)} copy-done((bf16[2048,512]{1,0:T(8,128)(2,1)S(1)}, bf16[2048,512]{1,0:T(8,128)(2,1)}, u32[]{:S(2)}) %copy-start.4) | copy-done | bytes 2097176
  11.5 1.2 %collective-permute-done.2.refs_3_ = bf16[256,512]{1,0:T(8,128)(2,1)S(1)} collective-permute-done((bf16[256,512]{1,0:T(8,128)(2,1)S(1)}, bf16[256,512]{1,0:T(8,128)(2,1)S(1)}, u32[]{:S(2)}, u32[]{:S(2)}) %collective-permute-start.2) | collective-permute-done | bytes 262176 | tf_op jit(solution)/shard_map/ppermute | solution.py:462
  12.6 2.2 %project.1 = (bf16[2,512,128]{2,1,0:T(8,128)(2,1)S(1)}, bf16[2,512,128]{2,1,0:T(8,128)(2,1)S(1)}, bf16[2,512,128]{2,1,0:T(8,128)(2,1)S(1)}, bf16[2,512,128]{2,1,0:T(8,128)(2,1)S(1)}) custom-call(bf16[256,512]{1,0:T(8,128)(2,1)S(1)} %get-tuple-element.60.refs_0_, bf16[256,512]{1,0:T(8,128)(2,1)S(1)} %collective-permute-done.1.refs_1_, ...), custom_call_target="tpu_custom_call" | custom-call | tf_op jit(solution)/shard_map/project/pallas_call | solution.py:449
  14.8 1.6 %collective-permute-start.3 = (bf16[2,512,128]{2,1,0:T(8,128)(2,1)S(1)}, bf16[2,512,128]{2,1,0:T(8,128)(2,1)S(1)}, u32[]{:S(2)}, u32[]{:S(2)}) collective-permute-start(bf16[2,512,128]{2,1,0:T(8,128)(2,1)S(1)} %get-tuple-element.68), channel_id=1, source_target_pairs={{0,4},{4,8},{8,12},{12,0},{1,5},{5,9},{9,13},{13,1},{2,6},{6,10},{... | collective-permute-start | bytes 786440 | tf_op jit(solution)/shard_map/ppermute | solution.py:479
  16.4 1.6 %collective-permute-start.4 = (bf16[2,512,128]{2,1,0:T(8,128)(2,1)S(1)}, bf16[2,512,128]{2,1,0:T(8,128)(2,1)S(1)}, u32[]{:S(2)}, u32[]{:S(2)}) collective-permute-start(bf16[2,512,128]{2,1,0:T(8,128)(2,1)S(1)} %get-tuple-element.69), channel_id=1, source_target_pairs={{0,8},{4,12},{8,0},{12,4},{1,9},{5,13},{9,1},{13,5},{2,10},{6,14},... | collective-permute-start | bytes 786440 | tf_op jit(solution)/shard_map/ppermute | solution.py:479
  18.0 1.4 %collective-permute-start.5 = (bf16[2,512,128]{2,1,0:T(8,128)(2,1)S(1)}, bf16[2,512,128]{2,1,0:T(8,128)(2,1)S(1)}, u32[]{:S(2)}, u32[]{:S(2)}) collective-permute-start(bf16[2,512,128]{2,1,0:T(8,128)(2,1)S(1)} %get-tuple-element.70), channel_id=1, source_target_pairs={{0,12},{4,0},{8,4},{12,8},{1,13},{5,1},{9,5},{13,9},{2,14},{6,2},{... | collective-permute-start | bytes 786440 | tf_op jit(solution)/shard_map/ppermute | solution.py:479
  19.4 3.0 %prepare.1 = (f32[2,128,640]{2,1,0:T(8,128)S(1)}, f32[2,128,640]{2,1,0:T(8,128)S(1)}, bf16[256,512]{1,0:T(8,128)(2,1)S(1)}, bf16[512,128]{1,0:T(8,128)(2,1)S(1)}, bf16[512,128]{1,0:T(8,128)(2,1)S(1)}) custom-call(f32[2,32,64]{2,1,0:T(8,128)S(1)} %bitcast.9, f32[8,1024]{1,0:T(8,128)S(1)} %copy-done.13, f32[8,1024]{1,0:T(8,128)S(1)} %copy-done.11, ...), custom_call_target="tpu_custom_call" | custom-call | tf_op jit(solution)/shard_map/prepare/pallas_call | solution.py:449
  22.4 2.6 %collective-permute-done.3.refs_1_ = bf16[2,512,128]{2,1,0:T(8,128)(2,1)S(1)} collective-permute-done((bf16[2,512,128]{2,1,0:T(8,128)(2,1)S(1)}, bf16[2,512,128]{2,1,0:T(8,128)(2,1)S(1)}, u32[]{:S(2)}, u32[]{:S(2)}) %collective-permute-start.3) | collective-permute-done | bytes 262176 | tf_op jit(solution)/shard_map/ppermute | solution.py:479
  25.6 4.4 %collective-permute-done.5.refs_3_ = bf16[2,512,128]{2,1,0:T(8,128)(2,1)S(1)} collective-permute-done((bf16[2,512,128]{2,1,0:T(8,128)(2,1)S(1)}, bf16[2,512,128]{2,1,0:T(8,128)(2,1)S(1)}, u32[]{:S(2)}, u32[]{:S(2)}) %collective-permute-start.5) | collective-permute-done | bytes 262176 | tf_op jit(solution)/shard_map/ppermute | solution.py:479
  30.0 3.0 %key_side.1 = (bf16[4,2,512,128]{3,2,1,0:T(8,128)(2,1)S(1)}, f32[2,4,128,640]{3,2,1,0:T(8,128)S(1)}, bf16[2,4,256,640]{3,2,1,0:T(8,128)(2,1)S(1)}, bf16[2,4,256,...) custom-call(bf16[2,512,128]{2,1,0:T(8,128)(2,1)S(1)} %get-tuple-element.67.refs_0_, ...), custom_call_target="tpu_custom_call" | custom-call | tf_op jit(solution)/shard_map/key_side/pallas_call | solution.py:449
  33.0 4.7 %collective-permute-start.6 = (bf16[2,272,128]{2,1,0:T(8,128)(2,1)S(1)}, bf16[2,272,128]{2,1,0:T(8,128)(2,1)S(1)}, u32[]{:S(2)}, u32[]{:S(2)}) collective-permute-start(bf16[2,272,128]{2,1,0:T(8,128)(2,1)S(1)} %get-tuple-element.73), channel_id=1, source_target_pairs={{0,16},{1,17},{2,18},{3,19},{4,20},{5,21},{6,22},{7,23},{8,24},{9,... | collective-permute-start | bytes 417800 | tf_op jit(solution)/shard_map/ppermute | solution.py:554
  37.7 2.9 %collective-permute-done.6.carry_ref = bf16[2,272,128]{2,1,0:T(8,128)(2,1)S(1)} collective-permute-done((bf16[2,272,128]{2,1,0:T(8,128)(2,1)S(1)}, bf16[2,272,128]{2,1,0:T(8,128)(2,1)S(1)}, u32[]{:S(2)}, u32[]{:S(2)}) %collective-permute-start.6) | collective-permute-done | bytes 139296 | tf_op jit(solution)/shard_map/ppermute | solution.py:554
  40.6 8.5 %query_side.1 = (bf16[2,4,128,128]{3,2,1,0:T(8,128)(2,1)S(1)}, bf16[2,4,256,128]{3,2,1,0:T(8,128)(2,1)S(1)}, bf16[2,4,256,128]{3,2,1,0:T(8,128)(2,1)S(1)}, f32[2...) custom-call(bf16[2,272,128]{2,1,0:T(8,128)(2,1)S(1)} %collective-permute-done.6.carry_ref, ...), custom_call_target="tpu_custom_call" | custom-call | tf_op jit(solution)/shard_map/query_side/pallas_call | solution.py:449
  49.2 3.5 %collective-permute-start.7 = (bf16[2,272,128]{2,1,0:T(8,128)(2,1)S(1)}, bf16[2,272,128]{2,1,0:T(8,128)(2,1)S(1)}, u32[]{:S(2)}, u32[]{:S(2)}) collective-permute-start(bf16[2,272,128]{2,1,0:T(8,128)(2,1)S(1)} %get-tuple-element.80.window_ref), channel_id=1, source_target_pairs={{0,16},{16,0},{1,17},{17,1},{2,18},{18,2},{3,19},{19,3},{4,20},{20... | collective-permute-start | bytes 417800 | tf_op jit(solution)/shard_map/ppermute | solution.py:570
  52.7 3.0 %collective-permute-done.7.refs_0_ = bf16[2,272,128]{2,1,0:T(8,128)(2,1)S(1)} collective-permute-done((bf16[2,272,128]{2,1,0:T(8,128)(2,1)S(1)}, bf16[2,272,128]{2,1,0:T(8,128)(2,1)S(1)}, u32[]{:S(2)}, u32[]{:S(2)}) %collective-permute-start.7) | collective-permute-done | bytes 139296 | tf_op jit(solution)/shard_map/ppermute | solution.py:570
  55.7 6.1 %key_gradients.1 = (bf16[2,384,128]{2,1,0:T(8,128)(2,1)S(1)}, bf16[2,384,128]{2,1,0:T(8,128)(2,1)S(1)}, bf16[2,384,128]{2,1,0:T(8,128)(2,1)S(1)}, bf16[2,384,128...) custom-call(bf16[2,272,128]{2,1,0:T(8,128)(2,1)S(1)} %get-tuple-element.80.window_ref, ...), custom_call_target="tpu_custom_call" | custom-call | tf_op jit(solution)/shard_map/key_gradients/pallas_call | solution.py:449
  61.8 1.2 %collective-permute-start.8 = (bf16[2,384,128]{2,1,0:T(8,128)(2,1)S(1)}, bf16[2,384,128]{2,1,0:T(8,128)(2,1)S(1)}, u32[]{:S(2)}, u32[]{:S(2)}) collective-permute-start(bf16[2,384,128]{2,1,0:T(8,128)(2,1)S(1)} %get-tuple-element.89), channel_id=1, source_target_pairs={{0,4},{4,8},{8,12},{12,0},{1,5},{5,9},{9,13},{13,1},{2,6},{6,10},{... | collective-permute-start | bytes 589832 | tf_op jit(solution)/shard_map/ppermute | solution.py:479
  63.0 4.9 %collective-permute-start.9 = (bf16[2,384,128]{2,1,0:T(8,128)(2,1)S(1)}, bf16[2,384,128]{2,1,0:T(8,128)(2,1)S(1)}, u32[]{:S(2)}, u32[]{:S(2)}) collective-permute-start(bf16[2,384,128]{2,1,0:T(8,128)(2,1)S(1)} %get-tuple-element.90), channel_id=1, source_target_pairs={{0,8},{4,12},{8,0},{12,4},{1,9},{5,13},{9,1},{13,5},{2,10},{6,14},... | collective-permute-start | bytes 589832 | tf_op jit(solution)/shard_map/ppermute | solution.py:479
  67.9 2.0 %collective-permute-start.10 = (bf16[2,384,128]{2,1,0:T(8,128)(2,1)S(1)}, bf16[2,384,128]{2,1,0:T(8,128)(2,1)S(1)}, u32[]{:S(2)}, u32[]{:S(2)}) collective-permute-start(bf16[2,384,128]{2,1,0:T(8,128)(2,1)S(1)} %get-tuple-element.91), channel_id=1, source_target_pairs={{0,12},{4,0},{8,4},{12,8},{1,13},{5,1},{9,5},{13,9},{2,14},{6,2},{... | collective-permute-start | bytes 589832 | tf_op jit(solution)/shard_map/ppermute | solution.py:479
  69.9 3.2 %collective-permute-done.8.refs_1_ = bf16[2,384,128]{2,1,0:T(8,128)(2,1)S(1)} collective-permute-done((bf16[2,384,128]{2,1,0:T(8,128)(2,1)S(1)}, bf16[2,384,128]{2,1,0:T(8,128)(2,1)S(1)}, u32[]{:S(2)}, u32[]{:S(2)}) %collective-permute-start.8) | collective-permute-done | bytes 196640 | tf_op jit(solution)/shard_map/ppermute | solution.py:479
  73.7 2.2 %collective-permute-done.10.refs_3_ = bf16[2,384,128]{2,1,0:T(8,128)(2,1)S(1)} collective-permute-done((bf16[2,384,128]{2,1,0:T(8,128)(2,1)S(1)}, bf16[2,384,128]{2,1,0:T(8,128)(2,1)S(1)}, u32[]{:S(2)}, u32[]{:S(2)}) %collective-permute-start.10) | collective-permute-done | bytes 196640 | tf_op jit(solution)/shard_map/ppermute | solution.py:479
  76.0 1.9 %input_gradient.1 = (bf16[256,512]{1,0:T(8,128)(2,1)}, bf16[256,512]{1,0:T(8,128)(2,1)}, bf16[256,512]{1,0:T(8,128)(2,1)}, bf16[2,256,512]{2,1,0:T(8,128)(2,1)S(1)}, bf16[3,256,512]{2,1,0:T(8,128)(2,1)S(1)}) custom-call(bf16[2,384,128]{2,1,0:T(8,128)(2,1)S(1)} %get-tuple-element.92.refs_0_, bf16[2,384,128]{2,1,0:T(8,128)(2,1)S(1)} %collective-permute-done.8.refs_1_, ...), custom_call_target="tpu_custom_call" | custom-call | tf_op jit(solution)/shard_map/input_gradient/pallas_call | solution.py:449
  77.9 1.0 %input_gradient_rest.1 = bf16[2,256,512]{2,1,0:T(8,128)(2,1)S(1)} custom-call(bf16[3,256,512]{2,1,0:T(8,128)(2,1)S(1)} %get-tuple-element.96.refs_0_, bf16[2048,512]{1,0:T(8,128)(2,1)S(1)} %copy-done.5, bf16[2048,512]{1,0:T(8,128)(2,1)S(1)} %copy-done.3, bf16[2048,512]{1,0:T(8,128)(2,1)S(1)} %copy-done.1), custom_call_target="tpu_custom_call" | custom-call | tf_op jit(solution)/shard_map/input_gradient_rest/pallas_call | solution.py:449
  80.1 3.2 %collective-permute-start.15 = (bf16[2,272,128]{2,1,0:T(8,128)(2,1)S(1)}, bf16[2,272,128]{2,1,0:T(8,128)(2,1)S(1)}, u32[]{:S(2)}, u32[]{:S(2)}) collective-permute-start(bf16[2,272,128]{2,1,0:T(8,128)(2,1)S(1)} %get-tuple-element.101.refs_0_), channel_id=1, source_target_pairs={{0,12},{4,0},{8,4},{12,8},{1,13},{5,1},{9,5},{13,9},{2,14},{6,2},{... | collective-permute-start | bytes 417800 | tf_op jit(solution)/shard_map/ppermute | solution.py:479
  83.5 1.7 %collective-permute-start.13 = (bf16[2,272,128]{2,1,0:T(8,128)(2,1)S(1)}, bf16[2,272,128]{2,1,0:T(8,128)(2,1)S(1)}, u32[]{:S(2)}, u32[]{:S(2)}) collective-permute-start(bf16[2,272,128]{2,1,0:T(8,128)(2,1)S(1)} %get-tuple-element.101.refs_0_), channel_id=1, source_target_pairs={{0,4},{4,8},{8,12},{12,0},{1,5},{5,9},{9,13},{13,1},{2,6},{6,10},{... | collective-permute-start | bytes 417800 | tf_op jit(solution)/shard_map/ppermute | solution.py:479
  85.2 2.1 %collective-permute-done.15.refs_3_ = bf16[2,272,128]{2,1,0:T(8,128)(2,1)S(1)} collective-permute-done((bf16[2,272,128]{2,1,0:T(8,128)(2,1)S(1)}, bf16[2,272,128]{2,1,0:T(8,128)(2,1)S(1)}, u32[]{:S(2)}, u32[]{:S(2)}) %collective-permute-start.15) | collective-permute-done | bytes 139296 | tf_op jit(solution)/shard_map/ppermute | solution.py:479
  87.3 2.7 %collective-permute-done.14.refs_2_ = bf16[2,272,128]{2,1,0:T(8,128)(2,1)S(1)} collective-permute-done((bf16[2,272,128]{2,1,0:T(8,128)(2,1)S(1)}, bf16[2,272,128]{2,1,0:T(8,128)(2,1)S(1)}, u32[]{:S(2)}, u32[]{:S(2)}) %collective-permute-start.14) | collective-permute-done | bytes 139296 | tf_op jit(solution)/shard_map/ppermute | solution.py:479
  90.0 1.0 %collective-permute-done.13.refs_1_ = bf16[2,272,128]{2,1,0:T(8,128)(2,1)S(1)} collective-permute-done((bf16[2,272,128]{2,1,0:T(8,128)(2,1)S(1)}, bf16[2,272,128]{2,1,0:T(8,128)(2,1)S(1)}, u32[]{:S(2)}, u32[]{:S(2)}) %collective-permute-start.13) | collective-permute-done | bytes 139296 | tf_op jit(solution)/shard_map/ppermute | solution.py:479
  91.0 2.6 %prefix_gradients.1 = (f32[8,64,1024]{2,1,0:T(8,128)}, f32[8,1024]{1,0:T(8,128)}) custom-call(bf16[2,272,128]{2,1,0:T(8,128)(2,1)S(1)} %get-tuple-element.101.refs_0_, bf16[2,272,128]{2,1,0:T(8,128)(2,1)S(1)} %collective-permute-done.13.refs_1_, bf16[2,272,128]{2,1,0:T(8,128)(2,1)S(1)} %collective-permute-done.14.refs_2_, ...), custom_call_target="tpu_custom_call" | custom-call | tf_op jit(solution)/shard_map/prefix_gradients/pallas_call | solution.py:449
  (40 shorter events, 6.4 us)
Async XLA Ops:
  0.6 10.2 %collective-permute-start = (bf16[256,512]{1,0:T(8,128)(2,1)}, bf16[256,512]{1,0:T(8,128)(2,1)S(1)}, u32[]{:S(2)}, u32[]{:S(2)}) collective-permute-start(bf16[256,512]{1,0:T(8,128)(2,1)} %refs_4_.2), channel_id=1, source_target_pairs={{0,2},{1,3},{2,0},{3,1},{4,6},{5,7},{6,4},{7,5},{8,10},{9,11},{10,... | collective-permute-start | bytes 786440 | tf_op jit(solution)/shard_map/ppermute | solution.py:462
  3.6 7.9 %collective-permute-start.1 = (bf16[256,512]{1,0:T(8,128)(2,1)}, bf16[256,512]{1,0:T(8,128)(2,1)S(1)}, u32[]{:S(2)}, u32[]{:S(2)}) collective-permute-start(bf16[256,512]{1,0:T(8,128)(2,1)} %refs_4_.2), channel_id=1, source_target_pairs={{0,1},{1,0},{2,3},{3,2},{4,5},{5,4},{6,7},{7,6},{8,9},{9,8},{10,11... | collective-permute-start | bytes 786440 | tf_op jit(solution)/shard_map/ppermute | solution.py:462
  3.6 1.6 %copy-start = (bf16[2048,512]{1,0:T(8,128)(2,1)S(1)}, bf16[2048,512]{1,0:T(8,128)(2,1)}, u32[]{:S(2)}) copy-start(bf16[2048,512]{1,0:T(8,128)(2,1)} %refs_3_.3) | copy-start | bytes 6291460
  5.2 1.6 %copy-start.2 = (bf16[2048,512]{1,0:T(8,128)(2,1)S(1)}, bf16[2048,512]{1,0:T(8,128)(2,1)}, u32[]{:S(2)}) copy-start(bf16[2048,512]{1,0:T(8,128)(2,1)} %refs_2_.3) | copy-start | bytes 6291460
  6.8 1.6 %copy-start.4 = (bf16[2048,512]{1,0:T(8,128)(2,1)S(1)}, bf16[2048,512]{1,0:T(8,128)(2,1)}, u32[]{:S(2)}) copy-start(bf16[2048,512]{1,0:T(8,128)(2,1)} %refs_1_.3) | copy-start | bytes 6291460
  8.4 0.9 %copy-start.9 = (bf16[256,512]{1,0:T(8,128)(2,1)S(1)}, bf16[256,512]{1,0:T(8,128)(2,1)}, u32[]{:S(2)}) copy-start(bf16[256,512]{1,0:T(8,128)(2,1)} %refs_3_.2) | copy-start | bytes 786436
  9.4 0.9 %copy-start.10 = (bf16[256,512]{1,0:T(8,128)(2,1)S(1)}, bf16[256,512]{1,0:T(8,128)(2,1)}, u32[]{:S(2)}) copy-start(bf16[256,512]{1,0:T(8,128)(2,1)} %refs_4_.2) | copy-start | bytes 786436
  10.8 8.6 %copy-start.6 = (f32[8,1024,64]{1,2,0:T(8,128)S(1)}, f32[8,1024,64]{1,2,0:T(8,128)}, u32[]{:S(2)}) copy-start(f32[8,1024,64]{1,2,0:T(8,128)} %param.19) | copy-start | bytes 6291460
  10.9 8.6 %copy-start.7 = (bf16[1024,640]{1,0:T(8,128)(2,1)S(1)}, bf16[1024,640]{1,0:T(8,128)(2,1)}, u32[]{:S(2)}) copy-start(bf16[1024,640]{1,0:T(8,128)(2,1)} %constant.2.clone.map_ref.refs_6_) | copy-start | bytes 3932164
  10.9 8.5 %copy-start.8 = (f32[8,1024,64]{1,2,0:T(8,128)S(1)}, f32[8,1024,64]{1,2,0:T(8,128)}, u32[]{:S(2)}) copy-start(f32[8,1024,64]{1,2,0:T(8,128)} %param.16) | copy-start | bytes 6291460
  10.9 8.5 %copy-start.11 = (f32[8,1024]{1,0:T(8,128)S(1)}, f32[8,1024]{1,0:T(8,128)}, u32[]{:S(2)}) copy-start(f32[8,1024]{1,0:T(8,128)} %refs_5_.3) | copy-start | bytes 98308
  10.9 8.5 %copy-start.12 = (f32[2,64,32]{1,2,0:T(8,128)S(1)}, f32[2,64,32]{1,2,0:T(8,128)}, u32[]{:S(2)}) copy-start(f32[2,64,32]{1,2,0:T(8,128)} %param.15) | copy-start | bytes 49156
  10.9 8.5 %copy-start.13 = (f32[8,1024]{1,0:T(8,128)S(1)}, f32[8,1024]{1,0:T(8,128)}, u32[]{:S(2)}) copy-start(f32[8,1024]{1,0:T(8,128)} %norm_ref.1) | copy-start | bytes 98308
  10.9 1.7 %collective-permute-start.2 = (bf16[256,512]{1,0:T(8,128)(2,1)S(1)}, bf16[256,512]{1,0:T(8,128)(2,1)S(1)}, u32[]{:S(2)}, u32[]{:S(2)}) collective-permute-start(bf16[256,512]{1,0:T(8,128)(2,1)S(1)} %collective-permute-done.refs_2_), channel_id=1, source_target_pairs={{0,1},{1,0},{2,3},{3,2},{4,5},{5,4},{6,7},{7,6},{8,9},{9,8},{10,11... | collective-permute-start | bytes 786440 | tf_op jit(solution)/shard_map/ppermute | solution.py:462
  14.8 10.1 %collective-permute-start.3 = (bf16[2,512,128]{2,1,0:T(8,128)(2,1)S(1)}, bf16[2,512,128]{2,1,0:T(8,128)(2,1)S(1)}, u32[]{:S(2)}, u32[]{:S(2)}) collective-permute-start(bf16[2,512,128]{2,1,0:T(8,128)(2,1)S(1)} %get-tuple-element.68), channel_id=1, source_target_pairs={{0,4},{4,8},{8,12},{12,0},{1,5},{5,9},{9,13},{13,1},{2,6},{6,10},{... | collective-permute-start | bytes 786440 | tf_op jit(solution)/shard_map/ppermute | solution.py:479
  16.4 9.2 %collective-permute-start.4 = (bf16[2,512,128]{2,1,0:T(8,128)(2,1)S(1)}, bf16[2,512,128]{2,1,0:T(8,128)(2,1)S(1)}, u32[]{:S(2)}, u32[]{:S(2)}) collective-permute-start(bf16[2,512,128]{2,1,0:T(8,128)(2,1)S(1)} %get-tuple-element.69), channel_id=1, source_target_pairs={{0,8},{4,12},{8,0},{12,4},{1,9},{5,13},{9,1},{13,5},{2,10},{6,14},... | collective-permute-start | bytes 786440 | tf_op jit(solution)/shard_map/ppermute | solution.py:479
  18.0 12.0 %collective-permute-start.5 = (bf16[2,512,128]{2,1,0:T(8,128)(2,1)S(1)}, bf16[2,512,128]{2,1,0:T(8,128)(2,1)S(1)}, u32[]{:S(2)}, u32[]{:S(2)}) collective-permute-start(bf16[2,512,128]{2,1,0:T(8,128)(2,1)S(1)} %get-tuple-element.70), channel_id=1, source_target_pairs={{0,12},{4,0},{8,4},{12,8},{1,13},{5,1},{9,5},{13,9},{2,14},{6,2},{... | collective-permute-start | bytes 786440 | tf_op jit(solution)/shard_map/ppermute | solution.py:479
  33.0 7.6 %collective-permute-start.6 = (bf16[2,272,128]{2,1,0:T(8,128)(2,1)S(1)}, bf16[2,272,128]{2,1,0:T(8,128)(2,1)S(1)}, u32[]{:S(2)}, u32[]{:S(2)}) collective-permute-start(bf16[2,272,128]{2,1,0:T(8,128)(2,1)S(1)} %get-tuple-element.73), channel_id=1, source_target_pairs={{0,16},{1,17},{2,18},{3,19},{4,20},{5,21},{6,22},{7,23},{8,24},{9,... | collective-permute-start | bytes 417800 | tf_op jit(solution)/shard_map/ppermute | solution.py:554
  49.2 6.5 %collective-permute-start.7 = (bf16[2,272,128]{2,1,0:T(8,128)(2,1)S(1)}, bf16[2,272,128]{2,1,0:T(8,128)(2,1)S(1)}, u32[]{:S(2)}, u32[]{:S(2)}) collective-permute-start(bf16[2,272,128]{2,1,0:T(8,128)(2,1)S(1)} %get-tuple-element.80.window_ref), channel_id=1, source_target_pairs={{0,16},{16,0},{1,17},{17,1},{2,18},{18,2},{3,19},{19,3},{4,20},{20... | collective-permute-start | bytes 417800 | tf_op jit(solution)/shard_map/ppermute | solution.py:570
  55.7 20.3 %copy-start.1 = (bf16[2048,512]{1,0:T(8,128)(2,1)S(1)}, bf16[2048,512]{1,0:T(8,128)(2,1)}, u32[]{:S(2)}) copy-start(bf16[2048,512]{1,0:T(8,128)(2,1)} %refs_3_.3) | copy-start | bytes 6291460
  55.7 20.3 %copy-start.3 = (bf16[2048,512]{1,0:T(8,128)(2,1)S(1)}, bf16[2048,512]{1,0:T(8,128)(2,1)}, u32[]{:S(2)}) copy-start(bf16[2048,512]{1,0:T(8,128)(2,1)} %refs_2_.3) | copy-start | bytes 6291460
  55.7 20.3 %copy-start.5 = (bf16[2048,512]{1,0:T(8,128)(2,1)S(1)}, bf16[2048,512]{1,0:T(8,128)(2,1)}, u32[]{:S(2)}) copy-start(bf16[2048,512]{1,0:T(8,128)(2,1)} %refs_1_.3) | copy-start | bytes 6291460
  61.8 11.4 %collective-permute-start.8 = (bf16[2,384,128]{2,1,0:T(8,128)(2,1)S(1)}, bf16[2,384,128]{2,1,0:T(8,128)(2,1)S(1)}, u32[]{:S(2)}, u32[]{:S(2)}) collective-permute-start(bf16[2,384,128]{2,1,0:T(8,128)(2,1)S(1)} %get-tuple-element.89), channel_id=1, source_target_pairs={{0,4},{4,8},{8,12},{12,0},{1,5},{5,9},{9,13},{13,1},{2,6},{6,10},{... | collective-permute-start | bytes 589832 | tf_op jit(solution)/shard_map/ppermute | solution.py:479
  63.0 10.7 %collective-permute-start.9 = (bf16[2,384,128]{2,1,0:T(8,128)(2,1)S(1)}, bf16[2,384,128]{2,1,0:T(8,128)(2,1)S(1)}, u32[]{:S(2)}, u32[]{:S(2)}) collective-permute-start(bf16[2,384,128]{2,1,0:T(8,128)(2,1)S(1)} %get-tuple-element.90), channel_id=1, source_target_pairs={{0,8},{4,12},{8,0},{12,4},{1,9},{5,13},{9,1},{13,5},{2,10},{6,14},... | collective-permute-start | bytes 589832 | tf_op jit(solution)/shard_map/ppermute | solution.py:479
  67.9 8.0 %collective-permute-start.10 = (bf16[2,384,128]{2,1,0:T(8,128)(2,1)S(1)}, bf16[2,384,128]{2,1,0:T(8,128)(2,1)S(1)}, u32[]{:S(2)}, u32[]{:S(2)}) collective-permute-start(bf16[2,384,128]{2,1,0:T(8,128)(2,1)S(1)} %get-tuple-element.91), channel_id=1, source_target_pairs={{0,12},{4,0},{8,4},{12,8},{1,13},{5,1},{9,5},{13,9},{2,14},{6,2},{... | collective-permute-start | bytes 589832 | tf_op jit(solution)/shard_map/ppermute | solution.py:479
  77.9 1.9 %collective-permute-start.11 = (bf16[2,256,512]{2,1,0:T(8,128)(2,1)S(1)}, bf16[2,256,512]{2,1,0:T(8,128)(2,1)S(1)}, u32[]{:S(2)}, u32[]{:S(2)}) collective-permute-start(bf16[2,256,512]{2,1,0:T(8,128)(2,1)S(1)} %get-tuple-element.97), channel_id=1, source_target_pairs={{0,1},{1,0},{2,3},{3,2},{4,5},{5,4},{6,7},{7,6},{8,9},{9,8},{10,11... | collective-permute-start | bytes 1572872 | tf_op jit(solution)/shard_map/ppermute | solution.py:462
  80.0 13.6 %collective-permute-start.12 = (bf16[1,256,512]{2,1,0:T(8,128)(2,1)S(1)}, bf16[1,256,512]{2,1,0:T(8,128)(2,1)S(1)}, u32[]{:S(2)}, u32[]{:S(2)}) collective-permute-start(bf16[1,256,512]{2,1,0:T(8,128)(2,1)S(1)} %slice.9), channel_id=1, source_target_pairs={{0,2},{1,3},{2,0},{3,1},{4,6},{5,7},{6,4},{7,5},{8,10},{9,11},{10,... | collective-permute-start | bytes 786440 | tf_op jit(solution)/shard_map/ppermute | solution.py:462
  80.1 7.3 %collective-permute-start.15 = (bf16[2,272,128]{2,1,0:T(8,128)(2,1)S(1)}, bf16[2,272,128]{2,1,0:T(8,128)(2,1)S(1)}, u32[]{:S(2)}, u32[]{:S(2)}) collective-permute-start(bf16[2,272,128]{2,1,0:T(8,128)(2,1)S(1)} %get-tuple-element.101.refs_0_), channel_id=1, source_target_pairs={{0,12},{4,0},{8,4},{12,8},{1,13},{5,1},{9,5},{13,9},{2,14},{6,2},{... | collective-permute-start | bytes 417800 | tf_op jit(solution)/shard_map/ppermute | solution.py:479
  83.2 6.8 %collective-permute-start.14 = (bf16[2,272,128]{2,1,0:T(8,128)(2,1)S(1)}, bf16[2,272,128]{2,1,0:T(8,128)(2,1)S(1)}, u32[]{:S(2)}, u32[]{:S(2)}) collective-permute-start(bf16[2,272,128]{2,1,0:T(8,128)(2,1)S(1)} %get-tuple-element.101.refs_0_), channel_id=1, source_target_pairs={{0,8},{4,12},{8,0},{12,4},{1,9},{5,13},{9,1},{13,5},{2,10},{6,14},... | collective-permute-start | bytes 417800 | tf_op jit(solution)/shard_map/ppermute | solution.py:479
  83.5 7.5 %collective-permute-start.13 = (bf16[2,272,128]{2,1,0:T(8,128)(2,1)S(1)}, bf16[2,272,128]{2,1,0:T(8,128)(2,1)S(1)}, u32[]{:S(2)}, u32[]{:S(2)}) collective-permute-start(bf16[2,272,128]{2,1,0:T(8,128)(2,1)S(1)} %get-tuple-element.101.refs_0_), channel_id=1, source_target_pairs={{0,4},{4,8},{8,12},{12,0},{1,5},{5,9},{9,13},{13,1},{2,6},{6,10},{... | collective-permute-start | bytes 417800 | tf_op jit(solution)/shard_map/ppermute | solution.py:479

commit v6 on v5

--- a/solution.py
+++ b/solution.py
@@ -263,26 +263,15 @@
         total_ref[m] = pack_window(state, hd, sk)
 
 
-def query_kernel(
-    sk, hd, carry_ref, base_ref, qkv_ref, kdot_ref, state_ref, wb_ref, ba_ref, bb_ref,
-    dq_ref, qdot_ref, dn_ref, cot_ref, total_ref,
-):
+def query_first_kernel(sk, hd, qkv_ref, kdot_ref, wb_ref, qdot_ref, parts_ref, feat_ref, dots_ref, near_ref):
     blocks, mine, packed, _ = qkv_ref.shape
     rows = packed // 2
-    half = rows // 2
-    width = state_ref.shape[3]
-    tiles = width // LANES
+    tiles = tile_count(sk)
     lane = lane_of(rows)
-    low = lane < hd
     causal = lax.broadcasted_iota(jnp.int32, (rows, rows), 0) >= lax.broadcasted_iota(
         jnp.int32, (rows, rows), 1
     )
-    r_i = lax.broadcasted_iota(jnp.int32, (2 * LANES, LANES), 0) % LANES
-    c_i = lax.broadcasted_iota(jnp.int32, (2 * LANES, LANES), 1)
-    adder = jnp.where((r_i < hd) & (c_i >= hd), -1.0 / (LANES - hd), 0.0).astype(BF16)
     for m in range(mine):
-        total = jnp.zeros((LANES, width), F32)
-        base = base_ref[m] if carry_ref is None else base_ref[m] + whole_state(carry_ref[m], hd, sk)
         for c in range(blocks):
             gq = qkv_ref[c, m, rows:]
             e0, e1, d0, d1 = sketched(gq, wb_ref[...])
@@ -295,11 +284,41 @@
                 jnp.where(lane < 3 * sk, hi.astype(F32), 0.0),
             ).astype(BF16)
             qdot_ref[m, c] = qdot
+            parts_ref[m, c] = jnp.concatenate([e0, e1, d0, d1], axis=1)
+            feat_ref[m, c] = feat
+            ones = jnp.where(lane < hd, qkv_ref[c, m, :rows].astype(F32), 1.0).astype(BF16)
+            dots = jnp.where(causal, mm(qdot, kdot_ref[m, c], NT), 0.0)
+            dots_ref[m, c] = dots
+            near_ref[m, c] = mm((dots * dots).astype(BF16), ones)
+
+
+def query_kernel(
+    sk, hd, carry_ref, base_ref, qkv_ref, kdot_ref, state_ref, parts_ref, feat_ref, dots_ref, near_ref,
+    ba_ref, bb_ref, dq_ref, dn_ref, cot_ref, total_ref,
+):
+    blocks, mine, packed, _ = qkv_ref.shape
+    rows = packed // 2
+    half = rows // 2
+    width = state_ref.shape[3]
+    tiles = width // LANES
+    lane = lane_of(rows)
+    low = lane < hd
+    r_i = lax.broadcasted_iota(jnp.int32, (2 * LANES, LANES), 0) % LANES
+    c_i = lax.broadcasted_iota(jnp.int32, (2 * LANES, LANES), 1)
+    adder = jnp.where((r_i < hd) & (c_i >= hd), -1.0 / (LANES - hd), 0.0).astype(BF16)
+    for m in range(mine):
+        total = jnp.zeros((LANES, width), F32)
+        base = base_ref[m] if carry_ref is None else base_ref[m] + whole_state(carry_ref[m], hd, sk)
+        for c in range(blocks):
+            gq = qkv_ref[c, m, rows:]
+            e0, e1, d0, d1 = (parts_ref[m, c, :, LANES * i : LANES * (i + 1)] for i in range(4))
+            e, d = e0 * e1, d0 * d1
+            feat = feat_ref[m, c]
             kdot = kdot_ref[m, c]
             state = (base + state_ref[m, c]).astype(BF16)
             ones = jnp.where(low, qkv_ref[c, m, :rows].astype(F32), 1.0).astype(BF16)
-            dots = jnp.where(causal, mm(qdot, kdot, NT), 0.0)
-            num = mm(feat, state, NT) + mm((dots * dots).astype(BF16), ones)
+            dots = dots_ref[m, c]
+            num = mm(feat, state, NT) + near_ref[m, c]
             inv = 1.0 / (1.0 + num)
             inv = jnp.where(low, pltpu.roll(inv, hd, 1), inv)
             g = gq.astype(F32)
@@ -328,8 +347,27 @@
         total_ref[m] = pack_window(total, hd, sk)
 
 
+def reverse_first_kernel(sk, hd, qkv_ref, kdot_ref, qdot_ref, dn_ref, wb_ref, parts_ref, near_ref, dv_ref):
+    mine, blocks, rows, _ = dn_ref.shape
+    lane = lane_of(rows)
+    causal = lax.broadcasted_iota(jnp.int32, (rows, rows), 0) <= lax.broadcasted_iota(
+        jnp.int32, (rows, rows), 1
+    )
+    for m in range(mine):
+        for c in range(blocks):
+            vk = qkv_ref[c, m, :rows]
+            parts_ref[m, c] = jnp.concatenate(sketched(vk, wb_ref[...]), axis=1)
+            qdot = qdot_ref[m, c]
+            dn = dn_ref[m, c]
+            ones = jnp.where(lane < hd, vk.astype(F32), 1.0).astype(BF16)
+            dots = jnp.where(causal, mm(kdot_ref[m, c], qdot, NT), 0.0)
+            cot_dots = (2.0 * dots * mm(ones, dn, NT)).astype(BF16)
+            near_ref[m, c] = mm(cot_dots, qdot)
+            dv_ref[m, c] = mm((dots * dots).astype(BF16), dn)
+
+
 def reverse_kernel(
-    sk, hd, others, window_ref, qkv_ref, dq_ref, feat_ref, kdot_ref, qdot_ref, dn_ref, cot_ref, base_ref, wb_ref, bb_ref, *refs
+    sk, hd, others, window_ref, qkv_ref, dq_ref, feat_ref, dn_ref, cot_ref, base_ref, parts_ref, near_ref, dv_ref, bb_ref, *refs
 ):
     other_refs = refs[:others]
     out_refs = refs[others:-2]
@@ -348,9 +386,6 @@
     weights = lane_weights(sk, width)
     lane = lane_of(rows)
     low = lane < hd
-    causal = lax.broadcasted_iota(jnp.int32, (rows, rows), 0) <= lax.broadcasted_iota(
-        jnp.int32, (rows, rows), 1
-    )
     for m in range(mine):
         state = base_ref[m]
         if later is not None:
@@ -358,15 +393,11 @@
         for c in reversed(range(blocks)):
             after = state.astype(BF16)
             vk = qkv_ref[c, m, :rows]
-            e0, e1, d0, d1 = sketched(vk, wb_ref[...])
+            e0, e1, d0, d1 = (parts_ref[m, c, :, LANES * i : LANES * (i + 1)] for i in range(4))
             e, d = e0 * e1, d0 * d1
-            qdot = qdot_ref[m, c]
-            dn = dn_ref[m, c]
             ones = jnp.where(low, vk.astype(F32), 1.0).astype(BF16)
-            dots = jnp.where(causal, mm(kdot_ref[m, c], qdot, NT), 0.0)
-            cot_dots = (2.0 * dots * mm(ones, dn, NT)).astype(BF16)
-            near = mm(cot_dots, qdot)
-            dv = mm(feat_ref[m, c], after, NT) + mm((dots * dots).astype(BF16), dn)
+            near = near_ref[m, c]
+            dv = mm(feat_ref[m, c], after, NT) + dv_ref[m, c]
             cot = mm(ones, after)
             cot_e, cot_d = feature_pull(cot, e, d, sk, tiles)
             cot_e = cot_e + jnp.where(lane < 2 * sk, near, 0.0)
@@ -554,25 +585,44 @@
         carry.append(lax.ppermute(total, "group", [(i, i + d) for i in range(groups - d)]))
     carry = carry[:1] if len(carry) < 2 else [sum(x.astype(F32) for x in carry).astype(BF16)]
     side = partial(query_kernel, sk, hd) if carry else partial(query_kernel, sk, hd, None)
-    dq, qdot, dn, cots, window = call(
+    whole = ((mine, local, rows, LANES), F32)
+    parts = ((mine, local, rows, 4 * LANES), F32)
+    qdot, query_parts, query_feats, dots, near = call(
+        partial(query_first_kernel, sk, hd),
+        "query_first",
+        [
+            ((mine, local, rows, LANES), BF16),
+            parts,
+            ((mine, local, rows, lanes), BF16),
+            ((mine, local, rows, rows), F32),
+            whole,
+        ],
+        [qkv, kdot, wb],
+    )
+    dq, dn, cots, window = call(
         side,
         "query_side",
         [
             ((mine, local, half, LANES), BF16),
             ((mine, local, rows, LANES), BF16),
-            ((mine, local, rows, LANES), BF16),
             ((mine, local, LANES, lanes), F32),
             small,
         ],
-        [*carry, base, qkv, kdot, states, wb, ba, bb],
+        [*carry, base, qkv, kdot, states, query_parts, query_feats, dots, near, ba, bb],
     )
 
     others = [lax.ppermute(window, "group", [(i, (i + d) % groups) for i in range(groups)]) for d in range(1, groups)]
+    key_parts, key_near, dv = call(
+        partial(reverse_first_kernel, sk, hd),
+        "key_first",
+        [parts, whole, whole],
+        [qkv, kdot, qdot, dn, wb],
+    )
     *gradients, window = call(
         partial(reverse_kernel, sk, hd, len(others)),
         "key_gradients",
         [((mine, packed, LANES), BF16)] * local + [small],
-        [window, qkv, dq, key_feats, kdot, qdot, dn, cots, base_after, wb, bb, *others],
+        [window, qkv, dq, key_feats, dn, cots, base_after, key_parts, key_near, dv, bb, *others],
         scratch=[back_blocks],
     )
     gradients = exchange(gradients)

time: 94.7 us -> 92.4 us (0.976)
  waiting for transfers between devices: 27.5 us -> 23.2 us
  Pallas kernels: 28.8 us -> 30.8 us
    ppermute x1, waiting for transfers between devices: 3.04 us -> 0.62 us  [body(): lax.ppermute(window, 'group', [(i, (i + d) % groups) for i in range(group...]
    pallas_call x9 -> x11, Pallas kernels: 28.8 us -> 30.8 us  [call(): pl.pallas_call(kernel, in_specs=[vmem] * len(arrays) + [pl.BlockSpec(memo...]
    ppermute x1, waiting for transfers between devices: 2.94 us -> 1.07 us  [body(): lax.ppermute(total, 'group', [(i, i + d) for i in range(groups - d)])]
  transfers between devices with their start and end apart: 16 -> 16, of which waited for: 13 -> 13; matrix products, arithmetic and copies ran while one was open for 0% -> 0% of each run, Pallas kernels for 7% -> 12%
where the time goes in v6:
time: 92.4 us; the launch traced here: 92.1 us
  Pallas kernels  30.8 us (33%)
  starting transfers between devices  29.7 us (32%)
  waiting for transfers between devices  23.2 us (25%)
  local copies, waits for them, and re-layouts  6.74 us (7%)
    pallas_call x11, Pallas kernels, call(): pl.pallas_call(kernel, in_specs=[vmem] * len(arrays) + [pl.BlockSpec(memo...  30.8 us
    ppermute x9, waiting for transfers between devices, send(): lax.ppermute(x, 'local', [(i, (i + shift) % local) for i in range(local)])  19.4 us
    ppermute x9, starting transfers between devices, send(): lax.ppermute(x, 'local', [(i, (i + shift) % local) for i in range(local)])  17.8 us
    unnamed x28, local copies, waits for them, and re-layouts  6.72 us
    ppermute x1, starting transfers between devices, body(): lax.ppermute(total, 'group', [(i, i + d) for i in range(groups - d)])  4.68 us
    ppermute x5, starting transfers between devices, hop(): return lax.ppermute(x, axis, [(i, i ^ distance) for i in range(count)])  3.65 us
    ppermute x1, starting transfers between devices, body(): lax.ppermute(window, 'group', [(i, (i + d) % groups) for i in range(group...  3.49 us
    ppermute x5, waiting for transfers between devices, hop(): return lax.ppermute(x, axis, [(i, i ^ distance) for i in range(count)])  2.06 us
  transfers between devices with their start and end apart: 16, of which 13 were waited for; matrix products, arithmetic and copies ran while one was open for 0% of the time, Pallas kernels for 12%

profile of v6, /device:TPU:0, one launch (start us, length us, event | category | flops | bytes accessed | tf_op | source)
XLA Modules:
  0.0 92.1 jit_solution(7391889201643277607)
XLA Ops:
  0.6 3.0 %collective-permute-start = (bf16[256,512]{1,0:T(8,128)(2,1)}, bf16[256,512]{1,0:T(8,128)(2,1)S(1)}, u32[]{:S(2)}, u32[]{:S(2)}) collective-permute-start(bf16[256,512]{1,0:T(8,128)(2,1)} %refs_4_.2), channel_id=1, source_target_pairs={{0,2},{1,3},{2,0},{3,1},{4,6},{5,7},{6,4},{7,5},{8,10},{9,11},{10,... | collective-permute-start | bytes 786440 | tf_op jit(solution)/shard_map/ppermute | solution.py:493
  3.6 1.6 %copy-done = bf16[2048,512]{1,0:T(8,128)(2,1)S(1)} copy-done((bf16[2048,512]{1,0:T(8,128)(2,1)S(1)}, bf16[2048,512]{1,0:T(8,128)(2,1)}, u32[]{:S(2)}) %copy-start) | copy-done | bytes 2097176
  5.2 1.6 %copy-done.2 = bf16[2048,512]{1,0:T(8,128)(2,1)S(1)} copy-done((bf16[2048,512]{1,0:T(8,128)(2,1)S(1)}, bf16[2048,512]{1,0:T(8,128)(2,1)}, u32[]{:S(2)}) %copy-start.2) | copy-done | bytes 2097176
  6.8 1.6 %copy-done.4 = bf16[2048,512]{1,0:T(8,128)(2,1)S(1)} copy-done((bf16[2048,512]{1,0:T(8,128)(2,1)S(1)}, bf16[2048,512]{1,0:T(8,128)(2,1)}, u32[]{:S(2)}) %copy-start.4) | copy-done | bytes 2097176
  11.5 1.2 %collective-permute-done.2.refs_3_ = bf16[256,512]{1,0:T(8,128)(2,1)S(1)} collective-permute-done((bf16[256,512]{1,0:T(8,128)(2,1)S(1)}, bf16[256,512]{1,0:T(8,128)(2,1)S(1)}, u32[]{:S(2)}, u32[]{:S(2)}) %collective-permute-start.2) | collective-permute-done | bytes 262176 | tf_op jit(solution)/shard_map/ppermute | solution.py:493
  12.6 2.2 %project.1 = (bf16[2,512,128]{2,1,0:T(8,128)(2,1)S(1)}, bf16[2,512,128]{2,1,0:T(8,128)(2,1)S(1)}, bf16[2,512,128]{2,1,0:T(8,128)(2,1)S(1)}, bf16[2,512,128]{2,1,0:T(8,128)(2,1)S(1)}) custom-call(bf16[256,512]{1,0:T(8,128)(2,1)S(1)} %get-tuple-element.67.refs_0_, bf16[256,512]{1,0:T(8,128)(2,1)S(1)} %collective-permute-done.1.refs_1_, ...), custom_call_target="tpu_custom_call" | custom-call | tf_op jit(solution)/shard_map/project/pallas_call | solution.py:480
  14.8 1.6 %collective-permute-start.3 = (bf16[2,512,128]{2,1,0:T(8,128)(2,1)S(1)}, bf16[2,512,128]{2,1,0:T(8,128)(2,1)S(1)}, u32[]{:S(2)}, u32[]{:S(2)}) collective-permute-start(bf16[2,512,128]{2,1,0:T(8,128)(2,1)S(1)} %get-tuple-element.75), channel_id=1, source_target_pairs={{0,4},{4,8},{8,12},{12,0},{1,5},{5,9},{9,13},{13,1},{2,6},{6,10},{... | collective-permute-start | bytes 786440 | tf_op jit(solution)/shard_map/ppermute | solution.py:510
  16.4 1.6 %collective-permute-start.4 = (bf16[2,512,128]{2,1,0:T(8,128)(2,1)S(1)}, bf16[2,512,128]{2,1,0:T(8,128)(2,1)S(1)}, u32[]{:S(2)}, u32[]{:S(2)}) collective-permute-start(bf16[2,512,128]{2,1,0:T(8,128)(2,1)S(1)} %get-tuple-element.76), channel_id=1, source_target_pairs={{0,8},{4,12},{8,0},{12,4},{1,9},{5,13},{9,1},{13,5},{2,10},{6,14},... | collective-permute-start | bytes 786440 | tf_op jit(solution)/shard_map/ppermute | solution.py:510
  18.0 1.4 %collective-permute-start.5 = (bf16[2,512,128]{2,1,0:T(8,128)(2,1)S(1)}, bf16[2,512,128]{2,1,0:T(8,128)(2,1)S(1)}, u32[]{:S(2)}, u32[]{:S(2)}) collective-permute-start(bf16[2,512,128]{2,1,0:T(8,128)(2,1)S(1)} %get-tuple-element.77), channel_id=1, source_target_pairs={{0,12},{4,0},{8,4},{12,8},{1,13},{5,1},{9,5},{13,9},{2,14},{6,2},{... | collective-permute-start | bytes 786440 | tf_op jit(solution)/shard_map/ppermute | solution.py:510
  19.4 3.0 %prepare.1 = (f32[2,128,640]{2,1,0:T(8,128)S(1)}, f32[2,128,640]{2,1,0:T(8,128)S(1)}, bf16[256,512]{1,0:T(8,128)(2,1)S(1)}, bf16[512,128]{1,0:T(8,128)(2,1)S(1)}, bf16[512,128]{1,0:T(8,128)(2,1)S(1)}) custom-call(f32[2,32,64]{2,1,0:T(8,128)S(1)} %bitcast.9, f32[8,1024]{1,0:T(8,128)S(1)} %copy-done.13, f32[8,1024]{1,0:T(8,128)S(1)} %copy-done.11, ...), custom_call_target="tpu_custom_call" | custom-call | tf_op jit(solution)/shard_map/prepare/pallas_call | solution.py:480
  22.4 2.6 %collective-permute-done.3.refs_1_ = bf16[2,512,128]{2,1,0:T(8,128)(2,1)S(1)} collective-permute-done((bf16[2,512,128]{2,1,0:T(8,128)(2,1)S(1)}, bf16[2,512,128]{2,1,0:T(8,128)(2,1)S(1)}, u32[]{:S(2)}, u32[]{:S(2)}) %collective-permute-start.3) | collective-permute-done | bytes 262176 | tf_op jit(solution)/shard_map/ppermute | solution.py:510
  25.6 4.4 %collective-permute-done.5.refs_3_ = bf16[2,512,128]{2,1,0:T(8,128)(2,1)S(1)} collective-permute-done((bf16[2,512,128]{2,1,0:T(8,128)(2,1)S(1)}, bf16[2,512,128]{2,1,0:T(8,128)(2,1)S(1)}, u32[]{:S(2)}, u32[]{:S(2)}) %collective-permute-start.5) | collective-permute-done | bytes 262176 | tf_op jit(solution)/shard_map/ppermute | solution.py:510
  30.0 3.0 %key_side.1 = (bf16[4,2,512,128]{3,2,1,0:T(8,128)(2,1)S(1)}, f32[2,4,128,640]{3,2,1,0:T(8,128)S(1)}, bf16[2,4,256,640]{3,2,1,0:T(8,128)(2,1)S(1)}, bf16[2,4,256,...) custom-call(bf16[2,512,128]{2,1,0:T(8,128)(2,1)S(1)} %get-tuple-element.74.refs_0_, ...), custom_call_target="tpu_custom_call" | custom-call | tf_op jit(solution)/shard_map/key_side/pallas_call | solution.py:480
  33.0 4.7 %collective-permute-start.6 = (bf16[2,272,128]{2,1,0:T(8,128)(2,1)S(1)}, bf16[2,272,128]{2,1,0:T(8,128)(2,1)S(1)}, u32[]{:S(2)}, u32[]{:S(2)}) collective-permute-start(bf16[2,272,128]{2,1,0:T(8,128)(2,1)S(1)} %get-tuple-element.80), channel_id=1, source_target_pairs={{0,16},{1,17},{2,18},{3,19},{4,20},{5,21},{6,22},{7,23},{8,24},{9,... | collective-permute-start | bytes 417800 | tf_op jit(solution)/shard_map/ppermute | solution.py:585
  37.7 1.9 %query_first.1 = (bf16[2,4,256,128]{3,2,1,0:T(8,128)(2,1)S(1)}, f32[2,4,256,512]{3,2,1,0:T(8,128)S(1)}, bf16[2,4,256,640]{3,2,1,0:T(8,128)(2,1)S(1)}, f32[2,4,25...) custom-call(bf16[4,2,512,128]{3,2,1,0:T(8,128)(2,1)S(1)} %get-tuple-element.82.qkv_ref, ...), custom_call_target="tpu_custom_call" | custom-call | tf_op jit(solution)/shard_map/query_first/pallas_call | solution.py:480
  39.6 1.1 %collective-permute-done.6.carry_ref = bf16[2,272,128]{2,1,0:T(8,128)(2,1)S(1)} collective-permute-done((bf16[2,272,128]{2,1,0:T(8,128)(2,1)S(1)}, bf16[2,272,128]{2,1,0:T(8,128)(2,1)S(1)}, u32[]{:S(2)}, u32[]{:S(2)}) %collective-permute-start.6) | collective-permute-done | bytes 139296 | tf_op jit(solution)/shard_map/ppermute | solution.py:585
  40.6 7.9 %query_side.1 = (bf16[2,4,128,128]{3,2,1,0:T(8,128)(2,1)S(1)}, bf16[2,4,256,128]{3,2,1,0:T(8,128)(2,1)S(1)}, f32[2,4,128,640]{3,2,1,0:T(8,128)S(1)}, bf16[2,272,128]{2,1,0:T(8,128)(2,1)S(1)}) custom-call(bf16[2,272,128]{2,1,0:T(8,128)(2,1)S(1)} %collective-permute-done.6.carry_ref, f32[2,128,640]{2,1,0:T(8,128)S(1)} %get-tuple-element.81.base_ref, ...), custom_call_target="tpu_custom_call" | custom-call | tf_op jit(solution)/shard_map/query_side/pallas_call | solution.py:480
  48.5 3.5 %collective-permute-start.7 = (bf16[2,272,128]{2,1,0:T(8,128)(2,1)S(1)}, bf16[2,272,128]{2,1,0:T(8,128)(2,1)S(1)}, u32[]{:S(2)}, u32[]{:S(2)}) collective-permute-start(bf16[2,272,128]{2,1,0:T(8,128)(2,1)S(1)} %get-tuple-element.91.window_ref), channel_id=1, source_target_pairs={{0,16},{16,0},{1,17},{17,1},{2,18},{18,2},{3,19},{19,3},{4,20},{20... | collective-permute-start | bytes 417800 | tf_op jit(solution)/shard_map/ppermute | solution.py:614
  52.0 2.4 %key_first.1 = (f32[2,4,256,512]{3,2,1,0:T(8,128)S(1)}, f32[2,4,256,128]{3,2,1,0:T(8,128)S(1)}, f32[2,4,256,128]{3,2,1,0:T(8,128)S(1)}) custom-call(bf16[4,2,512,128]{3,2,1,0:T(8,128)(2,1)S(1)} %get-tuple-element.82.qkv_ref, bf16[2,4,256,128]{3,2,1,0:T(8,128)(2,1)S(1)} %get-tuple-element.83.kdot_ref, ...), custom_call_target="tpu_custom_call" | custom-call | tf_op jit(solution)/shard_map/key_first/pallas_call | solution.py:480
  55.1 4.5 %key_gradients.1 = (bf16[2,384,128]{2,1,0:T(8,128)(2,1)S(1)}, bf16[2,384,128]{2,1,0:T(8,128)(2,1)S(1)}, bf16[2,384,128]{2,1,0:T(8,128)(2,1)S(1)}, bf16[2,384,128...) custom-call(bf16[2,272,128]{2,1,0:T(8,128)(2,1)S(1)} %get-tuple-element.91.window_ref, ...), custom_call_target="tpu_custom_call" | custom-call | tf_op jit(solution)/shard_map/key_gradients/pallas_call | solution.py:480
  59.6 1.2 %collective-permute-start.8 = (bf16[2,384,128]{2,1,0:T(8,128)(2,1)S(1)}, bf16[2,384,128]{2,1,0:T(8,128)(2,1)S(1)}, u32[]{:S(2)}, u32[]{:S(2)}) collective-permute-start(bf16[2,384,128]{2,1,0:T(8,128)(2,1)S(1)} %get-tuple-element.103), channel_id=1, source_target_pairs={{0,4},{4,8},{8,12},{12,0},{1,5},{5,9},{9,13},{13,1},{2,6},{6,10},{... | collective-permute-start | bytes 589832 | tf_op jit(solution)/shard_map/ppermute | solution.py:510
  60.8 4.9 %collective-permute-start.9 = (bf16[2,384,128]{2,1,0:T(8,128)(2,1)S(1)}, bf16[2,384,128]{2,1,0:T(8,128)(2,1)S(1)}, u32[]{:S(2)}, u32[]{:S(2)}) collective-permute-start(bf16[2,384,128]{2,1,0:T(8,128)(2,1)S(1)} %get-tuple-element.104), channel_id=1, source_target_pairs={{0,8},{4,12},{8,0},{12,4},{1,9},{5,13},{9,1},{13,5},{2,10},{6,14},... | collective-permute-start | bytes 589832 | tf_op jit(solution)/shard_map/ppermute | solution.py:510
  65.7 2.0 %collective-permute-start.10 = (bf16[2,384,128]{2,1,0:T(8,128)(2,1)S(1)}, bf16[2,384,128]{2,1,0:T(8,128)(2,1)S(1)}, u32[]{:S(2)}, u32[]{:S(2)}) collective-permute-start(bf16[2,384,128]{2,1,0:T(8,128)(2,1)S(1)} %get-tuple-element.105), channel_id=1, source_target_pairs={{0,12},{4,0},{8,4},{12,8},{1,13},{5,1},{9,5},{13,9},{2,14},{6,2},{... | collective-permute-start | bytes 589832 | tf_op jit(solution)/shard_map/ppermute | solution.py:510
  67.7 3.2 %collective-permute-done.8.refs_1_ = bf16[2,384,128]{2,1,0:T(8,128)(2,1)S(1)} collective-permute-done((bf16[2,384,128]{2,1,0:T(8,128)(2,1)S(1)}, bf16[2,384,128]{2,1,0:T(8,128)(2,1)S(1)}, u32[]{:S(2)}, u32[]{:S(2)}) %collective-permute-start.8) | collective-permute-done | bytes 196640 | tf_op jit(solution)/shard_map/ppermute | solution.py:510
  71.5 2.2 %collective-permute-done.10.refs_3_ = bf16[2,384,128]{2,1,0:T(8,128)(2,1)S(1)} collective-permute-done((bf16[2,384,128]{2,1,0:T(8,128)(2,1)S(1)}, bf16[2,384,128]{2,1,0:T(8,128)(2,1)S(1)}, u32[]{:S(2)}, u32[]{:S(2)}) %collective-permute-start.10) | collective-permute-done | bytes 196640 | tf_op jit(solution)/shard_map/ppermute | solution.py:510
  73.7 1.9 %input_gradient.1 = (bf16[256,512]{1,0:T(8,128)(2,1)}, bf16[256,512]{1,0:T(8,128)(2,1)}, bf16[256,512]{1,0:T(8,128)(2,1)}, bf16[2,256,512]{2,1,0:T(8,128)(2,1)S(1)}, bf16[3,256,512]{2,1,0:T(8,128)(2,1)S(1)}) custom-call(bf16[2,384,128]{2,1,0:T(8,128)(2,1)S(1)} %get-tuple-element.106.refs_0_, bf16[2,384,128]{2,1,0:T(8,128)(2,1)S(1)} %collective-permute-done.8.refs_1_, ...), custom_call_target="tpu_custom_call" | custom-call | tf_op jit(solution)/shard_map/input_gradient/pallas_call | solution.py:480
  77.8 3.2 %collective-permute-start.15 = (bf16[2,272,128]{2,1,0:T(8,128)(2,1)S(1)}, bf16[2,272,128]{2,1,0:T(8,128)(2,1)S(1)}, u32[]{:S(2)}, u32[]{:S(2)}) collective-permute-start(bf16[2,272,128]{2,1,0:T(8,128)(2,1)S(1)} %get-tuple-element.115.refs_0_), channel_id=1, source_target_pairs={{0,12},{4,0},{8,4},{12,8},{1,13},{5,1},{9,5},{13,9},{2,14},{6,2},{... | collective-permute-start | bytes 417800 | tf_op jit(solution)/shard_map/ppermute | solution.py:510
  81.3 1.7 %collective-permute-start.13 = (bf16[2,272,128]{2,1,0:T(8,128)(2,1)S(1)}, bf16[2,272,128]{2,1,0:T(8,128)(2,1)S(1)}, u32[]{:S(2)}, u32[]{:S(2)}) collective-permute-start(bf16[2,272,128]{2,1,0:T(8,128)(2,1)S(1)} %get-tuple-element.115.refs_0_), channel_id=1, source_target_pairs={{0,4},{4,8},{8,12},{12,0},{1,5},{5,9},{9,13},{13,1},{2,6},{6,10},{... | collective-permute-start | bytes 417800 | tf_op jit(solution)/shard_map/ppermute | solution.py:510
  82.9 2.1 %collective-permute-done.15.refs_3_ = bf16[2,272,128]{2,1,0:T(8,128)(2,1)S(1)} collective-permute-done((bf16[2,272,128]{2,1,0:T(8,128)(2,1)S(1)}, bf16[2,272,128]{2,1,0:T(8,128)(2,1)S(1)}, u32[]{:S(2)}, u32[]{:S(2)}) %collective-permute-start.15) | collective-permute-done | bytes 139296 | tf_op jit(solution)/shard_map/ppermute | solution.py:510
  85.1 2.7 %collective-permute-done.14.refs_2_ = bf16[2,272,128]{2,1,0:T(8,128)(2,1)S(1)} collective-permute-done((bf16[2,272,128]{2,1,0:T(8,128)(2,1)S(1)}, bf16[2,272,128]{2,1,0:T(8,128)(2,1)S(1)}, u32[]{:S(2)}, u32[]{:S(2)}) %collective-permute-start.14) | collective-permute-done | bytes 139296 | tf_op jit(solution)/shard_map/ppermute | solution.py:510
  87.8 1.0 %collective-permute-done.13.refs_1_ = bf16[2,272,128]{2,1,0:T(8,128)(2,1)S(1)} collective-permute-done((bf16[2,272,128]{2,1,0:T(8,128)(2,1)S(1)}, bf16[2,272,128]{2,1,0:T(8,128)(2,1)S(1)}, u32[]{:S(2)}, u32[]{:S(2)}) %collective-permute-start.13) | collective-permute-done | bytes 139296 | tf_op jit(solution)/shard_map/ppermute | solution.py:510
  88.8 2.6 %prefix_gradients.1 = (f32[8,64,1024]{2,1,0:T(8,128)}, f32[8,1024]{1,0:T(8,128)}) custom-call(bf16[2,272,128]{2,1,0:T(8,128)(2,1)S(1)} %get-tuple-element.115.refs_0_, bf16[2,272,128]{2,1,0:T(8,128)(2,1)S(1)} %collective-permute-done.13.refs_1_, bf16[2,272,128]{2,1,0:T(8,128)(2,1)S(1)} %collective-permute-done.14.refs_2_, ...), custom_call_target="tpu_custom_call" | custom-call | tf_op jit(solution)/shard_map/prefix_gradients/pallas_call | solution.py:480
  (42 shorter events, 8.0 us)
Async XLA Ops:
  0.6 10.2 %collective-permute-start = (bf16[256,512]{1,0:T(8,128)(2,1)}, bf16[256,512]{1,0:T(8,128)(2,1)S(1)}, u32[]{:S(2)}, u32[]{:S(2)}) collective-permute-start(bf16[256,512]{1,0:T(8,128)(2,1)} %refs_4_.2), channel_id=1, source_target_pairs={{0,2},{1,3},{2,0},{3,1},{4,6},{5,7},{6,4},{7,5},{8,10},{9,11},{10,... | collective-permute-start | bytes 786440 | tf_op jit(solution)/shard_map/ppermute | solution.py:493
  3.6 7.9 %collective-permute-start.1 = (bf16[256,512]{1,0:T(8,128)(2,1)}, bf16[256,512]{1,0:T(8,128)(2,1)S(1)}, u32[]{:S(2)}, u32[]{:S(2)}) collective-permute-start(bf16[256,512]{1,0:T(8,128)(2,1)} %refs_4_.2), channel_id=1, source_target_pairs={{0,1},{1,0},{2,3},{3,2},{4,5},{5,4},{6,7},{7,6},{8,9},{9,8},{10,11... | collective-permute-start | bytes 786440 | tf_op jit(solution)/shard_map/ppermute | solution.py:493
  3.6 1.6 %copy-start = (bf16[2048,512]{1,0:T(8,128)(2,1)S(1)}, bf16[2048,512]{1,0:T(8,128)(2,1)}, u32[]{:S(2)}) copy-start(bf16[2048,512]{1,0:T(8,128)(2,1)} %refs_3_.3) | copy-start | bytes 6291460
  5.2 1.6 %copy-start.2 = (bf16[2048,512]{1,0:T(8,128)(2,1)S(1)}, bf16[2048,512]{1,0:T(8,128)(2,1)}, u32[]{:S(2)}) copy-start(bf16[2048,512]{1,0:T(8,128)(2,1)} %refs_2_.3) | copy-start | bytes 6291460
  6.8 1.6 %copy-start.4 = (bf16[2048,512]{1,0:T(8,128)(2,1)S(1)}, bf16[2048,512]{1,0:T(8,128)(2,1)}, u32[]{:S(2)}) copy-start(bf16[2048,512]{1,0:T(8,128)(2,1)} %refs_1_.3) | copy-start | bytes 6291460
  8.4 0.9 %copy-start.9 = (bf16[256,512]{1,0:T(8,128)(2,1)S(1)}, bf16[256,512]{1,0:T(8,128)(2,1)}, u32[]{:S(2)}) copy-start(bf16[256,512]{1,0:T(8,128)(2,1)} %refs_3_.2) | copy-start | bytes 786436
  9.4 0.9 %copy-start.10 = (bf16[256,512]{1,0:T(8,128)(2,1)S(1)}, bf16[256,512]{1,0:T(8,128)(2,1)}, u32[]{:S(2)}) copy-start(bf16[256,512]{1,0:T(8,128)(2,1)} %refs_4_.2) | copy-start | bytes 786436
  10.8 8.6 %copy-start.6 = (f32[8,1024,64]{1,2,0:T(8,128)S(1)}, f32[8,1024,64]{1,2,0:T(8,128)}, u32[]{:S(2)}) copy-start(f32[8,1024,64]{1,2,0:T(8,128)} %param.19) | copy-start | bytes 6291460
  10.9 8.6 %copy-start.7 = (bf16[1024,640]{1,0:T(8,128)(2,1)S(1)}, bf16[1024,640]{1,0:T(8,128)(2,1)}, u32[]{:S(2)}) copy-start(bf16[1024,640]{1,0:T(8,128)(2,1)} %constant.2.clone.map_ref.refs_6_) | copy-start | bytes 3932164
  10.9 8.5 %copy-start.8 = (f32[8,1024,64]{1,2,0:T(8,128)S(1)}, f32[8,1024,64]{1,2,0:T(8,128)}, u32[]{:S(2)}) copy-start(f32[8,1024,64]{1,2,0:T(8,128)} %param.16) | copy-start | bytes 6291460
  10.9 8.5 %copy-start.11 = (f32[8,1024]{1,0:T(8,128)S(1)}, f32[8,1024]{1,0:T(8,128)}, u32[]{:S(2)}) copy-start(f32[8,1024]{1,0:T(8,128)} %refs_5_.3) | copy-start | bytes 98308
  10.9 8.5 %copy-start.12 = (f32[2,64,32]{1,2,0:T(8,128)S(1)}, f32[2,64,32]{1,2,0:T(8,128)}, u32[]{:S(2)}) copy-start(f32[2,64,32]{1,2,0:T(8,128)} %param.15) | copy-start | bytes 49156
  10.9 8.5 %copy-start.13 = (f32[8,1024]{1,0:T(8,128)S(1)}, f32[8,1024]{1,0:T(8,128)}, u32[]{:S(2)}) copy-start(f32[8,1024]{1,0:T(8,128)} %norm_ref.1) | copy-start | bytes 98308
  10.9 1.7 %collective-permute-start.2 = (bf16[256,512]{1,0:T(8,128)(2,1)S(1)}, bf16[256,512]{1,0:T(8,128)(2,1)S(1)}, u32[]{:S(2)}, u32[]{:S(2)}) collective-permute-start(bf16[256,512]{1,0:T(8,128)(2,1)S(1)} %collective-permute-done.refs_2_), channel_id=1, source_target_pairs={{0,1},{1,0},{2,3},{3,2},{4,5},{5,4},{6,7},{7,6},{8,9},{9,8},{10,11... | collective-permute-start | bytes 786440 | tf_op jit(solution)/shard_map/ppermute | solution.py:493
  14.8 10.1 %collective-permute-start.3 = (bf16[2,512,128]{2,1,0:T(8,128)(2,1)S(1)}, bf16[2,512,128]{2,1,0:T(8,128)(2,1)S(1)}, u32[]{:S(2)}, u32[]{:S(2)}) collective-permute-start(bf16[2,512,128]{2,1,0:T(8,128)(2,1)S(1)} %get-tuple-element.75), channel_id=1, source_target_pairs={{0,4},{4,8},{8,12},{12,0},{1,5},{5,9},{9,13},{13,1},{2,6},{6,10},{... | collective-permute-start | bytes 786440 | tf_op jit(solution)/shard_map/ppermute | solution.py:510
  16.4 9.2 %collective-permute-start.4 = (bf16[2,512,128]{2,1,0:T(8,128)(2,1)S(1)}, bf16[2,512,128]{2,1,0:T(8,128)(2,1)S(1)}, u32[]{:S(2)}, u32[]{:S(2)}) collective-permute-start(bf16[2,512,128]{2,1,0:T(8,128)(2,1)S(1)} %get-tuple-element.76), channel_id=1, source_target_pairs={{0,8},{4,12},{8,0},{12,4},{1,9},{5,13},{9,1},{13,5},{2,10},{6,14},... | collective-permute-start | bytes 786440 | tf_op jit(solution)/shard_map/ppermute | solution.py:510
  18.0 12.0 %collective-permute-start.5 = (bf16[2,512,128]{2,1,0:T(8,128)(2,1)S(1)}, bf16[2,512,128]{2,1,0:T(8,128)(2,1)S(1)}, u32[]{:S(2)}, u32[]{:S(2)}) collective-permute-start(bf16[2,512,128]{2,1,0:T(8,128)(2,1)S(1)} %get-tuple-element.77), channel_id=1, source_target_pairs={{0,12},{4,0},{8,4},{12,8},{1,13},{5,1},{9,5},{13,9},{2,14},{6,2},{... | collective-permute-start | bytes 786440 | tf_op jit(solution)/shard_map/ppermute | solution.py:510
  33.0 7.6 %collective-permute-start.6 = (bf16[2,272,128]{2,1,0:T(8,128)(2,1)S(1)}, bf16[2,272,128]{2,1,0:T(8,128)(2,1)S(1)}, u32[]{:S(2)}, u32[]{:S(2)}) collective-permute-start(bf16[2,272,128]{2,1,0:T(8,128)(2,1)S(1)} %get-tuple-element.80), channel_id=1, source_target_pairs={{0,16},{1,17},{2,18},{3,19},{4,20},{5,21},{6,22},{7,23},{8,24},{9,... | collective-permute-start | bytes 417800 | tf_op jit(solution)/shard_map/ppermute | solution.py:585
  48.5 6.5 %collective-permute-start.7 = (bf16[2,272,128]{2,1,0:T(8,128)(2,1)S(1)}, bf16[2,272,128]{2,1,0:T(8,128)(2,1)S(1)}, u32[]{:S(2)}, u32[]{:S(2)}) collective-permute-start(bf16[2,272,128]{2,1,0:T(8,128)(2,1)S(1)} %get-tuple-element.91.window_ref), channel_id=1, source_target_pairs={{0,16},{16,0},{1,17},{17,1},{2,18},{18,2},{3,19},{19,3},{4,20},{20... | collective-permute-start | bytes 417800 | tf_op jit(solution)/shard_map/ppermute | solution.py:614
  55.1 18.7 %copy-start.1 = (bf16[2048,512]{1,0:T(8,128)(2,1)S(1)}, bf16[2048,512]{1,0:T(8,128)(2,1)}, u32[]{:S(2)}) copy-start(bf16[2048,512]{1,0:T(8,128)(2,1)} %refs_3_.3) | copy-start | bytes 6291460
  55.1 18.7 %copy-start.3 = (bf16[2048,512]{1,0:T(8,128)(2,1)S(1)}, bf16[2048,512]{1,0:T(8,128)(2,1)}, u32[]{:S(2)}) copy-start(bf16[2048,512]{1,0:T(8,128)(2,1)} %refs_2_.3) | copy-start | bytes 6291460
  55.1 18.7 %copy-start.5 = (bf16[2048,512]{1,0:T(8,128)(2,1)S(1)}, bf16[2048,512]{1,0:T(8,128)(2,1)}, u32[]{:S(2)}) copy-start(bf16[2048,512]{1,0:T(8,128)(2,1)} %refs_1_.3) | copy-start | bytes 6291460
  59.6 11.4 %collective-permute-start.8 = (bf16[2,384,128]{2,1,0:T(8,128)(2,1)S(1)}, bf16[2,384,128]{2,1,0:T(8,128)(2,1)S(1)}, u32[]{:S(2)}, u32[]{:S(2)}) collective-permute-start(bf16[2,384,128]{2,1,0:T(8,128)(2,1)S(1)} %get-tuple-element.103), channel_id=1, source_target_pairs={{0,4},{4,8},{8,12},{12,0},{1,5},{5,9},{9,13},{13,1},{2,6},{6,10},{... | collective-permute-start | bytes 589832 | tf_op jit(solution)/shard_map/ppermute | solution.py:510
  60.8 10.7 %collective-permute-start.9 = (bf16[2,384,128]{2,1,0:T(8,128)(2,1)S(1)}, bf16[2,384,128]{2,1,0:T(8,128)(2,1)S(1)}, u32[]{:S(2)}, u32[]{:S(2)}) collective-permute-start(bf16[2,384,128]{2,1,0:T(8,128)(2,1)S(1)} %get-tuple-element.104), channel_id=1, source_target_pairs={{0,8},{4,12},{8,0},{12,4},{1,9},{5,13},{9,1},{13,5},{2,10},{6,14},... | collective-permute-start | bytes 589832 | tf_op jit(solution)/shard_map/ppermute | solution.py:510
  65.7 8.0 %collective-permute-start.10 = (bf16[2,384,128]{2,1,0:T(8,128)(2,1)S(1)}, bf16[2,384,128]{2,1,0:T(8,128)(2,1)S(1)}, u32[]{:S(2)}, u32[]{:S(2)}) collective-permute-start(bf16[2,384,128]{2,1,0:T(8,128)(2,1)S(1)} %get-tuple-element.105), channel_id=1, source_target_pairs={{0,12},{4,0},{8,4},{12,8},{1,13},{5,1},{9,5},{13,9},{2,14},{6,2},{... | collective-permute-start | bytes 589832 | tf_op jit(solution)/shard_map/ppermute | solution.py:510
  75.7 1.9 %collective-permute-start.11 = (bf16[2,256,512]{2,1,0:T(8,128)(2,1)S(1)}, bf16[2,256,512]{2,1,0:T(8,128)(2,1)S(1)}, u32[]{:S(2)}, u32[]{:S(2)}) collective-permute-start(bf16[2,256,512]{2,1,0:T(8,128)(2,1)S(1)} %get-tuple-element.111), channel_id=1, source_target_pairs={{0,1},{1,0},{2,3},{3,2},{4,5},{5,4},{6,7},{7,6},{8,9},{9,8},{10,11... | collective-permute-start | bytes 1572872 | tf_op jit(solution)/shard_map/ppermute | solution.py:493
  77.7 13.6 %collective-permute-start.12 = (bf16[1,256,512]{2,1,0:T(8,128)(2,1)S(1)}, bf16[1,256,512]{2,1,0:T(8,128)(2,1)S(1)}, u32[]{:S(2)}, u32[]{:S(2)}) collective-permute-start(bf16[1,256,512]{2,1,0:T(8,128)(2,1)S(1)} %slice.9), channel_id=1, source_target_pairs={{0,2},{1,3},{2,0},{3,1},{4,6},{5,7},{6,4},{7,5},{8,10},{9,11},{10,... | collective-permute-start | bytes 786440 | tf_op jit(solution)/shard_map/ppermute | solution.py:493
  77.8 7.3 %collective-permute-start.15 = (bf16[2,272,128]{2,1,0:T(8,128)(2,1)S(1)}, bf16[2,272,128]{2,1,0:T(8,128)(2,1)S(1)}, u32[]{:S(2)}, u32[]{:S(2)}) collective-permute-start(bf16[2,272,128]{2,1,0:T(8,128)(2,1)S(1)} %get-tuple-element.115.refs_0_), channel_id=1, source_target_pairs={{0,12},{4,0},{8,4},{12,8},{1,13},{5,1},{9,5},{13,9},{2,14},{6,2},{... | collective-permute-start | bytes 417800 | tf_op jit(solution)/shard_map/ppermute | solution.py:510
  81.0 6.8 %collective-permute-start.14 = (bf16[2,272,128]{2,1,0:T(8,128)(2,1)S(1)}, bf16[2,272,128]{2,1,0:T(8,128)(2,1)S(1)}, u32[]{:S(2)}, u32[]{:S(2)}) collective-permute-start(bf16[2,272,128]{2,1,0:T(8,128)(2,1)S(1)} %get-tuple-element.115.refs_0_), channel_id=1, source_target_pairs={{0,8},{4,12},{8,0},{12,4},{1,9},{5,13},{9,1},{13,5},{2,10},{6,14},... | collective-permute-start | bytes 417800 | tf_op jit(solution)/shard_map/ppermute | solution.py:510
  81.3 7.5 %collective-permute-start.13 = (bf16[2,272,128]{2,1,0:T(8,128)(2,1)S(1)}, bf16[2,272,128]{2,1,0:T(8,128)(2,1)S(1)}, u32[]{:S(2)}, u32[]{:S(2)}) collective-permute-start(bf16[2,272,128]{2,1,0:T(8,128)(2,1)S(1)} %get-tuple-element.115.refs_0_), channel_id=1, source_target_pairs={{0,4},{4,8},{8,12},{12,0},{1,5},{5,9},{9,13},{13,1},{2,6},{6,10},{... | collective-permute-start | bytes 417800 | tf_op jit(solution)/shard_map/ppermute | solution.py:510

commit v7 on v6

--- a/solution.py
+++ b/solution.py
@@ -96,11 +96,11 @@
 
 
 def slot_of(place, other, local):
-    return lax.rem(other - place + local, local)
+    return lax.bitwise_xor(place, other)
 
 
 def came_in(place, other, local):
-    return lax.rem(place - other + local, local)
+    return lax.bitwise_xor(place, other)
 
 
 def prepare_kernel(
@@ -507,7 +507,7 @@
     group = lax.axis_index("group")
 
     def send(x, shift):
-        return lax.ppermute(x, "local", [(i, (i + shift) % local) for i in range(local)])
+        return lax.ppermute(x, "local", [(i, i ^ shift) for i in range(local)])
 
     def exchange(x):
         order = sorted(range(1, local), key=lambda s: -min(s, local - s))

time: 92.4 us -> 91.3 us (0.988)
  starting transfers between devices: 29.7 us -> 25.3 us
  waiting for transfers between devices: 23.2 us -> 26.5 us
    ppermute x9, starting transfers between devices: 17.8 us -> 13.6 us  [send(): return lax.ppermute(x, 'local', [(i, i ^ shift) for i in range(local)])]
    ppermute x9, waiting for transfers between devices: 19.4 us -> 23.3 us  [send(): return lax.ppermute(x, 'local', [(i, i ^ shift) for i in range(local)])]
  transfers between devices with their start and end apart: 16 -> 16, of which waited for: 13 -> 11; matrix products, arithmetic and copies ran while one was open for 0% -> 0% of each run, Pallas kernels for 12% -> 13%
where the time goes in v7:
time: 91.3 us; the launch traced here: 91 us
  Pallas kernels  30.7 us (34%)
  waiting for transfers between devices  26.5 us (29%)
  starting transfers between devices  25.3 us (28%)
  local copies, waits for them, and re-layouts  6.74 us (7%)
    pallas_call x11, Pallas kernels, call(): pl.pallas_call(kernel, in_specs=[vmem] * len(arrays) + [pl.BlockSpec(memo...  30.7 us
    ppermute x9, waiting for transfers between devices, send(): return lax.ppermute(x, 'local', [(i, i ^ shift) for i in range(local)])  23.3 us
    ppermute x9, starting transfers between devices, send(): return lax.ppermute(x, 'local', [(i, i ^ shift) for i in range(local)])  13.6 us
    unnamed x28, local copies, waits for them, and re-layouts  6.72 us
    ppermute x1, starting transfers between devices, body(): lax.ppermute(total, 'group', [(i, i + d) for i in range(groups - d)])  4.68 us
    ppermute x5, starting transfers between devices, hop(): return lax.ppermute(x, axis, [(i, i ^ distance) for i in range(count)])  3.65 us
    ppermute x1, starting transfers between devices, body(): lax.ppermute(window, 'group', [(i, (i + d) % groups) for i in range(group...  3.41 us
    ppermute x5, waiting for transfers between devices, hop(): return lax.ppermute(x, axis, [(i, i ^ distance) for i in range(count)])  2.06 us
  transfers between devices with their start and end apart: 16, of which 11 were waited for; matrix products, arithmetic and copies ran while one was open for 0% of the time, Pallas kernels for 13%

profile of v7, /device:TPU:0, one launch (start us, length us, event | category | flops | bytes accessed | tf_op | source)
XLA Modules:
  0.0 91.0 jit_solution(8013067828723878729)
XLA Ops:
  0.6 3.0 %collective-permute-start = (bf16[256,512]{1,0:T(8,128)(2,1)}, bf16[256,512]{1,0:T(8,128)(2,1)S(1)}, u32[]{:S(2)}, u32[]{:S(2)}) collective-permute-start(bf16[256,512]{1,0:T(8,128)(2,1)} %refs_4_.2), channel_id=1, source_target_pairs={{0,2},{1,3},{2,0},{3,1},{4,6},{5,7},{6,4},{7,5},{8,10},{9,11},{10,... | collective-permute-start | bytes 786440 | tf_op jit(solution)/shard_map/ppermute | solution.py:493
  3.6 1.6 %copy-done = bf16[2048,512]{1,0:T(8,128)(2,1)S(1)} copy-done((bf16[2048,512]{1,0:T(8,128)(2,1)S(1)}, bf16[2048,512]{1,0:T(8,128)(2,1)}, u32[]{:S(2)}) %copy-start) | copy-done | bytes 2097176
  5.2 1.6 %copy-done.2 = bf16[2048,512]{1,0:T(8,128)(2,1)S(1)} copy-done((bf16[2048,512]{1,0:T(8,128)(2,1)S(1)}, bf16[2048,512]{1,0:T(8,128)(2,1)}, u32[]{:S(2)}) %copy-start.2) | copy-done | bytes 2097176
  6.8 1.6 %copy-done.4 = bf16[2048,512]{1,0:T(8,128)(2,1)S(1)} copy-done((bf16[2048,512]{1,0:T(8,128)(2,1)S(1)}, bf16[2048,512]{1,0:T(8,128)(2,1)}, u32[]{:S(2)}) %copy-start.4) | copy-done | bytes 2097176
  8.4 0.9 %copy-done.9 = bf16[256,512]{1,0:T(8,128)(2,1)S(1)} copy-done((bf16[256,512]{1,0:T(8,128)(2,1)S(1)}, bf16[256,512]{1,0:T(8,128)(2,1)}, u32[]{:S(2)}) %copy-start.9) | copy-done | bytes 262168
  9.4 0.9 %copy-done.10 = bf16[256,512]{1,0:T(8,128)(2,1)S(1)} copy-done((bf16[256,512]{1,0:T(8,128)(2,1)S(1)}, bf16[256,512]{1,0:T(8,128)(2,1)}, u32[]{:S(2)}) %copy-start.10) | copy-done | bytes 262168
  11.5 1.2 %collective-permute-done.2.refs_3_ = bf16[256,512]{1,0:T(8,128)(2,1)S(1)} collective-permute-done((bf16[256,512]{1,0:T(8,128)(2,1)S(1)}, bf16[256,512]{1,0:T(8,128)(2,1)S(1)}, u32[]{:S(2)}, u32[]{:S(2)}) %collective-permute-start.2) | collective-permute-done | bytes 262176 | tf_op jit(solution)/shard_map/ppermute | solution.py:493
  12.6 2.0 %project.1 = (bf16[2,512,128]{2,1,0:T(8,128)(2,1)S(1)}, bf16[2,512,128]{2,1,0:T(8,128)(2,1)S(1)}, bf16[2,512,128]{2,1,0:T(8,128)(2,1)S(1)}, bf16[2,512,128]{2,1,0:T(8,128)(2,1)S(1)}) custom-call(bf16[256,512]{1,0:T(8,128)(2,1)S(1)} %get-tuple-element.67.refs_0_, bf16[256,512]{1,0:T(8,128)(2,1)S(1)} %collective-permute-done.1.refs_1_, ...), custom_call_target="tpu_custom_call" | custom-call | tf_op jit(solution)/shard_map/project/pallas_call | solution.py:480
  14.7 1.6 %collective-permute-start.3 = (bf16[2,512,128]{2,1,0:T(8,128)(2,1)S(1)}, bf16[2,512,128]{2,1,0:T(8,128)(2,1)S(1)}, u32[]{:S(2)}, u32[]{:S(2)}) collective-permute-start(bf16[2,512,128]{2,1,0:T(8,128)(2,1)S(1)} %get-tuple-element.75), channel_id=1, source_target_pairs={{0,4},{4,0},{8,12},{12,8},{1,5},{5,1},{9,13},{13,9},{2,6},{6,2},{1... | collective-permute-start | bytes 786440 | tf_op jit(solution)/shard_map/ppermute | solution.py:510
  16.3 1.6 %collective-permute-start.4 = (bf16[2,512,128]{2,1,0:T(8,128)(2,1)S(1)}, bf16[2,512,128]{2,1,0:T(8,128)(2,1)S(1)}, u32[]{:S(2)}, u32[]{:S(2)}) collective-permute-start(bf16[2,512,128]{2,1,0:T(8,128)(2,1)S(1)} %get-tuple-element.76), channel_id=1, source_target_pairs={{0,8},{4,12},{8,0},{12,4},{1,9},{5,13},{9,1},{13,5},{2,10},{6,14},... | collective-permute-start | bytes 786440 | tf_op jit(solution)/shard_map/ppermute | solution.py:510
  18.3 3.0 %prepare.1 = (f32[2,128,640]{2,1,0:T(8,128)S(1)}, f32[2,128,640]{2,1,0:T(8,128)S(1)}, bf16[256,512]{1,0:T(8,128)(2,1)S(1)}, bf16[512,128]{1,0:T(8,128)(2,1)S(1)}, bf16[512,128]{1,0:T(8,128)(2,1)S(1)}) custom-call(f32[2,32,64]{2,1,0:T(8,128)S(1)} %bitcast.9, f32[8,1024]{1,0:T(8,128)S(1)} %copy-done.13, f32[8,1024]{1,0:T(8,128)S(1)} %copy-done.11, ...), custom_call_target="tpu_custom_call" | custom-call | tf_op jit(solution)/shard_map/prepare/pallas_call | solution.py:480
  21.2 2.1 %collective-permute-done.3.refs_1_ = bf16[2,512,128]{2,1,0:T(8,128)(2,1)S(1)} collective-permute-done((bf16[2,512,128]{2,1,0:T(8,128)(2,1)S(1)}, bf16[2,512,128]{2,1,0:T(8,128)(2,1)S(1)}, u32[]{:S(2)}, u32[]{:S(2)}) %collective-permute-start.3) | collective-permute-done | bytes 262176 | tf_op jit(solution)/shard_map/ppermute | solution.py:510
  23.3 2.1 %collective-permute-done.4.refs_2_ = bf16[2,512,128]{2,1,0:T(8,128)(2,1)S(1)} collective-permute-done((bf16[2,512,128]{2,1,0:T(8,128)(2,1)S(1)}, bf16[2,512,128]{2,1,0:T(8,128)(2,1)S(1)}, u32[]{:S(2)}, u32[]{:S(2)}) %collective-permute-start.4) | collective-permute-done | bytes 262176 | tf_op jit(solution)/shard_map/ppermute | solution.py:510
  25.4 4.7 %collective-permute-done.5.refs_3_ = bf16[2,512,128]{2,1,0:T(8,128)(2,1)S(1)} collective-permute-done((bf16[2,512,128]{2,1,0:T(8,128)(2,1)S(1)}, bf16[2,512,128]{2,1,0:T(8,128)(2,1)S(1)}, u32[]{:S(2)}, u32[]{:S(2)}) %collective-permute-start.5) | collective-permute-done | bytes 262176 | tf_op jit(solution)/shard_map/ppermute | solution.py:510
  30.1 3.0 %key_side.1 = (bf16[4,2,512,128]{3,2,1,0:T(8,128)(2,1)S(1)}, f32[2,4,128,640]{3,2,1,0:T(8,128)S(1)}, bf16[2,4,256,640]{3,2,1,0:T(8,128)(2,1)S(1)}, bf16[2,4,256,...) custom-call(bf16[2,512,128]{2,1,0:T(8,128)(2,1)S(1)} %get-tuple-element.74.refs_0_, ...), custom_call_target="tpu_custom_call" | custom-call | tf_op jit(solution)/shard_map/key_side/pallas_call | solution.py:480
  33.2 4.7 %collective-permute-start.6 = (bf16[2,272,128]{2,1,0:T(8,128)(2,1)S(1)}, bf16[2,272,128]{2,1,0:T(8,128)(2,1)S(1)}, u32[]{:S(2)}, u32[]{:S(2)}) collective-permute-start(bf16[2,272,128]{2,1,0:T(8,128)(2,1)S(1)} %get-tuple-element.80), channel_id=1, source_target_pairs={{0,16},{1,17},{2,18},{3,19},{4,20},{5,21},{6,22},{7,23},{8,24},{9,... | collective-permute-start | bytes 417800 | tf_op jit(solution)/shard_map/ppermute | solution.py:585
  37.8 1.9 %query_first.1 = (bf16[2,4,256,128]{3,2,1,0:T(8,128)(2,1)S(1)}, f32[2,4,256,512]{3,2,1,0:T(8,128)S(1)}, bf16[2,4,256,640]{3,2,1,0:T(8,128)(2,1)S(1)}, f32[2,4,25...) custom-call(bf16[4,2,512,128]{3,2,1,0:T(8,128)(2,1)S(1)} %get-tuple-element.82.qkv_ref, ...), custom_call_target="tpu_custom_call" | custom-call | tf_op jit(solution)/shard_map/query_first/pallas_call | solution.py:480
  40.2 7.9 %query_side.1 = (bf16[2,4,128,128]{3,2,1,0:T(8,128)(2,1)S(1)}, bf16[2,4,256,128]{3,2,1,0:T(8,128)(2,1)S(1)}, f32[2,4,128,640]{3,2,1,0:T(8,128)S(1)}, bf16[2,272,128]{2,1,0:T(8,128)(2,1)S(1)}) custom-call(bf16[2,272,128]{2,1,0:T(8,128)(2,1)S(1)} %collective-permute-done.6.carry_ref, f32[2,128,640]{2,1,0:T(8,128)S(1)} %get-tuple-element.81.base_ref, ...), custom_call_target="tpu_custom_call" | custom-call | tf_op jit(solution)/shard_map/query_side/pallas_call | solution.py:480
  48.2 3.4 %collective-permute-start.7 = (bf16[2,272,128]{2,1,0:T(8,128)(2,1)S(1)}, bf16[2,272,128]{2,1,0:T(8,128)(2,1)S(1)}, u32[]{:S(2)}, u32[]{:S(2)}) collective-permute-start(bf16[2,272,128]{2,1,0:T(8,128)(2,1)S(1)} %get-tuple-element.91.window_ref), channel_id=1, source_target_pairs={{0,16},{16,0},{1,17},{17,1},{2,18},{18,2},{3,19},{19,3},{4,20},{20... | collective-permute-start | bytes 417800 | tf_op jit(solution)/shard_map/ppermute | solution.py:614
  51.6 2.4 %key_first.1 = (f32[2,4,256,512]{3,2,1,0:T(8,128)S(1)}, f32[2,4,256,128]{3,2,1,0:T(8,128)S(1)}, f32[2,4,256,128]{3,2,1,0:T(8,128)S(1)}) custom-call(bf16[4,2,512,128]{3,2,1,0:T(8,128)(2,1)S(1)} %get-tuple-element.82.qkv_ref, bf16[2,4,256,128]{3,2,1,0:T(8,128)(2,1)S(1)} %get-tuple-element.83.kdot_ref, ...), custom_call_target="tpu_custom_call" | custom-call | tf_op jit(solution)/shard_map/key_first/pallas_call | solution.py:480
  54.6 4.5 %key_gradients.1 = (bf16[2,384,128]{2,1,0:T(8,128)(2,1)S(1)}, bf16[2,384,128]{2,1,0:T(8,128)(2,1)S(1)}, bf16[2,384,128]{2,1,0:T(8,128)(2,1)S(1)}, bf16[2,384,128...) custom-call(bf16[2,272,128]{2,1,0:T(8,128)(2,1)S(1)} %get-tuple-element.91.window_ref, ...), custom_call_target="tpu_custom_call" | custom-call | tf_op jit(solution)/shard_map/key_gradients/pallas_call | solution.py:480
  59.1 1.6 %collective-permute-start.8 = (bf16[2,384,128]{2,1,0:T(8,128)(2,1)S(1)}, bf16[2,384,128]{2,1,0:T(8,128)(2,1)S(1)}, u32[]{:S(2)}, u32[]{:S(2)}) collective-permute-start(bf16[2,384,128]{2,1,0:T(8,128)(2,1)S(1)} %get-tuple-element.103), channel_id=1, source_target_pairs={{0,4},{4,0},{8,12},{12,8},{1,5},{5,1},{9,13},{13,9},{2,6},{6,2},{1... | collective-permute-start | bytes 589832 | tf_op jit(solution)/shard_map/ppermute | solution.py:510
  60.7 4.9 %collective-permute-start.9 = (bf16[2,384,128]{2,1,0:T(8,128)(2,1)S(1)}, bf16[2,384,128]{2,1,0:T(8,128)(2,1)S(1)}, u32[]{:S(2)}, u32[]{:S(2)}) collective-permute-start(bf16[2,384,128]{2,1,0:T(8,128)(2,1)S(1)} %get-tuple-element.104), channel_id=1, source_target_pairs={{0,8},{4,12},{8,0},{12,4},{1,9},{5,13},{9,1},{13,5},{2,10},{6,14},... | collective-permute-start | bytes 589832 | tf_op jit(solution)/shard_map/ppermute | solution.py:510
  65.5 5.8 %collective-permute-done.9.refs_2_ = bf16[2,384,128]{2,1,0:T(8,128)(2,1)S(1)} collective-permute-done((bf16[2,384,128]{2,1,0:T(8,128)(2,1)S(1)}, bf16[2,384,128]{2,1,0:T(8,128)(2,1)S(1)}, u32[]{:S(2)}, u32[]{:S(2)}) %collective-permute-start.9) | collective-permute-done | bytes 196640 | tf_op jit(solution)/shard_map/ppermute | solution.py:510
  71.3 2.4 %collective-permute-done.10.refs_3_ = bf16[2,384,128]{2,1,0:T(8,128)(2,1)S(1)} collective-permute-done((bf16[2,384,128]{2,1,0:T(8,128)(2,1)S(1)}, bf16[2,384,128]{2,1,0:T(8,128)(2,1)S(1)}, u32[]{:S(2)}, u32[]{:S(2)}) %collective-permute-start.10) | collective-permute-done | bytes 196640 | tf_op jit(solution)/shard_map/ppermute | solution.py:510
  73.8 1.8 %input_gradient.1 = (bf16[256,512]{1,0:T(8,128)(2,1)}, bf16[256,512]{1,0:T(8,128)(2,1)}, bf16[256,512]{1,0:T(8,128)(2,1)}, bf16[2,256,512]{2,1,0:T(8,128)(2,1)S(1)}, bf16[3,256,512]{2,1,0:T(8,128)(2,1)S(1)}) custom-call(bf16[2,384,128]{2,1,0:T(8,128)(2,1)S(1)} %get-tuple-element.106.refs_0_, bf16[2,384,128]{2,1,0:T(8,128)(2,1)S(1)} %collective-permute-done.8.refs_1_, ...), custom_call_target="tpu_custom_call" | custom-call | tf_op jit(solution)/shard_map/input_gradient/pallas_call | solution.py:480
  75.6 1.0 %input_gradient_rest.1 = bf16[2,256,512]{2,1,0:T(8,128)(2,1)S(1)} custom-call(bf16[3,256,512]{2,1,0:T(8,128)(2,1)S(1)} %get-tuple-element.110.refs_0_, bf16[2048,512]{1,0:T(8,128)(2,1)S(1)} %copy-done.5, bf16[2048,512]{1,0:T(8,128)(2,1)S(1)} %copy-done.3, bf16[2048,512]{1,0:T(8,128)(2,1)S(1)} %copy-done.1), custom_call_target="tpu_custom_call" | custom-call | tf_op jit(solution)/shard_map/input_gradient_rest/pallas_call | solution.py:480
  76.6 0.9 collective-permute-done.11
  77.8 2.8 %collective-permute-start.15 = (bf16[2,272,128]{2,1,0:T(8,128)(2,1)S(1)}, bf16[2,272,128]{2,1,0:T(8,128)(2,1)S(1)}, u32[]{:S(2)}, u32[]{:S(2)}) collective-permute-start(bf16[2,272,128]{2,1,0:T(8,128)(2,1)S(1)} %get-tuple-element.115.refs_0_), channel_id=1, source_target_pairs={{0,12},{4,8},{8,4},{12,0},{1,13},{5,9},{9,5},{13,1},{2,14},{6,10},... | collective-permute-start | bytes 417800 | tf_op jit(solution)/shard_map/ppermute | solution.py:510
  81.3 3.9 %collective-permute-done.15.refs_3_ = bf16[2,272,128]{2,1,0:T(8,128)(2,1)S(1)} collective-permute-done((bf16[2,272,128]{2,1,0:T(8,128)(2,1)S(1)}, bf16[2,272,128]{2,1,0:T(8,128)(2,1)S(1)}, u32[]{:S(2)}, u32[]{:S(2)}) %collective-permute-start.15) | collective-permute-done | bytes 139296 | tf_op jit(solution)/shard_map/ppermute | solution.py:510
  85.2 2.3 %collective-permute-done.14.refs_2_ = bf16[2,272,128]{2,1,0:T(8,128)(2,1)S(1)} collective-permute-done((bf16[2,272,128]{2,1,0:T(8,128)(2,1)S(1)}, bf16[2,272,128]{2,1,0:T(8,128)(2,1)S(1)}, u32[]{:S(2)}, u32[]{:S(2)}) %collective-permute-start.14) | collective-permute-done | bytes 139296 | tf_op jit(solution)/shard_map/ppermute | solution.py:510
  87.5 2.7 %prefix_gradients.1 = (f32[8,64,1024]{2,1,0:T(8,128)}, f32[8,1024]{1,0:T(8,128)}) custom-call(bf16[2,272,128]{2,1,0:T(8,128)(2,1)S(1)} %get-tuple-element.115.refs_0_, bf16[2,272,128]{2,1,0:T(8,128)(2,1)S(1)} %collective-permute-done.13.refs_1_, bf16[2,272,128]{2,1,0:T(8,128)(2,1)S(1)} %collective-permute-done.14.refs_2_, ...), custom_call_target="tpu_custom_call" | custom-call | tf_op jit(solution)/shard_map/prefix_gradients/pallas_call | solution.py:480
  (42 shorter events, 4.4 us)
Async XLA Ops:
  0.6 10.2 %collective-permute-start = (bf16[256,512]{1,0:T(8,128)(2,1)}, bf16[256,512]{1,0:T(8,128)(2,1)S(1)}, u32[]{:S(2)}, u32[]{:S(2)}) collective-permute-start(bf16[256,512]{1,0:T(8,128)(2,1)} %refs_4_.2), channel_id=1, source_target_pairs={{0,2},{1,3},{2,0},{3,1},{4,6},{5,7},{6,4},{7,5},{8,10},{9,11},{10,... | collective-permute-start | bytes 786440 | tf_op jit(solution)/shard_map/ppermute | solution.py:493
  3.6 7.9 %collective-permute-start.1 = (bf16[256,512]{1,0:T(8,128)(2,1)}, bf16[256,512]{1,0:T(8,128)(2,1)S(1)}, u32[]{:S(2)}, u32[]{:S(2)}) collective-permute-start(bf16[256,512]{1,0:T(8,128)(2,1)} %refs_4_.2), channel_id=1, source_target_pairs={{0,1},{1,0},{2,3},{3,2},{4,5},{5,4},{6,7},{7,6},{8,9},{9,8},{10,11... | collective-permute-start | bytes 786440 | tf_op jit(solution)/shard_map/ppermute | solution.py:493
  3.6 1.6 %copy-start = (bf16[2048,512]{1,0:T(8,128)(2,1)S(1)}, bf16[2048,512]{1,0:T(8,128)(2,1)}, u32[]{:S(2)}) copy-start(bf16[2048,512]{1,0:T(8,128)(2,1)} %refs_3_.3) | copy-start | bytes 6291460
  5.2 1.6 %copy-start.2 = (bf16[2048,512]{1,0:T(8,128)(2,1)S(1)}, bf16[2048,512]{1,0:T(8,128)(2,1)}, u32[]{:S(2)}) copy-start(bf16[2048,512]{1,0:T(8,128)(2,1)} %refs_2_.3) | copy-start | bytes 6291460
  6.8 1.6 %copy-start.4 = (bf16[2048,512]{1,0:T(8,128)(2,1)S(1)}, bf16[2048,512]{1,0:T(8,128)(2,1)}, u32[]{:S(2)}) copy-start(bf16[2048,512]{1,0:T(8,128)(2,1)} %refs_1_.3) | copy-start | bytes 6291460
  8.4 0.9 %copy-start.9 = (bf16[256,512]{1,0:T(8,128)(2,1)S(1)}, bf16[256,512]{1,0:T(8,128)(2,1)}, u32[]{:S(2)}) copy-start(bf16[256,512]{1,0:T(8,128)(2,1)} %refs_3_.2) | copy-start | bytes 786436
  9.4 0.9 %copy-start.10 = (bf16[256,512]{1,0:T(8,128)(2,1)S(1)}, bf16[256,512]{1,0:T(8,128)(2,1)}, u32[]{:S(2)}) copy-start(bf16[256,512]{1,0:T(8,128)(2,1)} %refs_4_.2) | copy-start | bytes 786436
  10.8 7.4 %copy-start.6 = (f32[8,1024,64]{1,2,0:T(8,128)S(1)}, f32[8,1024,64]{1,2,0:T(8,128)}, u32[]{:S(2)}) copy-start(f32[8,1024,64]{1,2,0:T(8,128)} %param.19) | copy-start | bytes 6291460
  10.9 7.4 %copy-start.7 = (bf16[1024,640]{1,0:T(8,128)(2,1)S(1)}, bf16[1024,640]{1,0:T(8,128)(2,1)}, u32[]{:S(2)}) copy-start(bf16[1024,640]{1,0:T(8,128)(2,1)} %constant.2.clone.map_ref.refs_6_) | copy-start | bytes 3932164
  10.9 7.4 %copy-start.8 = (f32[8,1024,64]{1,2,0:T(8,128)S(1)}, f32[8,1024,64]{1,2,0:T(8,128)}, u32[]{:S(2)}) copy-start(f32[8,1024,64]{1,2,0:T(8,128)} %param.16) | copy-start | bytes 6291460
  10.9 7.4 %copy-start.11 = (f32[8,1024]{1,0:T(8,128)S(1)}, f32[8,1024]{1,0:T(8,128)}, u32[]{:S(2)}) copy-start(f32[8,1024]{1,0:T(8,128)} %refs_5_.3) | copy-start | bytes 98308
  10.9 7.4 %copy-start.12 = (f32[2,64,32]{1,2,0:T(8,128)S(1)}, f32[2,64,32]{1,2,0:T(8,128)}, u32[]{:S(2)}) copy-start(f32[2,64,32]{1,2,0:T(8,128)} %param.15) | copy-start | bytes 49156
  10.9 7.4 %copy-start.13 = (f32[8,1024]{1,0:T(8,128)S(1)}, f32[8,1024]{1,0:T(8,128)}, u32[]{:S(2)}) copy-start(f32[8,1024]{1,0:T(8,128)} %norm_ref.1) | copy-start | bytes 98308
  10.9 1.7 %collective-permute-start.2 = (bf16[256,512]{1,0:T(8,128)(2,1)S(1)}, bf16[256,512]{1,0:T(8,128)(2,1)S(1)}, u32[]{:S(2)}, u32[]{:S(2)}) collective-permute-start(bf16[256,512]{1,0:T(8,128)(2,1)S(1)} %collective-permute-done.refs_2_), channel_id=1, source_target_pairs={{0,1},{1,0},{2,3},{3,2},{4,5},{5,4},{6,7},{7,6},{8,9},{9,8},{10,11... | collective-permute-start | bytes 786440 | tf_op jit(solution)/shard_map/ppermute | solution.py:493
  14.7 8.7 %collective-permute-start.3 = (bf16[2,512,128]{2,1,0:T(8,128)(2,1)S(1)}, bf16[2,512,128]{2,1,0:T(8,128)(2,1)S(1)}, u32[]{:S(2)}, u32[]{:S(2)}) collective-permute-start(bf16[2,512,128]{2,1,0:T(8,128)(2,1)S(1)} %get-tuple-element.75), channel_id=1, source_target_pairs={{0,4},{4,0},{8,12},{12,8},{1,5},{5,1},{9,13},{13,9},{2,6},{6,2},{1... | collective-permute-start | bytes 786440 | tf_op jit(solution)/shard_map/ppermute | solution.py:510
  16.3 9.2 %collective-permute-start.4 = (bf16[2,512,128]{2,1,0:T(8,128)(2,1)S(1)}, bf16[2,512,128]{2,1,0:T(8,128)(2,1)S(1)}, u32[]{:S(2)}, u32[]{:S(2)}) collective-permute-start(bf16[2,512,128]{2,1,0:T(8,128)(2,1)S(1)} %get-tuple-element.76), channel_id=1, source_target_pairs={{0,8},{4,12},{8,0},{12,4},{1,9},{5,13},{9,1},{13,5},{2,10},{6,14},... | collective-permute-start | bytes 786440 | tf_op jit(solution)/shard_map/ppermute | solution.py:510
  17.8 12.3 %collective-permute-start.5 = (bf16[2,512,128]{2,1,0:T(8,128)(2,1)S(1)}, bf16[2,512,128]{2,1,0:T(8,128)(2,1)S(1)}, u32[]{:S(2)}, u32[]{:S(2)}) collective-permute-start(bf16[2,512,128]{2,1,0:T(8,128)(2,1)S(1)} %get-tuple-element.77), channel_id=1, source_target_pairs={{0,12},{4,8},{8,4},{12,0},{1,13},{5,9},{9,5},{13,1},{2,14},{6,10},... | collective-permute-start | bytes 786440 | tf_op jit(solution)/shard_map/ppermute | solution.py:510
  33.2 7.1 %collective-permute-start.6 = (bf16[2,272,128]{2,1,0:T(8,128)(2,1)S(1)}, bf16[2,272,128]{2,1,0:T(8,128)(2,1)S(1)}, u32[]{:S(2)}, u32[]{:S(2)}) collective-permute-start(bf16[2,272,128]{2,1,0:T(8,128)(2,1)S(1)} %get-tuple-element.80), channel_id=1, source_target_pairs={{0,16},{1,17},{2,18},{3,19},{4,20},{5,21},{6,22},{7,23},{8,24},{9,... | collective-permute-start | bytes 417800 | tf_op jit(solution)/shard_map/ppermute | solution.py:585
  48.2 6.5 %collective-permute-start.7 = (bf16[2,272,128]{2,1,0:T(8,128)(2,1)S(1)}, bf16[2,272,128]{2,1,0:T(8,128)(2,1)S(1)}, u32[]{:S(2)}, u32[]{:S(2)}) collective-permute-start(bf16[2,272,128]{2,1,0:T(8,128)(2,1)S(1)} %get-tuple-element.91.window_ref), channel_id=1, source_target_pairs={{0,16},{16,0},{1,17},{17,1},{2,18},{18,2},{3,19},{19,3},{4,20},{20... | collective-permute-start | bytes 417800 | tf_op jit(solution)/shard_map/ppermute | solution.py:614
  54.6 19.2 %copy-start.1 = (bf16[2048,512]{1,0:T(8,128)(2,1)S(1)}, bf16[2048,512]{1,0:T(8,128)(2,1)}, u32[]{:S(2)}) copy-start(bf16[2048,512]{1,0:T(8,128)(2,1)} %refs_3_.3) | copy-start | bytes 6291460
  54.6 19.2 %copy-start.3 = (bf16[2048,512]{1,0:T(8,128)(2,1)S(1)}, bf16[2048,512]{1,0:T(8,128)(2,1)}, u32[]{:S(2)}) copy-start(bf16[2048,512]{1,0:T(8,128)(2,1)} %refs_2_.3) | copy-start | bytes 6291460
  54.6 19.2 %copy-start.5 = (bf16[2048,512]{1,0:T(8,128)(2,1)S(1)}, bf16[2048,512]{1,0:T(8,128)(2,1)}, u32[]{:S(2)}) copy-start(bf16[2048,512]{1,0:T(8,128)(2,1)} %refs_1_.3) | copy-start | bytes 6291460
  59.1 6.5 %collective-permute-start.8 = (bf16[2,384,128]{2,1,0:T(8,128)(2,1)S(1)}, bf16[2,384,128]{2,1,0:T(8,128)(2,1)S(1)}, u32[]{:S(2)}, u32[]{:S(2)}) collective-permute-start(bf16[2,384,128]{2,1,0:T(8,128)(2,1)S(1)} %get-tuple-element.103), channel_id=1, source_target_pairs={{0,4},{4,0},{8,12},{12,8},{1,5},{5,1},{9,13},{13,9},{2,6},{6,2},{1... | collective-permute-start | bytes 589832 | tf_op jit(solution)/shard_map/ppermute | solution.py:510
  60.7 10.7 %collective-permute-start.9 = (bf16[2,384,128]{2,1,0:T(8,128)(2,1)S(1)}, bf16[2,384,128]{2,1,0:T(8,128)(2,1)S(1)}, u32[]{:S(2)}, u32[]{:S(2)}) collective-permute-start(bf16[2,384,128]{2,1,0:T(8,128)(2,1)S(1)} %get-tuple-element.104), channel_id=1, source_target_pairs={{0,8},{4,12},{8,0},{12,4},{1,9},{5,13},{9,1},{13,5},{2,10},{6,14},... | collective-permute-start | bytes 589832 | tf_op jit(solution)/shard_map/ppermute | solution.py:510
  65.5 8.2 %collective-permute-start.10 = (bf16[2,384,128]{2,1,0:T(8,128)(2,1)S(1)}, bf16[2,384,128]{2,1,0:T(8,128)(2,1)S(1)}, u32[]{:S(2)}, u32[]{:S(2)}) collective-permute-start(bf16[2,384,128]{2,1,0:T(8,128)(2,1)S(1)} %get-tuple-element.105), channel_id=1, source_target_pairs={{0,12},{4,8},{8,4},{12,0},{1,13},{5,9},{9,5},{13,1},{2,14},{6,10},... | collective-permute-start | bytes 589832 | tf_op jit(solution)/shard_map/ppermute | solution.py:510
  75.6 1.9 %collective-permute-start.11 = (bf16[2,256,512]{2,1,0:T(8,128)(2,1)S(1)}, bf16[2,256,512]{2,1,0:T(8,128)(2,1)S(1)}, u32[]{:S(2)}, u32[]{:S(2)}) collective-permute-start(bf16[2,256,512]{2,1,0:T(8,128)(2,1)S(1)} %get-tuple-element.111), channel_id=1, source_target_pairs={{0,1},{1,0},{2,3},{3,2},{4,5},{5,4},{6,7},{7,6},{8,9},{9,8},{10,11... | collective-permute-start | bytes 1572872 | tf_op jit(solution)/shard_map/ppermute | solution.py:493
  77.7 12.5 %collective-permute-start.12 = (bf16[1,256,512]{2,1,0:T(8,128)(2,1)S(1)}, bf16[1,256,512]{2,1,0:T(8,128)(2,1)S(1)}, u32[]{:S(2)}, u32[]{:S(2)}) collective-permute-start(bf16[1,256,512]{2,1,0:T(8,128)(2,1)S(1)} %slice.9), channel_id=1, source_target_pairs={{0,2},{1,3},{2,0},{3,1},{4,6},{5,7},{6,4},{7,5},{8,10},{9,11},{10,... | collective-permute-start | bytes 786440 | tf_op jit(solution)/shard_map/ppermute | solution.py:493
  77.8 7.5 %collective-permute-start.15 = (bf16[2,272,128]{2,1,0:T(8,128)(2,1)S(1)}, bf16[2,272,128]{2,1,0:T(8,128)(2,1)S(1)}, u32[]{:S(2)}, u32[]{:S(2)}) collective-permute-start(bf16[2,272,128]{2,1,0:T(8,128)(2,1)S(1)} %get-tuple-element.115.refs_0_), channel_id=1, source_target_pairs={{0,12},{4,8},{8,4},{12,0},{1,13},{5,9},{9,5},{13,1},{2,14},{6,10},... | collective-permute-start | bytes 417800 | tf_op jit(solution)/shard_map/ppermute | solution.py:510
  80.5 7.0 %collective-permute-start.14 = (bf16[2,272,128]{2,1,0:T(8,128)(2,1)S(1)}, bf16[2,272,128]{2,1,0:T(8,128)(2,1)S(1)}, u32[]{:S(2)}, u32[]{:S(2)}) collective-permute-start(bf16[2,272,128]{2,1,0:T(8,128)(2,1)S(1)} %get-tuple-element.115.refs_0_), channel_id=1, source_target_pairs={{0,8},{4,12},{8,0},{12,4},{1,9},{5,13},{9,1},{13,5},{2,10},{6,14},... | collective-permute-start | bytes 417800 | tf_op jit(solution)/shard_map/ppermute | solution.py:510
  80.8 6.7 %collective-permute-start.13 = (bf16[2,272,128]{2,1,0:T(8,128)(2,1)S(1)}, bf16[2,272,128]{2,1,0:T(8,128)(2,1)S(1)}, u32[]{:S(2)}, u32[]{:S(2)}) collective-permute-start(bf16[2,272,128]{2,1,0:T(8,128)(2,1)S(1)} %get-tuple-element.115.refs_0_), channel_id=1, source_target_pairs={{0,4},{4,0},{8,12},{12,8},{1,5},{5,1},{9,13},{13,9},{2,6},{6,2},{1... | collective-permute-start | bytes 417800 | tf_op jit(solution)/shard_map/ppermute | solution.py:510
